TPU v7x, 32 devices: a whole 2x2x4 slice. The times are simulated.
32 devices in a mesh: dp: 2 (over x), tp: 16 (over z, y, core).
Axes of the slice: x: 2, y: 2, z: 4, core: 2. Of those that a mesh axis runs over, the one named last changes fastest.
Arguments:
- queries: bfloat16 [256, 128, 576], P(('dp', 'tp')), may hold values from -10 to 10
- new_latent: bfloat16 [256, 576], P(('dp', 'tp')), may hold values from -6 to 6
- resident: bfloat16 [192, 256, 576], P(('dp', 'tp')), may hold values from -6 to 6
- leaving: bfloat16 [64, 2, 256, 576], P(('dp', 'tp')), may hold values from -6 to 6
- res_len: int32 [192], P(('dp', 'tp')), may hold values from 1 to 256, as said below
- leave_len: int32 [32, 2], replicated, may hold values from 1 to 256, as said below
- mig_dest: int32 [32, 2], replicated, may hold values from 0 to 15, as said below
- stream: bfloat16 [256, 7168], P(('dp', 'tp')), may hold values from -6 to 6
- dense_gain: float32 [7168], replicated, may hold values from 0.1 to 1.9
- w_gate: bfloat16 [7168, 18432], P('dp', 'tp'), may hold values from -0.0625 to 0.0625
- w_up: bfloat16 [7168, 18432], P('dp', 'tp'), may hold values from -0.0625 to 0.0625
- w_down: bfloat16 [18432, 7168], P('tp', 'dp'), may hold values from -0.046875 to 0.046875
- moe_gain: float32 [7168], replicated, may hold values from 0.1 to 1.9
- expert_gate: bfloat16 [16, 7168, 2048], P('tp', None, 'dp'), may hold values from -0.0625 to 0.0625
- expert_up: bfloat16 [16, 7168, 2048], P('tp', None, 'dp'), may hold values from -0.0625 to 0.0625
- expert_down: bfloat16 [16, 2048, 7168], P('tp', 'dp'), may hold values from -0.125 to 0.125
- expert_ids: int32 [256, 8], P(('dp', 'tp')), may hold values from 0 to 15, all different within a row; in each aligned block of 8 rows (0 to 7, 8 to 15, ...) at most 5 rows name the same one
- gate_scores: float32 [256, 8], P(('dp', 'tp')), may hold values from 0.05 to 1
Outputs:
- context: bfloat16 [256, 128, 512], P(('dp', 'tp'))
- arrived: bfloat16 [64, 2, 256, 576], P(('dp', 'tp'))
- stream_out: bfloat16 [256, 7168], P(('dp', 'tp'))
Inputs may be any that keep to these rules, and one draw needn't show every extreme that they name: `mig_dest`: each device sends its 2 leaving requests to 2 different other devices of its dp index, and every device receives exactly 2 requests. `res_len`: some request holds all 256 positions. `leave_len`: some request holds all 256 positions. `expert_ids`: among the 8 rows of one device no expert is chosen by more than 5 rows, a bound that some block reaches; a row names 8 different experts.
All inputs are finite; a program needn't handle non-finite values.
Results may differ from a plain program's by a relative error of at most 0.023.
Values may be sent and summed in bfloat16 or wider, within the bound.
No kernel may reach another device: no remote copies, remote signals or barrier semaphores. Data moves between devices by JAX's collectives and lax.ppermute only.
A program may use at most 192 MiB of HBM per device.

v0:
```python
import jax
import jax.numpy as jnp
from jax import lax
from jax.sharding import PartitionSpec as P

VDIM = 512
QKD = 192


EPS = 1e-06
ROUTE_SCALE = 2.5


def rms_scale(rows, gain):
    values = rows.astype(jnp.float32)
    mean_square = jnp.mean(values * values, axis=-1, keepdims=True)
    return (values * lax.rsqrt(mean_square + EPS) * gain).astype(jnp.bfloat16)


def attend(queries, keys, lengths, newest):
    scale = QKD ** (-0.5)
    scores = jnp.einsum("rhl,rcl->rhc", queries, keys, preferred_element_type=jnp.float32) * scale
    positions = jnp.arange(keys.shape[1])
    valid = positions[None, None, :] < lengths[:, None, None]
    masked = jnp.where(valid, scores, -1e30)
    own_score = (
        jnp.einsum("rhl,rl->rh", queries, newest, preferred_element_type=jnp.float32) * scale
    )
    top = jnp.maximum(jnp.max(masked, axis=-1), own_score)
    expo = jnp.where(valid, jnp.exp(masked - top[..., None]), 0.0)
    own_expo = jnp.exp(own_score - top)
    total = jnp.sum(expo, axis=-1) + own_expo
    weights = (expo / total[..., None]).astype(jnp.bfloat16)
    own_weight = (own_expo / total).astype(jnp.bfloat16)
    context = jnp.einsum(
        "rhc,rcv->rhv", weights, keys[:, :, :VDIM], preferred_element_type=jnp.float32
    )
    context = context + own_weight.astype(jnp.float32)[..., None] * newest[:, None, :VDIM].astype(
        jnp.float32
    )
    return context.astype(jnp.bfloat16)


def on_device(
    queries,
    new_latent,
    resident,
    leaving,
    res_len,
    leave_len,
    mig_dest,
    stream,
    dense_gain,
    w_gate,
    w_up,
    w_down,
    moe_gain,
    expert_gate,
    expert_up,
    expert_down,
    expert_ids,
    gate_scores,
):
    tp_count = lax.axis_size("tp")
    dp_count = lax.axis_size("dp")
    tp_rank = lax.axis_index("tp")
    dp_rank = lax.axis_index("dp")
    moving = leaving.shape[0]
    device = dp_rank * tp_count + tp_rank
    peers = jnp.arange(tp_count)
    own_dest = lax.dynamic_index_in_dim(mig_dest, device, 0, keepdims=False)
    outgoing = jnp.zeros((tp_count,) + leaving.shape[1:], jnp.bfloat16)
    for slot in range(moving):
        outgoing = jnp.where(
            (peers == own_dest[slot])[:, None, None, None], leaving[slot][None], outgoing
        )
    incoming = lax.all_to_all(outgoing, "tp", split_axis=0, concat_axis=0, tiled=True)
    group_dest = lax.dynamic_slice_in_dim(mig_dest, dp_rank * tp_count, tp_count, 0)
    group_len = lax.dynamic_slice_in_dim(leave_len, dp_rank * tp_count, tp_count, 0)
    match = group_dest == tp_rank
    is_source = jnp.any(match, axis=1)
    which = jnp.sum(jnp.where(match, jnp.arange(moving)[None, :], 0), axis=1)
    order = jnp.cumsum(is_source.astype(jnp.int32)) - 1
    arrivals = []
    arrival_len = []
    for arrival in range(moving):
        pick = is_source & (order == arrival)
        source = jnp.sum(jnp.where(pick, peers, 0))
        slot = jnp.sum(jnp.where(pick, which, 0))
        arrivals.append(lax.dynamic_index_in_dim(incoming, source, 0, keepdims=False))
        source_len = lax.dynamic_index_in_dim(group_len, source, 0, keepdims=False)
        arrival_len.append(lax.dynamic_index_in_dim(source_len, slot, 0, keepdims=False))
    arrived = jnp.stack(arrivals, axis=0)
    arrived_len = jnp.stack(arrival_len, axis=0)
    stay = resident.shape[0]
    context_stay = attend(queries[:stay], resident, res_len, new_latent[:stay])
    context_moved = attend(queries[stay:], arrived[:, 0], arrived_len, new_latent[stay:])
    context = jnp.concatenate([context_stay, context_moved], axis=0)
    rows_dev = stream.shape[0]
    width = stream.shape[1]
    normed = rms_scale(stream, dense_gain)
    split = lax.all_to_all(normed[None, None], "dp", split_axis=3, concat_axis=1, tiled=True)
    gathered = lax.all_gather(split, "tp", axis=0, tiled=True)
    features = gathered.reshape(-1, gathered.shape[-1])
    gate_part = jnp.dot(features, w_gate, preferred_element_type=jnp.float32)
    up_part = jnp.dot(features, w_up, preferred_element_type=jnp.float32)
    gate, up = (
        lax.psum(gate_part.astype(jnp.bfloat16), "dp").astype(jnp.float32),
        lax.psum(up_part.astype(jnp.bfloat16), "dp").astype(jnp.float32),
    )
    hidden_all = (jax.nn.silu(gate) * up).astype(jnp.bfloat16)
    block = hidden_all
    ffn_share = lax.psum_scatter(
        jnp.dot(block, w_down, preferred_element_type=jnp.float32).astype(jnp.bfloat16),
        "tp",
        scatter_dimension=0,
        tiled=True,
    ).astype(jnp.float32)
    ffn_rows = lax.all_to_all(
        ffn_share.reshape(dp_count, rows_dev, ffn_share.shape[-1]).astype(jnp.bfloat16),
        "dp",
        split_axis=0,
        concat_axis=2,
        tiled=True,
    ).astype(jnp.float32)
    middle = (stream.astype(jnp.float32) + ffn_rows[0]).astype(jnp.bfloat16)
    mixed = rms_scale(middle, moe_gain)
    experts = expert_gate.shape[0] * tp_count
    top_count = expert_ids.shape[1]
    capacity = min(rows_dev, rows_dev * top_count // experts + 1)
    hits = (expert_ids[:, :, None] == jnp.arange(experts)[None, None, :]).astype(jnp.int32)
    row_hits = jnp.sum(hits, axis=1)
    before = jnp.cumsum(row_hits, axis=0) - row_hits
    slot_of = jnp.sum(hits * before[:, None, :], axis=2)
    target = expert_ids * capacity + slot_of
    placed = jnp.any(target[:, :, None] == jnp.arange(experts * capacity)[None, None, :], axis=1)
    outgoing_rows = jnp.dot(
        placed.T.astype(jnp.bfloat16), mixed, preferred_element_type=jnp.float32
    )
    outgoing_rows = outgoing_rows.astype(jnp.bfloat16).reshape(experts, capacity, width)
    received = lax.all_to_all(outgoing_rows, "tp", split_axis=0, concat_axis=0, tiled=True)
    pooled = lax.all_gather(received, "dp", axis=0, tiled=True)
    flat = pooled.reshape(-1, width)
    block = flat
    gate = jnp.dot(block, expert_gate[0], preferred_element_type=jnp.float32)
    up = jnp.dot(block, expert_up[0], preferred_element_type=jnp.float32)
    inner = (jax.nn.silu(gate) * up).astype(jnp.bfloat16)
    summed = lax.psum_scatter(
        jnp.dot(inner, expert_down[0], preferred_element_type=jnp.float32).astype(jnp.bfloat16),
        "dp",
        scatter_dimension=0,
        tiled=True,
    )
    results = summed.reshape(received.shape)
    returned = lax.all_to_all(results, "tp", split_axis=0, concat_axis=0, tiled=True)
    flat_back = returned.reshape(experts * capacity, width)
    picked = jnp.take(flat_back, target.reshape(-1), axis=0).reshape(rows_dev, top_count, width)
    shares = gate_scores / jnp.sum(gate_scores, axis=1, keepdims=True) * ROUTE_SCALE
    routed = jnp.einsum("rk,rkd->rd", shares, picked.astype(jnp.float32))
    stream_out = (middle.astype(jnp.float32) + routed).astype(jnp.bfloat16)
    return (context, arrived, stream_out)


def solution(mesh):
    placed = (
        P(("dp", "tp"), None, None),
        P(("dp", "tp"), None),
        P(("dp", "tp"), None, None),
        P(("dp", "tp"), None, None, None),
        P(("dp", "tp")),
        P(),
        P(),
        P(("dp", "tp"), None),
        P(),
        P("dp", "tp"),
        P("dp", "tp"),
        P("tp", "dp"),
        P(),
        P("tp", None, "dp"),
        P("tp", None, "dp"),
        P("tp", "dp", None),
        P(("dp", "tp"), None),
        P(("dp", "tp"), None),
    )
    return jax.shard_map(
        on_device,
        mesh=mesh,
        in_specs=placed,
        out_specs=(
            P(("dp", "tp"), None, None),
            P(("dp", "tp"), None, None, None),
            P(("dp", "tp"), None),
        ),
        check_vma=False,
    )
```

profile of v0, /device:TPU:0, one launch (start us, length us, event | category | flops | bytes accessed | tf_op | source)
XLA Modules:
  0.0 560.5 jit_solution(5394661257670916)
XLA Ops:
  9.3 6.0 %copy.62 = bf16[1,1,8,7168]{2,1,0,3:T(2,128)(2,1)} copy(bf16[1,1,8,7168]{3,2,1,0:T(8,128)(2,1)S(1)} %fusion.56) | data formatting | bytes 229376 | tf_op jit(solution)/shard_map/broadcast_in_dim | solution.py:102
  15.8 39.8 %reduce.4 = bf16[7168,8]{1,0:T(8,128)(2,1)S(1)} reduce(bf16[7168,1,1,8]{3,2,1,0:T(2,128)(2,1)} %bitcast.99, bf16[]{:T(256)} %broadcast.161), dimensions={1,2}, to_apply=%bitcast.80.reduce_sub_computation | reduce | bytes 229378
  55.6 1.9 reshape.230
  57.5 8.4 %all_to_all.42 = bf16[2,2,14336]{2,1,0:T(2,128)(2,1)S(1)} all-to-all(bf16[2,2,14336]{2,1,0:T(2,128)(2,1)S(1)} %reshape.230), channel_id=1, replica_groups=mesh['dp'=2,'tp'=16] {'dp'}, dimensions={0} | all-to-all | bytes 229376 | tf_op jit(solution)/shard_map/all_to_all | solution.py:102
  65.9 5.4 reshape.231
  71.3 6.8 %copy.63 = bf16[1,1,8,7168]{3,2,1,0:T(8,128)(2,1)S(1)} copy(bf16[1,1,8,7168]{2,1,0,3:T(2,128)(2,1)} %bitcast.100) | data formatting | bytes 229376 | tf_op jit(solution)/shard_map/all_to_all | solution.py:102
  79.1 40.9 %all-gather.6.cloned.1.call-done = bf16[16,2,1,8,3584]{4,3,2,1,0:T(8,128)(2,1)} async-done(((bf16[1,2,1,8,3584]{4,3,2,1,0:T(8,128)(2,1)}), bf16[16,2,1,8,3584]{4,3,2,1,0:T(8,128)(2,1)}) %all-gather.6.cloned.1.call-update) | async-done | bytes 1835024 | tf_op jit(solution)/shard_map/all_gather | solution.py:103
  119.9 7.4 %convolution_convert_fusion.2 = bf16[256,1152]{1,0:T(8,128)(2,1)} fusion(bf16[256,3584]{1,0:T(8,128)(2,1)} %bitcast.107, bf16[3584,1152]{1,0:T(8,128)(2,1)} %param.28), kind=kOutput, calls=%fused_computation.11 | convolution fusion | flops 2114224128 | bytes 10682368 | tf_op jit(solution)/shard_map/dot_general | solution.py:106
  127.3 6.8 %convolution_convert_fusion.3 = bf16[256,1152]{1,0:T(8,128)(2,1)} fusion(bf16[256,3584]{1,0:T(8,128)(2,1)S(1)} %bitcast.108, bf16[3584,1152]{1,0:T(8,128)(2,1)} %param.27), kind=kOutput, calls=%fused_computation.12 | convolution fusion | flops 2114224128 | bytes 10682368 | tf_op jit(solution)/shard_map/dot_general | solution.py:105
  134.2 41.9 %all-reduce.3.cloned.1.call-done = (bf16[256,1152]{1,0:T(8,128)(2,1)}, bf16[256,1152]{1,0:T(8,128)(2,1)}) async-done(((bf16[256,1152]{1,0:T(8,128)(2,1)}, bf16[256,1152]{1,0:T(8,128)(2,1)}), (bf16[256,1152]{1,0:T(8,128)(2,1)}, bf16[256,1152]{1,0:T(8,128)(2,1)})) %all-reduce.3.cloned.1.call-update) | async-done | bytes 1179664 | tf_op jit(solution)/shard_map/psum | solution.py:109
  176.0 7.6 %convolution_convert_fusion.1 = bf16[256,3584]{1,0:T(8,128)(2,1)} fusion(bf16[1152,3584]{1,0:T(8,128)(2,1)} %param.29, bf16[256,1152]{1,0:T(8,128)(2,1)} %get-tuple-element.24, bf16[256,1152]{1,0:T(8,128)(2,1)} %get-tuple-element.25), kind=kOutput, calls=%fused_computation.10 | convolution fusion | flops 2117206016 | bytes 11272192 | tf_op jit(solution)/shard_map/dot_general | solution.py:114
  184.7 59.6 %reduce-scatter.3.cloned.1.call-done = bf16[16,3584]{1,0:T(8,128)(2,1)} async-done(((bf16[256,3584]{1,0:T(8,128)(2,1)}), bf16[16,3584]{1,0:T(8,128)(2,1)}) %reduce-scatter.3.cloned.1.call-update) | async-done | bytes 114704 | tf_op jit(solution)/shard_map/reduce_scatter | solution.py:113
  244.3 3.4 all-to-all-start.2
  247.8 4.3 all-to-all-done.2
  254.3 3.8 all-to-all-start.3
  260.2 4.9 select_select_fusion
  265.1 29.6 %all-to-all-done.3 = bf16[16,5,7168]{2,1,0:T(8,128)(2,1)S(1)} async-done(((bf16[16,5,7168]{2,1,0:T(8,128)(2,1)}), bf16[16,5,7168]{2,1,0:T(8,128)(2,1)S(1)}, u32[]{:S(2)}, u32[]{:S(2)}) %all-to-all-start.3) | async-done | bytes 1146912 | tf_op jit(solution)/shard_map/all_to_all | solution.py:141
  294.7 10.2 %all-to-all-start = ((bf16[16,2,256,576]{2,3,1,0:T(8,128)(2,1)}), bf16[16,2,256,576]{2,3,1,0:T(8,128)(2,1)}, u32[]{:S(2)}, u32[]{:S(2)}) async-start(bf16[16,2,256,576]{2,3,1,0:T(8,128)(2,1)} %select_select_fusion), calls=%async_computation | async-start | bytes 18874368 | tf_op jit(solution)/shard_map/all_to_all | solution.py:77
  304.9 1.8 copy.65
  307.0 36.3 %all-gather.4.cloned.1.call-done = bf16[32,5,7168]{2,0,1:T(8,128)(2,1)} async-done(((bf16[16,5,7168]{2,0,1:T(8,128)(2,1)}), bf16[32,5,7168]{2,0,1:T(8,128)(2,1)}) %all-gather.4.cloned.1.call-update) | async-done | bytes 2293776 | tf_op jit(solution)/shard_map/all_gather | solution.py:142
  343.3 4.8 copy.66
  348.1 3.3 reshape.205
  351.4 7.9 %fusion.4 = f32[160,1024]{1,0:T(8,128)S(1)} fusion(bf16[160,7168]{1,0:T(8,128)(2,1)S(1)} %reshape.205, bf16[1,7168,1024]{2,1,0:T(8,128)(2,1)} %param.31), kind=kOutput, calls=%fused_computation.5 | convolution fusion | flops 2348810240 | bytes 17629184 | tf_op jit(solution)/shard_map/dot_general | solution.py:145
  359.3 7.9 %fusion.17 = bf16[160,1024]{1,0:T(8,128)(2,1)S(1)} fusion(bf16[160,7168]{1,0:T(8,128)(2,1)S(1)} %reshape.205, bf16[1,7168,1024]{2,1,0:T(8,128)(2,1)} %param.32, f32[160,1024]{1,0:T(8,128)S(1)} %fusion.4), kind=kOutput, calls=%fused_computation.25 | convolution fusion | flops 2349793280 | bytes 17956864 | tf_op jit(solution)/shard_map/dot_general | solution.py:146
  367.3 4.0 fusion.6
  382.7 2.1 fusion.81
  385.4 20.1 %reduce-scatter.5.cloned.1.call-done = bf16[80,7168]{1,0:T(8,128)(2,1)} async-done(((bf16[160,7168]{1,0:T(8,128)(2,1)}), bf16[80,7168]{1,0:T(8,128)(2,1)}) %reduce-scatter.5.cloned.1.call-update) | async-done | bytes 1146896 | tf_op jit(solution)/shard_map/reduce_scatter | solution.py:148
  405.5 2.6 reshape.206
  408.0 65.8 %all-to-all-done = bf16[16,2,256,576]{2,3,1,0:T(8,128)(2,1)} async-done(((bf16[16,2,256,576]{2,3,1,0:T(8,128)(2,1)}), bf16[16,2,256,576]{2,3,1,0:T(8,128)(2,1)}, u32[]{:S(2)}, u32[]{:S(2)}) %all-to-all-start) | async-done | bytes 9437216 | tf_op jit(solution)/shard_map/all_to_all | solution.py:77
  473.9 40.7 %all-to-all-start.4 = ((bf16[16,5,7168]{2,1,0:T(8,128)(2,1)}), bf16[16,5,7168]{2,1,0:T(8,128)(2,1)S(1)}, u32[]{:S(2)}, u32[]{:S(2)}) async-start(bf16[16,5,7168]{2,1,0:T(8,128)(2,1)} %reshape.206), calls=%async_computation.6 | async-start | bytes 3670016 | tf_op jit(solution)/shard_map/all_to_all | solution.py:155
  514.7 2.3 add_convert_fusion
  521.8 29.4 %all-to-all-done.4 = bf16[16,5,7168]{2,1,0:T(8,128)(2,1)S(1)} async-done(((bf16[16,5,7168]{2,1,0:T(8,128)(2,1)}), bf16[16,5,7168]{2,1,0:T(8,128)(2,1)S(1)}, u32[]{:S(2)}, u32[]{:S(2)}) %all-to-all-start.4) | async-done | bytes 1146912 | tf_op jit(solution)/shard_map/all_to_all | solution.py:155
  (103 shorter events, 21.2 us)
Async XLA Ops:
  7.2 112.8 %all-gather.6.cloned.1.call-start = ((), (), s32[]{:S(2)}) async-start(), calls=%async_computation.10 | async-start | bytes 1949696 | tf_op jit(solution)/shard_map/all_gather | solution.py:103
  78.8 97.2 %all-reduce.3.cloned.1.call-start = ((), (), s32[]{:S(2)}) async-start(), calls=%async_computation.11 | async-start | bytes 2359296 | tf_op jit(solution)/shard_map/psum | solution.py:109
  119.9 7.4 %copy-start.11 = (bf16[16,2,1,8,3584]{4,3,2,1,0:T(8,128)(2,1)S(1)}, bf16[16,2,1,8,3584]{4,3,2,1,0:T(8,128)(2,1)}, u32[]{:S(2)}) copy-start(bf16[16,2,1,8,3584]{4,3,2,1,0:T(8,128)(2,1)} %all-gather.6.cloned.1.call-done) | copy-start | bytes 5505028
  134.1 110.2 %reduce-scatter.3.cloned.1.call-start = ((), (), s32[]{:S(2)}) async-start(), calls=%async_computation.7 | async-start | bytes 1949696 | tf_op jit(solution)/shard_map/reduce_scatter | solution.py:113
  183.6 0.7 copy-start.5
  183.6 68.5 %copy-start.2 = (bf16[8,7168]{1,0:T(8,128)(2,1)S(1)}, bf16[8,7168]{1,0:T(8,128)(2,1)}, u32[]{:S(2)}) copy-start(bf16[8,7168]{1,0:T(8,128)(2,1)} %param.25) | copy-start | bytes 344068
  183.6 68.7 %copy-start.6 = (f32[7168]{0:T(1024)S(1)}, f32[7168]{0:T(1024)}, u32[]{:S(2)}) copy-start(f32[7168]{0:T(1024)} %param.30) | copy-start | bytes 86020
  244.3 7.7 %all-to-all-start.2 = ((bf16[2,8,3584]{2,1,0:T(8,128)(2,1)}), bf16[2,8,3584]{2,1,0:T(8,128)(2,1)S(1)}, u32[]{:S(2)}, u32[]{:S(2)}) async-start(bf16[2,8,3584]{2,1,0:T(8,128)(2,1)} %bitcast.103), calls=%async_computation.3 | async-start | bytes 229376 | tf_op jit(solution)/shard_map/all_to_all | solution.py:119
  254.3 3.9 copy-start.8
  254.3 5.8 %copy-start.1 = (bf16[2,2,256,576]{2,3,1,0:T(8,128)(2,1)S(1)}, bf16[2,2,256,576]{2,3,1,0:T(8,128)(2,1)}, u32[]{:S(2)}) copy-start(bf16[2,2,256,576]{2,3,1,0:T(8,128)(2,1)} %param.21) | copy-start | bytes 3538948
  254.3 40.4 %all-to-all-start.3 = ((bf16[16,5,7168]{2,1,0:T(8,128)(2,1)}), bf16[16,5,7168]{2,1,0:T(8,128)(2,1)S(1)}, u32[]{:S(2)}, u32[]{:S(2)}) async-start(bf16[16,5,7168]{2,1,0:T(8,128)(2,1)} %reshape.204), calls=%async_computation.4 | async-start | bytes 3670016 | tf_op jit(solution)/shard_map/all_to_all | solution.py:141
  294.7 179.2 %all-to-all-start = ((bf16[16,2,256,576]{2,3,1,0:T(8,128)(2,1)}), bf16[16,2,256,576]{2,3,1,0:T(8,128)(2,1)}, u32[]{:S(2)}, u32[]{:S(2)}) async-start(bf16[16,2,256,576]{2,3,1,0:T(8,128)(2,1)} %select_select_fusion), calls=%async_computation | async-start | bytes 18874368 | tf_op jit(solution)/shard_map/all_to_all | solution.py:77
  304.9 38.4 %all-gather.4.cloned.1.call-start = ((), (), s32[]{:S(2)}) async-start(), calls=%async_computation.8 | async-start | bytes 3440640 | tf_op jit(solution)/shard_map/all_gather | solution.py:142
  306.7 98.7 %reduce-scatter.5.cloned.1.call-start = ((), (), s32[]{:S(2)}) async-start(), calls=%async_computation.9 | async-start | bytes 3440640 | tf_op jit(solution)/shard_map/reduce_scatter | solution.py:148
  351.4 15.8 %slice-start = ((s8[14680064]{0:T(1024)(128)(4,1)}), s8[4194304]{0:T(1024)(128)(4,1)S(1)}, s32[]{:S(2)}) async-start(s8[14680064]{0:T(1024)(128)(4,1)} %bitcast.97), calls=%async_computation.12 | async-start | bytes 8388608
  351.4 15.8 %slice-start.1 = ((s8[14680064]{0:T(1024)(128)(4,1)}), s8[4194304]{0:T(1024)(128)(4,1)S(1)}, s32[]{:S(2)}) async-start(s8[14680064]{0:T(1024)(128)(4,1)} %bitcast.97), calls=%async_computation.13 | async-start | bytes 8388608
  359.3 8.0 %slice-start.2 = ((s8[14680064]{0:T(1024)(128)(4,1)}), s8[4194304]{0:T(1024)(128)(4,1)S(1)}, s32[]{:S(2)}) async-start(s8[14680064]{0:T(1024)(128)(4,1)} %bitcast.97), calls=%async_computation.14 | async-start | bytes 8388608
  359.3 8.0 %slice-start.3 = ((s8[14680064]{0:T(1024)(128)(4,1)}), s8[2097152]{0:T(1024)(128)(4,1)S(1)}, s32[]{:S(2)}) async-start(s8[14680064]{0:T(1024)(128)(4,1)} %bitcast.97), calls=%async_computation.15 | async-start | bytes 4194304
  371.3 9.0 %copy-start.7 = (f32[8,8]{1,0:T(8,128)S(1)}, f32[8,8]{1,0:T(8,128)}, u32[]{:S(2)}) copy-start(f32[8,8]{1,0:T(8,128)} %param.35) | copy-start | bytes 772
  371.3 9.1 %copy-start.9 = (s32[32,2]{0,1:T(2,128)S(1)}, s32[32,2]{0,1:T(2,128)}, u32[]{:S(2)}) copy-start(s32[32,2]{0,1:T(2,128)} %param.23) | copy-start | bytes 772
  371.3 11.1 %copy-start.10 = (s32[6]{0:T(128)S(1)}, s32[6]{0:T(128)}, u32[]{:S(2)}) copy-start(s32[6]{0:T(128)} %param.22) | copy-start | bytes 76
  371.3 11.2 %copy-start.4 = (bf16[8,576]{1,0:T(8,128)(2,1)S(1)}, bf16[8,576]{1,0:T(8,128)(2,1)}, u32[]{:S(2)}) copy-start(bf16[8,576]{1,0:T(8,128)(2,1)} %param.19) | copy-start | bytes 27652
  371.3 11.2 %copy-start = (bf16[8,128,576]{1,2,0:T(8,128)(2,1)S(1)}, bf16[8,128,576]{1,2,0:T(8,128)(2,1)}, u32[]{:S(2)}) copy-start(bf16[8,128,576]{1,2,0:T(8,128)(2,1)} %param.18) | copy-start | bytes 3538948
  384.8 23.3 %copy-start.3 = (f32[6,128,256]{2,1,0:T(8,128)}, f32[6,128,256]{2,1,0:T(8,128)S(1)}, u32[]{:S(2)}) copy-start(f32[6,128,256]{2,1,0:T(8,128)S(1)} %get-tuple-element.47) | copy-start | bytes 2359300
  473.9 77.3 %all-to-all-start.4 = ((bf16[16,5,7168]{2,1,0:T(8,128)(2,1)}), bf16[16,5,7168]{2,1,0:T(8,128)(2,1)S(1)}, u32[]{:S(2)}, u32[]{:S(2)}) async-start(bf16[16,5,7168]{2,1,0:T(8,128)(2,1)} %reshape.206), calls=%async_computation.6 | async-start | bytes 3670016 | tf_op jit(solution)/shard_map/all_to_all | solution.py:155
Sparse Core Ops, SparseCore 0:
  78.9 40.9 all-gather.5
  134.2 41.7 all-reduce.2
  183.7 60.5 reduce-scatter.2
  307.6 35.6 all-gather.3
  371.4 33.9 reduce-scatter.4
where the time goes:
time: 566 us; the launch traced here: 560 us
  waiting for transfers between devices  328 us (58%)
  starting transfers between devices  58.7 us (10%)
  other arithmetic  53.9 us (10%)
  matrix products  48.2 us (9%)
  local copies, waits for them, and re-layouts  41.5 us (7%)
  between operations  21.9 us (4%)
  blocking collectives  8.39 us (1%)
    all_to_all x1, waiting for transfers between devices, on_device(): lax.all_to_all(outgoing, 'tp', split_axis=0, concat_axis=0, tiled=True)  65.8 us
    reduce_scatter x1, waiting for transfers between devices, on_device(): lax.psum_scatter(jnp.dot(block, w_down, preferred_element_type=jnp.float3...  59.6 us
    psum x1, waiting for transfers between devices, on_device(): lax.psum(up_part.astype(jnp.bfloat16), 'dp').astype(jnp.float32)  41.9 us
    all_gather x1, waiting for transfers between devices, on_device(): gathered = lax.all_gather(split, 'tp', axis=0, tiled=True)  40.9 us
    all_to_all x1, starting transfers between devices, on_device(): lax.all_to_all(results, 'tp', split_axis=0, concat_axis=0, tiled=True)  40.7 us
    unnamed x2, other arithmetic  39.8 us
    all_gather x1, waiting for transfers between devices, on_device(): pooled = lax.all_gather(received, 'dp', axis=0, tiled=True)  36.3 us
    all_to_all x1, waiting for transfers between devices, on_device(): lax.all_to_all(outgoing_rows, 'tp', split_axis=0, concat_axis=0, tiled=True)  29.6 us
  transfers between devices with their start and end apart: 9, of which 9 were waited for; matrix products, arithmetic and copies ran while one was open for 9% of the time, Pallas kernels for 0%

commit v1 on v0

v1 whole, which is shorter than its diff:
```python
import jax
import jax.numpy as jnp
from jax import lax
from jax.sharding import PartitionSpec as P

VDIM = 512
QKD = 192


EPS = 1e-06
ROUTE_SCALE = 2.5
AXES = ("dp", "tp")


def rms_scale(rows, gain):
    values = rows.astype(jnp.float32)
    mean_square = jnp.mean(values * values, axis=-1, keepdims=True)
    return (values * lax.rsqrt(mean_square + EPS) * gain).astype(jnp.bfloat16)


def attend(queries, keys, lengths, newest):
    scale = QKD ** (-0.5)
    scores = jnp.einsum("rhl,rcl->rhc", queries, keys, preferred_element_type=jnp.float32) * scale
    positions = jnp.arange(keys.shape[1])
    valid = positions[None, None, :] < lengths[:, None, None]
    masked = jnp.where(valid, scores, -1e30)
    own_score = (
        jnp.einsum("rhl,rl->rh", queries, newest, preferred_element_type=jnp.float32) * scale
    )
    top = jnp.maximum(jnp.max(masked, axis=-1), own_score)
    expo = jnp.where(valid, jnp.exp(masked - top[..., None]), 0.0)
    own_expo = jnp.exp(own_score - top)
    total = jnp.sum(expo, axis=-1) + own_expo
    weights = (expo / total[..., None]).astype(jnp.bfloat16)
    own_weight = (own_expo / total).astype(jnp.bfloat16)
    context = jnp.einsum(
        "rhc,rcv->rhv", weights, keys[:, :, :VDIM], preferred_element_type=jnp.float32
    )
    context = context + own_weight.astype(jnp.float32)[..., None] * newest[:, None, :VDIM].astype(
        jnp.float32
    )
    return context.astype(jnp.bfloat16)


def swap(block, q, j):
    dp_count, tp_count = lax.axis_size("dp"), lax.axis_size("tp")
    pairs = [
        (p * tp_count + t, (p ^ q) * tp_count + (t ^ j))
        for p in range(dp_count)
        for t in range(tp_count)
    ]
    return lax.ppermute(block, AXES, pairs)


def far_masks():
    return range(4, lax.axis_size("tp"), 4)


def quad():
    return [(q, y) for q in range(lax.axis_size("dp")) for y in (0, 2) if (q, y) != (0, 0)]


def gather_far(rows):
    return jnp.stack([rows] + [swap(rows, 0, j) for j in far_masks()], axis=0)


def feature_part(rows, part, count):
    size = rows.shape[-1] // count
    return lax.dynamic_slice_in_dim(rows, part * size, size, axis=rows.ndim - 1)


def gather_parts(rows, dp_rank, dp_count):
    width = rows.shape[1]
    far = gather_far(rows).reshape(-1, width)
    parts = [feature_part(far, dp_rank, dp_count)]
    for q, y in quad():
        parts.append(swap(feature_part(far, dp_rank ^ q, dp_count), q, y))
    near = jnp.concatenate(parts, axis=0)
    return jnp.concatenate([near, swap(near, 0, 1)], axis=0)


def gather_rows(rows):
    far = gather_far(rows).reshape(-1, rows.shape[1])
    near = jnp.concatenate([far] + [swap(far, q, y) for q, y in quad()], axis=0)
    return jnp.concatenate([near, swap(near, 0, 1)], axis=0)


def realign(rows, q, dp_count):
    blocks = rows.reshape(2, dp_count, -1, rows.shape[1])
    return jnp.concatenate([blocks[:, at ^ q][:, None] for at in range(dp_count)], axis=1).reshape(rows.shape)


def wide(block):
    return block.astype(jnp.float32)


def reduce_core(total):
    half = total.shape[0] // 2
    got = swap(total[half:], 0, 1)
    return wide(total[:half]) + wide(got)


def reduce_far(total):
    out = total[0]
    for at, j in enumerate(far_masks()):
        out = out + wide(swap(total[at + 1].astype(jnp.bfloat16), 0, j))
    return out


def reduce_parts(total, dp_rank, dp_count, rows_dev):
    size = total.shape[1]
    near = reduce_core(total).reshape(dp_count, 2, -1, size)
    full = jnp.zeros((near.shape[2], size * dp_count), jnp.float32)
    for q in range(dp_count):
        if q == 0:
            part = near[0, 0]
        else:
            part = wide(swap(near[q, 0].astype(jnp.bfloat16), q, 0))
        part = part + wide(swap(near[q, 1].astype(jnp.bfloat16), q, 2))
        full = lax.dynamic_update_slice_in_dim(full, part, (dp_rank ^ q) * size, axis=1)
    return reduce_far(full.reshape(-1, rows_dev, size * dp_count))


def reduce_rows(total, dp_count, rows_dev):
    width = total.shape[1]
    near = reduce_core(total).reshape(dp_count, 2, -1, width)
    out = near[0, 0]
    for q, y in quad():
        out = out + wide(swap(near[q, y // 2].astype(jnp.bfloat16), q, y))
    return reduce_far(out.reshape(-1, rows_dev, width))


def migrate(leaving, group_dest, tp_rank):
    tp_count = lax.axis_size("tp")
    moving, layers, cache, lat = leaving.shape
    piece = layers * cache // tp_count
    outgoing = leaving.reshape(moving, tp_count, piece, lat).transpose(1, 0, 2, 3)
    spread = lax.all_to_all(outgoing, "tp", split_axis=0, concat_axis=0, tiled=True)
    packets = tp_count * moving
    dest = group_dest.reshape(-1)
    sender = jnp.arange(packets) // moving
    same = (dest[:, None] == dest[None, :]) & (sender[None, :] < sender[:, None])
    order = jnp.sum(same.astype(jnp.int32), axis=1)
    place = dest * moving + order
    source = jnp.sum(
        jnp.where(place[None, :] == jnp.arange(packets)[:, None], jnp.arange(packets)[None, :], 0),
        axis=1,
    )
    homing = jnp.take(spread.reshape(packets, piece, lat), source, axis=0)
    homing = homing.reshape(tp_count, moving, piece, lat)
    home = lax.all_to_all(homing, "tp", split_axis=0, concat_axis=0, tiled=True)
    arrived = home.transpose(1, 0, 2, 3).reshape(moving, layers, cache, lat)
    mine = lax.dynamic_slice_in_dim(source, tp_rank * moving, moving, 0)
    return arrived, mine


def on_device(
    queries,
    new_latent,
    resident,
    leaving,
    res_len,
    leave_len,
    mig_dest,
    stream,
    dense_gain,
    w_gate,
    w_up,
    w_down,
    moe_gain,
    expert_gate,
    expert_up,
    expert_down,
    expert_ids,
    gate_scores,
):
    tp_count = lax.axis_size("tp")
    dp_count = lax.axis_size("dp")
    tp_rank = lax.axis_index("tp")
    dp_rank = lax.axis_index("dp")
    group_dest = lax.dynamic_slice_in_dim(mig_dest, dp_rank * tp_count, tp_count, 0)
    group_len = lax.dynamic_slice_in_dim(leave_len, dp_rank * tp_count, tp_count, 0)
    arrived, mine = migrate(leaving, group_dest, tp_rank)
    arrived_len = jnp.take(group_len.reshape(-1), mine, axis=0)
    stay = resident.shape[0]
    context_stay = attend(queries[:stay], resident, res_len, new_latent[:stay])
    context_moved = attend(queries[stay:], arrived[:, 0], arrived_len, new_latent[stay:])
    context = jnp.concatenate([context_stay, context_moved], axis=0)

    rows_dev = stream.shape[0]
    normed = rms_scale(stream, dense_gain)
    features = gather_parts(normed, dp_rank, dp_count)
    gate_part = jnp.dot(features, w_gate, preferred_element_type=jnp.float32)
    up_part = jnp.dot(features, w_up, preferred_element_type=jnp.float32)
    gate, up = gate_part, up_part
    for q in range(1, dp_count):
        gate = gate + wide(realign(swap(gate_part.astype(jnp.bfloat16), q, 0), q, dp_count))
        up = up + wide(realign(swap(up_part.astype(jnp.bfloat16), q, 0), q, dp_count))
    hidden = (jax.nn.silu(gate) * up).astype(jnp.bfloat16)
    down = jnp.dot(hidden, w_down, preferred_element_type=jnp.float32).astype(jnp.bfloat16)
    ffn = reduce_parts(down, dp_rank, dp_count, rows_dev)
    middle = (stream.astype(jnp.float32) + ffn).astype(jnp.bfloat16)
    mixed = rms_scale(middle, moe_gain)

    shares = gate_scores / jnp.sum(gate_scores, axis=1, keepdims=True) * ROUTE_SCALE
    experts = tp_count * expert_gate.shape[0]
    chosen = expert_ids[:, :, None] == jnp.arange(experts)[None, None, :]
    table = jnp.sum(jnp.where(chosen, shares[:, :, None], 0.0), axis=1)
    high = table.astype(jnp.bfloat16)
    low = (table - wide(high)).astype(jnp.bfloat16)
    tail = jnp.pad(jnp.concatenate([high, low], axis=1), ((0, 0), (0, 128 - 2 * experts)))
    payload = jnp.concatenate([mixed, tail], axis=1)

    gathered = gather_rows(payload)
    width = mixed.shape[1]
    pooled = gathered[:, :width]
    lane = jnp.arange(128)
    mine_lane = (lane == tp_rank) | (lane == tp_rank + experts)
    row_share = jnp.sum(jnp.where(mine_lane, wide(gathered[:, width:]), 0.0), axis=1, keepdims=True)
    gate = jnp.dot(pooled, expert_gate[0], preferred_element_type=jnp.float32)
    up = jnp.dot(pooled, expert_up[0], preferred_element_type=jnp.float32)
    inner = (jax.nn.silu(gate) * up * row_share).astype(jnp.bfloat16)
    part = jnp.dot(inner, expert_down[0], preferred_element_type=jnp.float32).astype(jnp.bfloat16)
    routed = reduce_rows(part, dp_count, rows_dev)
    stream_out = (middle.astype(jnp.float32) + routed).astype(jnp.bfloat16)
    return (context, arrived, stream_out)


def solution(mesh):
    placed = (
        P(("dp", "tp"), None, None),
        P(("dp", "tp"), None),
        P(("dp", "tp"), None, None),
        P(("dp", "tp"), None, None, None),
        P(("dp", "tp")),
        P(),
        P(),
        P(("dp", "tp"), None),
        P(),
        P("dp", "tp"),
        P("dp", "tp"),
        P("tp", "dp"),
        P(),
        P("tp", None, "dp"),
        P("tp", None, "dp"),
        P("tp", "dp", None),
        P(("dp", "tp"), None),
        P(("dp", "tp"), None),
    )
    return jax.shard_map(
        on_device,
        mesh=mesh,
        in_specs=placed,
        out_specs=(
            P(("dp", "tp"), None, None),
            P(("dp", "tp"), None, None, None),
            P(("dp", "tp"), None),
        ),
        check_vma=False,
    )
```

time: 566 us -> 252 us (0.45)
  waiting for transfers between devices: 328 us -> 123 us
  other arithmetic: 53.9 us -> 14.5 us
  local copies, waits for them, and re-layouts: 41.5 us -> 20.4 us
  between operations: 21.9 us -> 1.34 us
  starting transfers between devices: 58.7 us -> 47.2 us
  blocking collectives: 8.39 us -> 0 us
    all_to_all x4 -> x2, waiting for transfers between devices: 129 us -> 0.01 us  [the longest x1 0.01 us: migrate(): lax.all_to_all(outgoing, 'tp', split_axis=0, concat_axis=0, tiled=True)]
    ppermute x0 -> x30, waiting for transfers between devices: none -> 123 us  [swap(): return lax.ppermute(block, AXES, pairs)]
    reduce_scatter x2 -> x0, waiting for transfers between devices: 79.7 us -> none  [the longest x1 59.6 us: on_device(): lax.psum_scatter(jnp.dot(block, w_down, preferred_element_type=jnp.float3...]
    all_gather x2 -> x0, waiting for transfers between devices: 77.2 us -> none  [the longest x1 40.9 us: on_device(): gathered = lax.all_gather(split, 'tp', axis=0, tiled=True)]
    all_to_all x4 -> x2, starting transfers between devices: 58.1 us -> 10.2 us  [the longest x1 6.35 us: migrate(): lax.all_to_all(outgoing, 'tp', split_axis=0, concat_axis=0, tiled=True)]
    psum x1 -> x0, waiting for transfers between devices: 41.9 us -> none  [on_device(): lax.psum(up_part.astype(jnp.bfloat16), 'dp').astype(jnp.float32)]
    unnamed x2 -> x3, other arithmetic: 39.8 us -> 0.05 us
    ppermute x0 -> x30, starting transfers between devices: none -> 37 us  [swap(): return lax.ppermute(block, AXES, pairs)]
  transfers between devices with their start and end apart: 9 -> 32, of which waited for: 9 -> 17; matrix products, arithmetic and copies ran while one was open for 9% -> 27% of each run, Pallas kernels for 0% -> 0%
where the time goes in v1:
time: 252 us
  waiting for transfers between devices  123 us (49%)
  starting transfers between devices  47.2 us (19%)
  matrix products  44.8 us (18%)
  local copies, waits for them, and re-layouts  20.4 us (8%)
  other arithmetic  14.5 us (6%)
    ppermute x30, waiting for transfers between devices, swap(): return lax.ppermute(block, AXES, pairs)  123 us
    ppermute x30, starting transfers between devices, swap(): return lax.ppermute(block, AXES, pairs)  37 us
    dot_general x1, matrix products, on_device(): jnp.dot(inner, expert_down[0], preferred_element_type=jnp.float32)  20.4 us
    unnamed x60, local copies, waits for them, and re-layouts  9.86 us
    dot_general x1, matrix products, on_device(): up = jnp.dot(pooled, expert_up[0], preferred_element_type=jnp.float32)  9.77 us
    all_to_all x1, starting transfers between devices, migrate(): lax.all_to_all(outgoing, 'tp', split_axis=0, concat_axis=0, tiled=True)  6.35 us
    dot_general x1, matrix products, on_device(): gate_part = jnp.dot(features, w_gate, preferred_element_type=jnp.float32)  6.09 us
  transfers between devices with their start and end apart: 32, of which 17 were waited for; matrix products, arithmetic and copies ran while one was open for 27% of the time, Pallas kernels for 0%

profile of v1, /device:TPU:0, one launch (start us, length us, event | category | flops | bytes accessed | tf_op | source)
XLA Modules:
  0.0 251.7 jit_solution(8134396552333776046)
XLA Ops:
  2.7 3.1 %collective-permute-start = (bf16[8,7168]{1,0:T(8,128)(2,1)S(1)}, bf16[8,7168]{1,0:T(8,128)(2,1)S(1)}, u32[]{:S(2)}, u32[]{:S(2)}) collective-permute-start(bf16[8,7168]{1,0:T(8,128)(2,1)S(1)} %fusion.48), channel_id=1, source_target_pairs={{0,4},{1,5},{2,6},{3,7},{4,0},{5,1},{6,2},{7,3},{8,12},{9,13},{10,... | collective-permute-start | bytes 344072 | tf_op jit(solution)/shard_map/ppermute | solution.py:52
  5.8 2.6 %collective-permute-start.1 = (bf16[8,7168]{1,0:T(8,128)(2,1)S(1)}, bf16[8,7168]{1,0:T(8,128)(2,1)S(1)}, u32[]{:S(2)}, u32[]{:S(2)}) collective-permute-start(bf16[8,7168]{1,0:T(8,128)(2,1)S(1)} %fusion.48), channel_id=1, source_target_pairs={{0,8},{1,9},{2,10},{3,11},{4,12},{5,13},{6,14},{7,15},{8,0},{9,1},... | collective-permute-start | bytes 344072 | tf_op jit(solution)/shard_map/ppermute | solution.py:52
  11.4 6.3 %all-to-all-start = ((bf16[16,2,32,576]{3,2,1,0:T(8,128)(2,1)}), bf16[16,2,32,576]{3,2,1,0:T(8,128)(2,1)}, u32[]{:S(2)}, u32[]{:S(2)}) async-start(bf16[16,2,32,576]{3,2,1,0:T(8,128)(2,1)} %copy.52), calls=%async_computation | async-start | bytes 2621440 | tf_op jit(solution)/shard_map/all_to_all | solution.py:138
  23.6 1.8 collective-permute-start.5
  25.7 16.8 %collective-permute-done.3 = bf16[32,3584]{1,0:T(8,128)(2,1)S(1)} collective-permute-done((bf16[32,3584]{1,0:T(8,128)(2,1)S(1)}, bf16[32,3584]{1,0:T(8,128)(2,1)S(1)}, u32[]{:S(2)}, u32[]{:S(2)}) %collective-permute-start.3) | collective-permute-done | bytes 229408 | tf_op jit(solution)/shard_map/ppermute | solution.py:52
  42.7 2.4 collective-permute-done.6
  45.2 6.1 %fusion.94 = (bf16[256,1152]{1,0:T(8,128)(2,1)S(1)}, f32[256,1152]{1,0:T(8,128)S(1)}) fusion(bf16[256,3584]{1,0:T(8,128)(2,1)S(1)} %constant_dynamic-update-slice_fusion, bf16[3584,1152]{1,0:T(8,128)(2,1)} %param.27), kind=kOutput, calls=%fused_computation.170 | convolution fusion | flops 2114224128 | bytes 11862016 | tf_op jit(solution)/shard_map/dot_general | solution.py:193
  52.9 2.5 %fusion.93 = (bf16[256,1152]{1,0:T(8,128)(2,1)S(1)}, f32[256,1152]{1,0:T(8,128)S(1)}) fusion(bf16[256,3584]{1,0:T(8,128)(2,1)S(1)} %constant_dynamic-update-slice_fusion, bf16[3584,1152]{1,0:T(8,128)(2,1)S(1)} %bitcast.145), kind=kOutput, calls=%fused_computation.169 | convolution fusion | flops 2114224128 | bytes 11862016 | tf_op jit(solution)/shard_map/dot_general | solution.py:194
  56.1 11.5 %collective-permute-done.7 = bf16[256,1152]{1,0:T(8,128)(2,1)S(1)} collective-permute-done((bf16[256,1152]{1,0:T(8,128)(2,1)S(1)}, bf16[256,1152]{1,0:T(8,128)(2,1)S(1)}, u32[]{:S(2)}, u32[]{:S(2)}) %collective-permute-start.7) | collective-permute-done | bytes 589856 | tf_op jit(solution)/shard_map/ppermute | solution.py:52
  67.6 11.8 %collective-permute-done.8 = bf16[256,1152]{1,0:T(8,128)(2,1)S(1)} collective-permute-done((bf16[256,1152]{1,0:T(8,128)(2,1)S(1)}, bf16[256,1152]{1,0:T(8,128)(2,1)S(1)}, u32[]{:S(2)}, u32[]{:S(2)}) %collective-permute-start.8) | collective-permute-done | bytes 589856 | tf_op jit(solution)/shard_map/ppermute | solution.py:52
  79.6 2.7 %convolution_convert_fusion = bf16[256,3584]{1,0:T(8,128)(2,1)S(1)} fusion(bf16[1152,3584]{1,0:T(8,128)(2,1)S(1)} %bitcast.147, f32[256,1152]{1,0:T(8,128)S(1)} %get-tuple-element.51, bf16[256,1152]{1,0:T(8,128)(2,1)S(1)} %bitcast.132, f32[256,1152]{1,0:T(8,128)S(1)} %get-tuple-element.53, bf16[256,1152]{1,0:T(8,128)(2,1)S(1)} %bitcast.131), kind=kOutput, calls=%fused_computation.9 | convolution fusion | flops 2117795840 | bytes 13631488 | tf_op jit(solution)/shard_map/dot_general | solution.py:200
  86.3 1.7 convert_add_fusion.1
  89.0 2.5 collective-permute-start.10
  93.1 4.6 %collective-permute-done.10 = bf16[32,3584]{1,0:T(8,128)(2,1)} collective-permute-done((bf16[32,3584]{1,0:T(8,128)(2,1)}, bf16[32,3584]{1,0:T(8,128)(2,1)}, u32[]{:S(2)}, u32[]{:S(2)}) %collective-permute-start.10) | collective-permute-done | bytes 229408 | tf_op jit(solution)/shard_map/ppermute | solution.py:52
  100.3 3.5 %collective-permute-done.12 = bf16[32,3584]{1,0:T(8,128)(2,1)S(1)} collective-permute-done((bf16[32,3584]{1,0:T(8,128)(2,1)S(1)}, bf16[32,3584]{1,0:T(8,128)(2,1)S(1)}, u32[]{:S(2)}, u32[]{:S(2)}) %collective-permute-start.12) | collective-permute-done | bytes 229408 | tf_op jit(solution)/shard_map/ppermute | solution.py:52
  104.9 2.8 %collective-permute-start.13 = (bf16[8,7168]{1,0:T(8,128)(2,1)S(1)}, bf16[8,7168]{1,0:T(8,128)(2,1)S(1)}, u32[]{:S(2)}, u32[]{:S(2)}) collective-permute-start(bf16[8,7168]{1,0:T(8,128)(2,1)S(1)} %get-tuple-element.36), channel_id=1, source_target_pairs={{0,4},{1,5},{2,6},{3,7},{4,0},{5,1},{6,2},{7,3},{8,12},{9,13},{10,... | collective-permute-start | bytes 344072 | tf_op jit(solution)/shard_map/ppermute | solution.py:52
  110.1 2.1 gather_fusion.1
  112.2 6.0 %collective-permute-done.14 = bf16[8,7168]{1,0:T(8,128)(2,1)S(1)} collective-permute-done((bf16[8,7168]{1,0:T(8,128)(2,1)S(1)}, bf16[8,7168]{1,0:T(8,128)(2,1)S(1)}, u32[]{:S(2)}, u32[]{:S(2)}) %collective-permute-start.14) | collective-permute-done | bytes 114720 | tf_op jit(solution)/shard_map/ppermute | solution.py:52
  119.5 2.1 collective-permute-start.16
  122.1 1.9 collective-permute-start.18
  125.4 3.9 %all-to-all-start.1 = ((bf16[16,2,32,576]{3,2,1,0:T(8,128)(2,1)}), bf16[16,2,32,576]{3,2,1,0:T(8,128)(2,1)S(1)}, u32[]{:S(2)}, u32[]{:S(2)}) async-start(bf16[16,2,32,576]{3,2,1,0:T(8,128)(2,1)} %broadcast_select_fusion), calls=%async_computation.1 | async-start | bytes 2621440 | tf_op jit(solution)/shard_map/all_to_all | solution.py:151
  129.3 3.1 %collective-permute-done.17 = bf16[8,7296]{1,0:T(8,128)(2,1)S(1)} collective-permute-done((bf16[8,7296]{1,0:T(8,128)(2,1)S(1)}, bf16[8,7296]{1,0:T(8,128)(2,1)S(1)}, u32[]{:S(2)}, u32[]{:S(2)}) %collective-permute-start.17) | collective-permute-done | bytes 116768 | tf_op jit(solution)/shard_map/ppermute | solution.py:52
  136.1 30.0 %collective-permute-done.19 = bf16[32,7296]{1,0:T(8,128)(2,1)S(1)} collective-permute-done((bf16[32,7296]{1,0:T(8,128)(2,1)S(1)}, bf16[32,7296]{1,0:T(8,128)(2,1)S(1)}, u32[]{:S(2)}, u32[]{:S(2)}) %collective-permute-start.19) | collective-permute-done | bytes 466976 | tf_op jit(solution)/shard_map/ppermute | solution.py:52
  166.5 3.7 %collective-permute-done.22 = bf16[128,7296]{1,0:T(8,128)(2,1)S(1)} collective-permute-done((bf16[128,7296]{1,0:T(8,128)(2,1)S(1)}, bf16[128,7296]{1,0:T(8,128)(2,1)S(1)}, u32[]{:S(2)}, u32[]{:S(2)}) %collective-permute-start.22) | collective-permute-done | bytes 1867808 | tf_op jit(solution)/shard_map/ppermute | solution.py:52
  170.4 9.8 %fusion.2 = f32[256,1024]{1,0:T(8,128)} fusion(bf16[1,7168,1024]{2,1,0:T(8,128)(2,1)} %param.32, bf16[256,7296]{1,0:T(8,128)(2,1)S(1)} %constant_dynamic-update-slice_fusion.5), kind=kOutput, calls=%fused_computation.4 | convolution fusion | flops 3758096384 | bytes 19398656 | tf_op jit(solution)/shard_map/dot_general | solution.py:221
  180.3 20.4 %fusion.6 = bf16[256,7168]{1,0:T(8,128)(2,1)} fusion(bf16[1,1024,7168]{2,1,0:T(8,128)(2,1)} %param.33, f32[256,1024]{1,0:T(8,128)} %fusion.2, bf16[1,7168,1024]{2,1,0:T(8,128)(2,1)} %param.31, bf16[256,7296]{1,0:T(8,128)(2,1)} %copy-done.10, f32[256]{0:T(256)S(1)} %select_reduce_fusion), kind=kOutput, calls=%fused_computation.8 | convolution fusion | flops 7519862784 | bytes 37749760 | tf_op jit(solution)/shard_map/dot_general | solution.py:223
  200.7 3.0 %slice.185 = bf16[128,7168]{1,0:T(8,128)(2,1)} slice(bf16[256,7168]{1,0:T(8,128)(2,1)} %fusion.6), slice={[128:256], [0:7168]} | slice | bytes 3670016 | tf_op jit(solution)/shard_map/slice | solution.py:99
  211.4 2.5 convert_add_fusion
  218.3 8.8 %collective-permute-done.24 = bf16[32,7168]{1,0:T(8,128)(2,1)S(1)} collective-permute-done((bf16[32,7168]{1,0:T(8,128)(2,1)S(1)}, bf16[32,7168]{1,0:T(8,128)(2,1)S(1)}, u32[]{:S(2)}, u32[]{:S(2)}) %collective-permute-start.24) | collective-permute-done | bytes 458784 | tf_op jit(solution)/shard_map/ppermute | solution.py:52
  228.1 10.1 %collective-permute-done.26 = bf16[32,7168]{1,0:T(8,128)(2,1)S(1)} collective-permute-done((bf16[32,7168]{1,0:T(8,128)(2,1)S(1)}, bf16[32,7168]{1,0:T(8,128)(2,1)S(1)}, u32[]{:S(2)}, u32[]{:S(2)}) %collective-permute-start.26) | collective-permute-done | bytes 458784 | tf_op jit(solution)/shard_map/ppermute | solution.py:52
  239.9 2.4 collective-permute-start.28
  244.5 6.5 %collective-permute-done.28 = bf16[8,7168]{1,0:T(8,128)(2,1)S(1)} collective-permute-done((bf16[8,7168]{1,0:T(8,128)(2,1)S(1)}, bf16[8,7168]{1,0:T(8,128)(2,1)S(1)}, u32[]{:S(2)}, u32[]{:S(2)}) %collective-permute-start.28) | collective-permute-done | bytes 114720 | tf_op jit(solution)/shard_map/ppermute | solution.py:52
  (182 shorter events, 51.5 us)
Async XLA Ops:
  2.7 18.5 %collective-permute-start = (bf16[8,7168]{1,0:T(8,128)(2,1)S(1)}, bf16[8,7168]{1,0:T(8,128)(2,1)S(1)}, u32[]{:S(2)}, u32[]{:S(2)}) collective-permute-start(bf16[8,7168]{1,0:T(8,128)(2,1)S(1)} %fusion.48), channel_id=1, source_target_pairs={{0,4},{1,5},{2,6},{3,7},{4,0},{5,1},{6,2},{7,3},{8,12},{9,13},{10,... | collective-permute-start | bytes 344072 | tf_op jit(solution)/shard_map/ppermute | solution.py:52
  5.8 15.5 %collective-permute-start.1 = (bf16[8,7168]{1,0:T(8,128)(2,1)S(1)}, bf16[8,7168]{1,0:T(8,128)(2,1)S(1)}, u32[]{:S(2)}, u32[]{:S(2)}) collective-permute-start(bf16[8,7168]{1,0:T(8,128)(2,1)S(1)} %fusion.48), channel_id=1, source_target_pairs={{0,8},{1,9},{2,10},{3,11},{4,12},{5,13},{6,14},{7,15},{8,0},{9,1},... | collective-permute-start | bytes 344072 | tf_op jit(solution)/shard_map/ppermute | solution.py:52
  8.4 12.9 %collective-permute-start.2 = (bf16[8,7168]{1,0:T(8,128)(2,1)S(1)}, bf16[8,7168]{1,0:T(8,128)(2,1)S(1)}, u32[]{:S(2)}, u32[]{:S(2)}) collective-permute-start(bf16[8,7168]{1,0:T(8,128)(2,1)S(1)} %fusion.48), channel_id=1, source_target_pairs={{0,12},{1,13},{2,14},{3,15},{4,8},{5,9},{6,10},{7,11},{8,4},{9,5},... | collective-permute-start | bytes 344072 | tf_op jit(solution)/shard_map/ppermute | solution.py:52
  11.4 98.7 %all-to-all-start = ((bf16[16,2,32,576]{3,2,1,0:T(8,128)(2,1)}), bf16[16,2,32,576]{3,2,1,0:T(8,128)(2,1)}, u32[]{:S(2)}, u32[]{:S(2)}) async-start(bf16[16,2,32,576]{3,2,1,0:T(8,128)(2,1)} %copy.52), calls=%async_computation | async-start | bytes 2621440 | tf_op jit(solution)/shard_map/all_to_all | solution.py:138
  22.1 20.4 %collective-permute-start.4 = (bf16[32,3584]{1,0:T(8,128)(2,1)S(1)}, bf16[32,3584]{1,0:T(8,128)(2,1)S(1)}, u32[]{:S(2)}, u32[]{:S(2)}) collective-permute-start(bf16[32,3584]{1,0:T(8,128)(2,1)S(1)} %get-tuple-element.39), channel_id=1, source_target_pairs={{0,16},{1,17},{2,18},{3,19},{4,20},{5,21},{6,22},{7,23},{8,24},{9,... | collective-permute-start | bytes 688136 | tf_op jit(solution)/shard_map/ppermute | solution.py:52
  23.6 18.9 %collective-permute-start.5 = (bf16[32,3584]{1,0:T(8,128)(2,1)S(1)}, bf16[32,3584]{1,0:T(8,128)(2,1)S(1)}, u32[]{:S(2)}, u32[]{:S(2)}) collective-permute-start(bf16[32,3584]{1,0:T(8,128)(2,1)S(1)} %get-tuple-element.39), channel_id=1, source_target_pairs={{0,18},{1,19},{2,16},{3,17},{4,22},{5,23},{6,20},{7,21},{8,26},{9,... | collective-permute-start | bytes 688136 | tf_op jit(solution)/shard_map/ppermute | solution.py:52
  25.4 17.1 %collective-permute-start.3 = (bf16[32,3584]{1,0:T(8,128)(2,1)S(1)}, bf16[32,3584]{1,0:T(8,128)(2,1)S(1)}, u32[]{:S(2)}, u32[]{:S(2)}) collective-permute-start(bf16[32,3584]{1,0:T(8,128)(2,1)S(1)} %get-tuple-element.22), channel_id=1, source_target_pairs={{0,2},{1,3},{2,0},{3,1},{4,6},{5,7},{6,4},{7,5},{8,10},{9,11},{10,... | collective-permute-start | bytes 688136 | tf_op jit(solution)/shard_map/ppermute | solution.py:52
  42.6 2.5 %collective-permute-start.6 = (bf16[128,3584]{1,0:T(8,128)(2,1)S(1)}, bf16[128,3584]{1,0:T(8,128)(2,1)S(1)}, u32[]{:S(2)}, u32[]{:S(2)}) collective-permute-start(bf16[128,3584]{1,0:T(8,128)(2,1)S(1)} %pad_maximum_fusion.2), channel_id=1, source_target_pairs={{0,1},{1,0},{2,3},{3,2},{4,5},{5,4},{6,7},{7,6},{8,9},{9,8},{10,11... | collective-permute-start | bytes 2752520 | tf_op jit(solution)/shard_map/ppermute | solution.py:52
  51.3 16.2 %collective-permute-start.7 = (bf16[256,1152]{1,0:T(8,128)(2,1)S(1)}, bf16[256,1152]{1,0:T(8,128)(2,1)S(1)}, u32[]{:S(2)}, u32[]{:S(2)}) collective-permute-start(bf16[256,1152]{1,0:T(8,128)(2,1)S(1)} %get-tuple-element.52), channel_id=1, source_target_pairs={{0,16},{1,17},{2,18},{3,19},{4,20},{5,21},{6,22},{7,23},{8,24},{9,... | collective-permute-start | bytes 1769480 | tf_op jit(solution)/shard_map/ppermute | solution.py:52
  55.4 24.0 %collective-permute-start.8 = (bf16[256,1152]{1,0:T(8,128)(2,1)S(1)}, bf16[256,1152]{1,0:T(8,128)(2,1)S(1)}, u32[]{:S(2)}, u32[]{:S(2)}) collective-permute-start(bf16[256,1152]{1,0:T(8,128)(2,1)S(1)} %get-tuple-element.50), channel_id=1, source_target_pairs={{0,16},{1,17},{2,18},{3,19},{4,20},{5,21},{6,22},{7,23},{8,24},{9,... | collective-permute-start | bytes 1769480 | tf_op jit(solution)/shard_map/ppermute | solution.py:52
  83.7 2.7 %collective-permute-start.9 = (bf16[128,3584]{1,0:T(8,128)(2,1)S(1)}, bf16[128,3584]{1,0:T(8,128)(2,1)}, u32[]{:S(2)}, u32[]{:S(2)}) collective-permute-start(bf16[128,3584]{1,0:T(8,128)(2,1)S(1)} %slice.173), channel_id=1, source_target_pairs={{0,1},{1,0},{2,3},{3,2},{4,5},{5,4},{6,7},{7,6},{8,9},{9,8},{10,11... | collective-permute-start | bytes 2752520 | tf_op jit(solution)/shard_map/ppermute | solution.py:52
  89.0 8.7 %collective-permute-start.10 = (bf16[32,3584]{1,0:T(8,128)(2,1)}, bf16[32,3584]{1,0:T(8,128)(2,1)}, u32[]{:S(2)}, u32[]{:S(2)}) collective-permute-start(bf16[32,3584]{1,0:T(8,128)(2,1)} %get-tuple-element.28), channel_id=1, source_target_pairs={{0,2},{1,3},{2,0},{3,1},{4,6},{5,7},{6,4},{7,5},{8,10},{9,11},{10,... | collective-permute-start | bytes 688136 | tf_op jit(solution)/shard_map/ppermute | solution.py:52
  91.5 8.8 %collective-permute-start.11 = (bf16[32,3584]{1,0:T(8,128)(2,1)}, bf16[32,3584]{1,0:T(8,128)(2,1)S(1)}, u32[]{:S(2)}, u32[]{:S(2)}) collective-permute-start(bf16[32,3584]{1,0:T(8,128)(2,1)} %get-tuple-element.26), channel_id=1, source_target_pairs={{0,16},{1,17},{2,18},{3,19},{4,20},{5,21},{6,22},{7,23},{8,24},{9,... | collective-permute-start | bytes 688136 | tf_op jit(solution)/shard_map/ppermute | solution.py:52
  93.1 10.7 %collective-permute-start.12 = (bf16[32,3584]{1,0:T(8,128)(2,1)S(1)}, bf16[32,3584]{1,0:T(8,128)(2,1)S(1)}, u32[]{:S(2)}, u32[]{:S(2)}) collective-permute-start(bf16[32,3584]{1,0:T(8,128)(2,1)S(1)} %get-tuple-element.27), channel_id=1, source_target_pairs={{0,18},{1,19},{2,16},{3,17},{4,22},{5,23},{6,20},{7,21},{8,26},{9,... | collective-permute-start | bytes 688136 | tf_op jit(solution)/shard_map/ppermute | solution.py:52
  104.9 7.3 %collective-permute-start.13 = (bf16[8,7168]{1,0:T(8,128)(2,1)S(1)}, bf16[8,7168]{1,0:T(8,128)(2,1)S(1)}, u32[]{:S(2)}, u32[]{:S(2)}) collective-permute-start(bf16[8,7168]{1,0:T(8,128)(2,1)S(1)} %get-tuple-element.36), channel_id=1, source_target_pairs={{0,4},{1,5},{2,6},{3,7},{4,0},{5,1},{6,2},{7,3},{8,12},{9,13},{10,... | collective-permute-start | bytes 344072 | tf_op jit(solution)/shard_map/ppermute | solution.py:52
  107.6 10.6 %collective-permute-start.14 = (bf16[8,7168]{1,0:T(8,128)(2,1)S(1)}, bf16[8,7168]{1,0:T(8,128)(2,1)S(1)}, u32[]{:S(2)}, u32[]{:S(2)}) collective-permute-start(bf16[8,7168]{1,0:T(8,128)(2,1)S(1)} %get-tuple-element.38), channel_id=1, source_target_pairs={{0,8},{1,9},{2,10},{3,11},{4,12},{5,13},{6,14},{7,15},{8,0},{9,1},... | collective-permute-start | bytes 344072 | tf_op jit(solution)/shard_map/ppermute | solution.py:52
  108.5 9.7 %collective-permute-start.15 = (bf16[8,7168]{1,0:T(8,128)(2,1)S(1)}, bf16[8,7168]{1,0:T(8,128)(2,1)S(1)}, u32[]{:S(2)}, u32[]{:S(2)}) collective-permute-start(bf16[8,7168]{1,0:T(8,128)(2,1)S(1)} %get-tuple-element.37), channel_id=1, source_target_pairs={{0,12},{1,13},{2,14},{3,15},{4,8},{5,9},{6,10},{7,11},{8,4},{9,5},... | collective-permute-start | bytes 344072 | tf_op jit(solution)/shard_map/ppermute | solution.py:52
  119.5 9.7 %collective-permute-start.16 = (bf16[8,7296]{1,0:T(8,128)(2,1)S(1)}, bf16[8,7296]{1,0:T(8,128)(2,1)S(1)}, u32[]{:S(2)}, u32[]{:S(2)}) collective-permute-start(bf16[8,7296]{1,0:T(8,128)(2,1)S(1)} %get-tuple-element.41), channel_id=1, source_target_pairs={{0,4},{1,5},{2,6},{3,7},{4,0},{5,1},{6,2},{7,3},{8,12},{9,13},{10,... | collective-permute-start | bytes 350216 | tf_op jit(solution)/shard_map/ppermute | solution.py:52
  121.6 10.8 %collective-permute-start.17 = (bf16[8,7296]{1,0:T(8,128)(2,1)S(1)}, bf16[8,7296]{1,0:T(8,128)(2,1)S(1)}, u32[]{:S(2)}, u32[]{:S(2)}) collective-permute-start(bf16[8,7296]{1,0:T(8,128)(2,1)S(1)} %get-tuple-element.41), channel_id=1, source_target_pairs={{0,8},{1,9},{2,10},{3,11},{4,12},{5,13},{6,14},{7,15},{8,0},{9,1},... | collective-permute-start | bytes 350216 | tf_op jit(solution)/shard_map/ppermute | solution.py:52
  122.1 10.3 %collective-permute-start.18 = (bf16[8,7296]{1,0:T(8,128)(2,1)S(1)}, bf16[8,7296]{1,0:T(8,128)(2,1)S(1)}, u32[]{:S(2)}, u32[]{:S(2)}) collective-permute-start(bf16[8,7296]{1,0:T(8,128)(2,1)S(1)} %get-tuple-element.41), channel_id=1, source_target_pairs={{0,12},{1,13},{2,14},{3,15},{4,8},{5,9},{6,10},{7,11},{8,4},{9,5},... | collective-permute-start | bytes 350216 | tf_op jit(solution)/shard_map/ppermute | solution.py:52
  125.4 80.3 %all-to-all-start.1 = ((bf16[16,2,32,576]{3,2,1,0:T(8,128)(2,1)}), bf16[16,2,32,576]{3,2,1,0:T(8,128)(2,1)S(1)}, u32[]{:S(2)}, u32[]{:S(2)}) async-start(bf16[16,2,32,576]{3,2,1,0:T(8,128)(2,1)} %broadcast_select_fusion), calls=%async_computation.1 | async-start | bytes 2621440 | tf_op jit(solution)/shard_map/all_to_all | solution.py:151
  132.5 33.7 %collective-permute-start.19 = (bf16[32,7296]{1,0:T(8,128)(2,1)S(1)}, bf16[32,7296]{1,0:T(8,128)(2,1)S(1)}, u32[]{:S(2)}, u32[]{:S(2)}) collective-permute-start(bf16[32,7296]{1,0:T(8,128)(2,1)S(1)} %maximum_bitcast_fusion), channel_id=1, source_target_pairs={{0,2},{1,3},{2,0},{3,1},{4,6},{5,7},{6,4},{7,5},{8,10},{9,11},{10,... | collective-permute-start | bytes 1400840 | tf_op jit(solution)/shard_map/ppermute | solution.py:52
  133.1 33.0 %collective-permute-start.20 = (bf16[32,7296]{1,0:T(8,128)(2,1)S(1)}, bf16[32,7296]{1,0:T(8,128)(2,1)S(1)}, u32[]{:S(2)}, u32[]{:S(2)}) collective-permute-start(bf16[32,7296]{1,0:T(8,128)(2,1)S(1)} %maximum_bitcast_fusion), channel_id=1, source_target_pairs={{0,16},{1,17},{2,18},{3,19},{4,20},{5,21},{6,22},{7,23},{8,24},{9,... | collective-permute-start | bytes 1400840 | tf_op jit(solution)/shard_map/ppermute | solution.py:52
  134.6 31.5 %collective-permute-start.21 = (bf16[32,7296]{1,0:T(8,128)(2,1)S(1)}, bf16[32,7296]{1,0:T(8,128)(2,1)S(1)}, u32[]{:S(2)}, u32[]{:S(2)}) collective-permute-start(bf16[32,7296]{1,0:T(8,128)(2,1)S(1)} %maximum_bitcast_fusion), channel_id=1, source_target_pairs={{0,18},{1,19},{2,16},{3,17},{4,22},{5,23},{6,20},{7,21},{8,26},{9,... | collective-permute-start | bytes 1400840 | tf_op jit(solution)/shard_map/ppermute | solution.py:52
  166.3 3.9 %collective-permute-start.22 = (bf16[128,7296]{1,0:T(8,128)(2,1)S(1)}, bf16[128,7296]{1,0:T(8,128)(2,1)S(1)}, u32[]{:S(2)}, u32[]{:S(2)}) collective-permute-start(bf16[128,7296]{1,0:T(8,128)(2,1)S(1)} %pad_maximum_fusion), channel_id=1, source_target_pairs={{0,1},{1,0},{2,3},{3,2},{4,5},{5,4},{6,7},{7,6},{8,9},{9,8},{10,11... | collective-permute-start | bytes 5603336 | tf_op jit(solution)/shard_map/ppermute | solution.py:52
  203.7 7.7 %collective-permute-start.23 = (bf16[128,7168]{1,0:T(8,128)(2,1)}, bf16[128,7168]{1,0:T(8,128)(2,1)}, u32[]{:S(2)}, u32[]{:S(2)}) collective-permute-start(bf16[128,7168]{1,0:T(8,128)(2,1)} %slice.185), channel_id=1, source_target_pairs={{0,1},{1,0},{2,3},{3,2},{4,5},{5,4},{6,7},{7,6},{8,9},{9,8},{10,11... | collective-permute-start | bytes 5505032 | tf_op jit(solution)/shard_map/ppermute | solution.py:52
  214.2 12.9 %collective-permute-start.24 = (bf16[32,7168]{1,0:T(8,128)(2,1)S(1)}, bf16[32,7168]{1,0:T(8,128)(2,1)S(1)}, u32[]{:S(2)}, u32[]{:S(2)}) collective-permute-start(bf16[32,7168]{1,0:T(8,128)(2,1)S(1)} %get-tuple-element.23), channel_id=1, source_target_pairs={{0,2},{1,3},{2,0},{3,1},{4,6},{5,7},{6,4},{7,5},{8,10},{9,11},{10,... | collective-permute-start | bytes 1376264 | tf_op jit(solution)/shard_map/ppermute | solution.py:52
  214.7 13.4 %collective-permute-start.25 = (bf16[32,7168]{1,0:T(8,128)(2,1)S(1)}, bf16[32,7168]{1,0:T(8,128)(2,1)S(1)}, u32[]{:S(2)}, u32[]{:S(2)}) collective-permute-start(bf16[32,7168]{1,0:T(8,128)(2,1)S(1)} %get-tuple-element.25), channel_id=1, source_target_pairs={{0,16},{1,17},{2,18},{3,19},{4,20},{5,21},{6,22},{7,23},{8,24},{9,... | collective-permute-start | bytes 1376264 | tf_op jit(solution)/shard_map/ppermute | solution.py:52
  216.2 22.0 %collective-permute-start.26 = (bf16[32,7168]{1,0:T(8,128)(2,1)S(1)}, bf16[32,7168]{1,0:T(8,128)(2,1)S(1)}, u32[]{:S(2)}, u32[]{:S(2)}) collective-permute-start(bf16[32,7168]{1,0:T(8,128)(2,1)S(1)} %get-tuple-element.24), channel_id=1, source_target_pairs={{0,18},{1,19},{2,16},{3,17},{4,22},{5,23},{6,20},{7,21},{8,26},{9,... | collective-permute-start | bytes 1376264 | tf_op jit(solution)/shard_map/ppermute | solution.py:52
  238.4 6.1 %collective-permute-start.27 = (bf16[8,7168]{1,0:T(8,128)(2,1)S(1)}, bf16[8,7168]{1,0:T(8,128)(2,1)S(1)}, u32[]{:S(2)}, u32[]{:S(2)}) collective-permute-start(bf16[8,7168]{1,0:T(8,128)(2,1)S(1)} %get-tuple-element.33), channel_id=1, source_target_pairs={{0,4},{1,5},{2,6},{3,7},{4,0},{5,1},{6,2},{7,3},{8,12},{9,13},{10,... | collective-permute-start | bytes 344072 | tf_op jit(solution)/shard_map/ppermute | solution.py:52
  239.9 11.1 %collective-permute-start.28 = (bf16[8,7168]{1,0:T(8,128)(2,1)S(1)}, bf16[8,7168]{1,0:T(8,128)(2,1)S(1)}, u32[]{:S(2)}, u32[]{:S(2)}) collective-permute-start(bf16[8,7168]{1,0:T(8,128)(2,1)S(1)} %get-tuple-element.35), channel_id=1, source_target_pairs={{0,8},{1,9},{2,10},{3,11},{4,12},{5,13},{6,14},{7,15},{8,0},{9,1},... | collective-permute-start | bytes 344072 | tf_op jit(solution)/shard_map/ppermute | solution.py:52
  242.4 8.7 %collective-permute-start.29 = (bf16[8,7168]{1,0:T(8,128)(2,1)S(1)}, bf16[8,7168]{1,0:T(8,128)(2,1)S(1)}, u32[]{:S(2)}, u32[]{:S(2)}) collective-permute-start(bf16[8,7168]{1,0:T(8,128)(2,1)S(1)} %get-tuple-element.34), channel_id=1, source_target_pairs={{0,12},{1,13},{2,14},{3,15},{4,8},{5,9},{6,10},{7,11},{8,4},{9,5},... | collective-permute-start | bytes 344072 | tf_op jit(solution)/shard_map/ppermute | solution.py:52
  (25 other events, 219.5 us)

commit v2 on v1

v2 whole, which is shorter than its diff:
```python
import functools

import jax
import jax.numpy as jnp
from jax import lax
from jax.experimental import pallas as pl
from jax.experimental.pallas import tpu as pltpu
from jax.sharding import PartitionSpec as P

VDIM = 512
QKD = 192


EPS = 1e-06
ROUTE_SCALE = 2.5
AXES = ("dp", "tp")
CUTS = 1
DOWN_CUTS = 2
DOWN_STEP = 896
STEP = 1024
SLOTS = 3
DENSE_STEP = 896
DENSE_VMEM = 14
HBM = pltpu.MemorySpace.HBM


def rms_scale(rows, gain):
    values = rows.astype(jnp.float32)
    mean_square = jnp.mean(values * values, axis=-1, keepdims=True)
    return (values * lax.rsqrt(mean_square + EPS) * gain).astype(jnp.bfloat16)


def attend(queries, keys, lengths, newest):
    scale = QKD ** (-0.5)
    scores = jnp.einsum("rhl,rcl->rhc", queries, keys, preferred_element_type=jnp.float32) * scale
    positions = jnp.arange(keys.shape[1])
    valid = positions[None, None, :] < lengths[:, None, None]
    masked = jnp.where(valid, scores, -1e30)
    own_score = (
        jnp.einsum("rhl,rl->rh", queries, newest, preferred_element_type=jnp.float32) * scale
    )
    top = jnp.maximum(jnp.max(masked, axis=-1), own_score)
    expo = jnp.where(valid, jnp.exp(masked - top[..., None]), 0.0)
    own_expo = jnp.exp(own_score - top)
    total = jnp.sum(expo, axis=-1) + own_expo
    weights = (expo / total[..., None]).astype(jnp.bfloat16)
    own_weight = (own_expo / total).astype(jnp.bfloat16)
    context = jnp.einsum(
        "rhc,rcv->rhv", weights, keys[:, :, :VDIM], preferred_element_type=jnp.float32
    )
    context = context + own_weight.astype(jnp.float32)[..., None] * newest[:, None, :VDIM].astype(
        jnp.float32
    )
    return context.astype(jnp.bfloat16)


def swap(block, q, j):
    dp_count, tp_count = lax.axis_size("dp"), lax.axis_size("tp")
    pairs = [
        (p * tp_count + t, (p ^ q) * tp_count + (t ^ j))
        for p in range(dp_count)
        for t in range(tp_count)
    ]
    return lax.ppermute(block, AXES, pairs)


def far_masks():
    return range(4, lax.axis_size("tp"), 4)


def quad():
    return [(q, y) for q in range(lax.axis_size("dp")) for y in (0, 2) if (q, y) != (0, 0)]


def gather_far(rows):
    return jnp.stack([rows] + [swap(rows, 0, j) for j in far_masks()], axis=0)


def feature_part(rows, part, count):
    size = rows.shape[-1] // count
    return lax.dynamic_slice_in_dim(rows, part * size, size, axis=rows.ndim - 1)


def near_parts(far, dp_rank, dp_count):
    far = far.reshape(-1, far.shape[-1])
    parts = [feature_part(far, dp_rank, dp_count)]
    for q, y in quad():
        parts.append(swap(feature_part(far, dp_rank ^ q, dp_count), q, y))
    return jnp.concatenate(parts, axis=0)


def gather_quad(far):
    far = far.reshape(-1, far.shape[-1])
    return [far] + [swap(far, q, y) for q, y in quad()]


def wide(block):
    return block.astype(jnp.float32)


def sum_dp(parts, dp_count):
    total, away = parts
    size = total.shape[0]
    for q in range(1, dp_count):
        total = total + wide(swap(away[(q - 1) * size : q * size], q, 0))
    return total


def reduce_core(mine, away, blocks):
    got = swap(away, 0, 1)
    size = mine.shape[0] // blocks
    return [wide(mine[at : at + size]) + wide(got[at : at + size]) for at in range(0, mine.shape[0], size)]


def reduce_far(blocks):
    out = blocks[0]
    for block, j in zip(blocks[1:], far_masks()):
        out = out + wide(swap(block.astype(jnp.bfloat16), 0, j))
    return out


def reduce_parts(near, dp_rank, dp_count, rows_dev):
    size = near[0].shape[1]
    parts = []
    for q in range(dp_count):
        part = near[2 * q] if q == 0 else wide(swap(near[2 * q].astype(jnp.bfloat16), q, 0))
        parts.append(part + wide(swap(near[2 * q + 1].astype(jnp.bfloat16), q, 2)))
    if dp_count == 2:
        first = dp_rank == 0
        full = jnp.concatenate([jnp.where(first, parts[0], parts[1]), jnp.where(first, parts[1], parts[0])], axis=1)
    else:
        full = jnp.zeros((parts[0].shape[0], size * dp_count), jnp.float32)
        for q in range(dp_count):
            full = lax.dynamic_update_slice_in_dim(full, parts[q], (dp_rank ^ q) * size, axis=1)
    return reduce_far([full[at : at + rows_dev] for at in range(0, full.shape[0], rows_dev)])


def reduce_rows(near, rows_dev):
    out = near[0]
    for q, y in quad():
        out = out + wide(swap(near[2 * q + y // 2].astype(jnp.bfloat16), q, y))
    return reduce_far([out[at : at + rows_dev] for at in range(0, out.shape[0], rows_dev)])


def cut_pieces(leaving):
    tp_count = lax.axis_size("tp")
    moving, layers, cache, lat = leaving.shape
    piece = layers * lat // tp_count
    turned = leaving.transpose(0, 1, 3, 2).reshape(moving, tp_count, piece, cache)
    return turned.transpose(1, 0, 2, 3)


def arrival_sources(group_dest):
    packets = group_dest.size
    moving = group_dest.shape[1]
    dest = group_dest.reshape(-1)
    at = jnp.arange(packets)
    earlier = (dest[:, None] == dest[None, :]) & (at[None, :] // moving < at[:, None] // moving)
    place = dest * moving + jnp.sum(earlier.astype(jnp.int32), axis=1)
    return jnp.sum(jnp.where(place[None, :] == at[:, None], at[None, :], 0), axis=1)


def sort_pieces(spread, source):
    packets = jnp.take(spread.reshape((-1,) + spread.shape[2:]), source, axis=0, mode="clip")
    return packets.reshape(spread.shape)


def join_pieces(home, shape):
    moving, layers, cache, lat = shape
    turned = home.transpose(1, 0, 2, 3).reshape(moving, layers, lat, cache)
    return turned.transpose(0, 1, 3, 2)


def in_hbm(weights):
    return pltpu.with_memory_space_constraint(weights, HBM)


def ring(copies, slots):
    count, make = copies
    for at in range(min(slots, count)):
        make(at).start()

    def free(at):
        @pl.when(at + slots < count)
        def _():
            make(at + slots).start()

    return (lambda at: make(at).wait()), free


def dense_kernel(groups, near_ref, other_ref, hbm, own_ref, away_ref, rows_ref, buf, sem):
    size = near_ref.shape[0] // groups
    steps = near_ref.shape[1] // DENSE_STEP

    def make(at):
        slot = lax.rem(at, SLOTS)
        return pltpu.make_async_copy(
            hbm.at[pl.ds(at * DENSE_STEP, DENSE_STEP)], buf.at[slot], sem.at[slot]
        )

    wait, free = ring((steps, make), SLOTS)
    for at in range(groups):
        part = slice(at * size, (at + 1) * size)
        rows_ref[2 * at * size : (2 * at + 1) * size] = near_ref[part]
        rows_ref[(2 * at + 1) * size : (2 * at + 2) * size] = other_ref[part]
    acc = jnp.zeros((rows_ref.shape[0], own_ref.shape[1]), jnp.float32)
    for at in range(steps):
        wait(at)
        rows = rows_ref[:, at * DENSE_STEP : (at + 1) * DENSE_STEP]
        acc = acc + jnp.dot(rows, buf[at % SLOTS], preferred_element_type=jnp.float32)
        free(at)
    own = own_ref.shape[0]
    own_ref[...] = acc[:own]
    away_ref[...] = acc[own:].astype(jnp.bfloat16)


def run_dense(near, other, weights, groups):
    count, width = 2 * near.shape[0], weights.shape[1]
    vmem, far = pl.BlockSpec(memory_space=pltpu.VMEM), pl.BlockSpec(memory_space=HBM)
    own = count // groups
    return pl.pallas_call(
        functools.partial(dense_kernel, groups),
        out_shape=(
            jax.ShapeDtypeStruct((own, width), jnp.float32),
            jax.ShapeDtypeStruct((count - own, width), jnp.bfloat16),
        ),
        in_specs=[vmem, vmem, far],
        out_specs=(vmem, vmem),
        scratch_shapes=[
            pltpu.VMEM((count, near.shape[1]), jnp.bfloat16),
            pltpu.VMEM((SLOTS, DENSE_STEP, width), jnp.bfloat16),
            pltpu.SemaphoreType.DMA((SLOTS,)),
        ],
        compiler_params=pltpu.CompilerParams(vmem_limit_bytes=DENSE_VMEM * 1024 * 1024),
    )(near, other, in_hbm(weights))


def up_kernel(first, last, base, width, experts, *refs):
    refs = list(refs)
    near_ref, other_ref, gate_hbm, up_hbm = refs[:4]
    del refs[:4]
    if not first:
        gate_in, up_in, share_in = refs[:3]
        del refs[:3]
    if last:
        inner_ref = refs.pop(0)
        gate_acc, up_acc = refs.pop(0), refs.pop(0)
    else:
        gate_acc, up_acc, share_out = refs[:3]
        del refs[:3]
    gate_buf, up_buf, gate_sem, up_sem = refs
    count = width // STEP

    def copies(hbm, buf, sem):
        def make(at):
            slot = lax.rem(at, SLOTS)
            return pltpu.make_async_copy(
                hbm.at[0, pl.ds(base + at * STEP, STEP)], buf.at[slot], sem.at[slot]
            )

        return count, make

    gate_wait, gate_free = ring(copies(gate_hbm, gate_buf, gate_sem), SLOTS)
    up_wait, up_free = ring(copies(up_hbm, up_buf, up_sem), SLOTS)
    if first:
        gate_acc[...] = jnp.zeros_like(gate_acc)
        up_acc[...] = jnp.zeros_like(up_acc)
        lane = lax.broadcasted_iota(jnp.int32, (1, 128), 1)
        rank = lax.axis_index("tp")
        mine = (lane == rank) | (lane == rank + experts)
        tail = jnp.concatenate([near_ref[:, width:], other_ref[:, width:]], axis=0)
        tail = jnp.where(mine, tail.astype(jnp.float32), 0.0)
        share = jnp.sum(tail, axis=1, keepdims=True)
    else:
        gate_acc[...] = gate_in[...]
        up_acc[...] = up_in[...]
        share = share_in[:, :1]
    if not last:
        share_out[...] = jnp.broadcast_to(share, share_out.shape)

    @pl.loop(0, count)
    def _(at):
        where = pl.ds(pl.multiple_of(at * STEP, 128), STEP)
        rows = jnp.concatenate([near_ref[:, where], other_ref[:, where]], axis=0)
        slot = lax.rem(at, SLOTS)
        gate_wait(at)
        gate_acc[...] += jnp.dot(rows, gate_buf[slot], preferred_element_type=jnp.float32)
        gate_free(at)
        up_wait(at)
        up_acc[...] += jnp.dot(rows, up_buf[slot], preferred_element_type=jnp.float32)
        up_free(at)

    if last:
        gate = gate_acc[...]
        inner_ref[...] = (gate / (1.0 + jnp.exp(-gate)) * up_acc[...] * share).astype(jnp.bfloat16)


def run_up(cut, near, other, gate_w, up_w, state, width, experts):
    first, last = cut == 0, cut == CUTS - 1
    count, hidden = 2 * near.shape[0], gate_w.shape[2]
    vmem, far = pl.BlockSpec(memory_space=pltpu.VMEM), pl.BlockSpec(memory_space=HBM)
    total = jax.ShapeDtypeStruct((count, hidden), jnp.float32)
    inner = jax.ShapeDtypeStruct((count, hidden), jnp.bfloat16)
    share = jax.ShapeDtypeStruct((count, 128), jnp.float32)
    scratch = [pltpu.VMEM((count, hidden), jnp.float32)] * 2 if last else []
    return pl.pallas_call(
        functools.partial(up_kernel, first, last, cut * width, width, experts),
        out_shape=inner if last else (total, total, share),
        in_specs=[vmem, vmem, far, far] + [vmem] * len(state),
        out_specs=vmem if last else (vmem, vmem, vmem),
        scratch_shapes=scratch
        + [pltpu.VMEM((SLOTS, STEP, hidden), jnp.bfloat16)] * 2
        + [pltpu.SemaphoreType.DMA((SLOTS,))] * 2,
        compiler_params=pltpu.CompilerParams(vmem_limit_bytes=18 * 1024 * 1024),
    )(near, other, in_hbm(gate_w), in_hbm(up_w), *state)


def down_kernel(base, inner_ref, down_hbm, near_ref, away_ref, buf, sem):
    half, width = near_ref.shape

    def make(at):
        slot = lax.rem(at, SLOTS)
        where = pl.ds(base + at * DOWN_STEP, DOWN_STEP)
        return pltpu.make_async_copy(down_hbm.at[0, :, where], buf.at[slot], sem.at[slot])

    wait, free = ring((width // DOWN_STEP, make), SLOTS)

    @pl.loop(0, width // DOWN_STEP)
    def _(at):
        wait(at)
        where = pl.ds(pl.multiple_of(at * DOWN_STEP, 128), DOWN_STEP)
        out = jnp.dot(inner_ref[...], buf[lax.rem(at, SLOTS)], preferred_element_type=jnp.float32)
        near_ref[:, where] = out[:half].astype(jnp.bfloat16)
        away_ref[:, where] = out[half:].astype(jnp.bfloat16)
        free(at)


def run_down(cut, inner, down_w, width):
    count, hidden = inner.shape
    vmem, far = pl.BlockSpec(memory_space=pltpu.VMEM), pl.BlockSpec(memory_space=HBM)
    half = jax.ShapeDtypeStruct((count // 2, width), jnp.bfloat16)
    return pl.pallas_call(
        functools.partial(down_kernel, cut * width),
        out_shape=(half, half),
        in_specs=[vmem, far],
        out_specs=(vmem, vmem),
        scratch_shapes=[
            pltpu.VMEM((SLOTS, hidden, DOWN_STEP), jnp.bfloat16),
            pltpu.SemaphoreType.DMA((SLOTS,)),
        ],
        compiler_params=pltpu.CompilerParams(vmem_limit_bytes=12 * 1024 * 1024),
    )(inner, in_hbm(down_w))


def on_device(
    queries,
    new_latent,
    resident,
    leaving,
    res_len,
    leave_len,
    mig_dest,
    stream,
    dense_gain,
    w_gate,
    w_up,
    w_down,
    moe_gain,
    expert_gate,
    expert_up,
    expert_down,
    expert_ids,
    gate_scores,
):
    tp_count = lax.axis_size("tp")
    dp_count = lax.axis_size("dp")
    tp_rank = lax.axis_index("tp")
    dp_rank = lax.axis_index("dp")
    group_dest = lax.dynamic_slice_in_dim(mig_dest, dp_rank * tp_count, tp_count, 0)
    group_len = lax.dynamic_slice_in_dim(leave_len, dp_rank * tp_count, tp_count, 0)
    rows_dev = stream.shape[0]
    normed = rms_scale(stream, dense_gain)
    near = near_parts(gather_far(normed), dp_rank, dp_count)
    other = swap(near, 0, 1)
    near, outgoing = lax.optimization_barrier((near, cut_pieces(leaving)))
    spread = lax.all_to_all(outgoing, "tp", split_axis=0, concat_axis=0, tiled=True)
    gate = sum_dp(run_dense(near, other, w_gate, dp_count), dp_count)
    up = sum_dp(run_dense(near, other, w_up, dp_count), dp_count)
    hidden = (jax.nn.silu(gate) * up).astype(jnp.bfloat16)
    near = []
    for q in range(dp_count):
        block = swap(hidden, q, 0) if q else hidden
        down = jnp.dot(block, w_down, preferred_element_type=jnp.float32).astype(jnp.bfloat16)
        half = down.shape[0] // 2
        near += reduce_core(down[:half], down[half:], 2)
    near[-1], spread = lax.optimization_barrier((near[-1], spread))
    ffn = reduce_parts(near, dp_rank, dp_count, rows_dev)
    middle = (stream.astype(jnp.float32) + ffn).astype(jnp.bfloat16)
    mixed = rms_scale(middle, moe_gain)

    shares = gate_scores / jnp.sum(gate_scores, axis=1, keepdims=True) * ROUTE_SCALE
    experts = tp_count * expert_gate.shape[0]
    chosen = expert_ids[:, :, None] == jnp.arange(experts)[None, None, :]
    table = jnp.sum(jnp.where(chosen, shares[:, :, None], 0.0), axis=1)
    high = table.astype(jnp.bfloat16)
    low = (table - wide(high)).astype(jnp.bfloat16)
    tail = jnp.pad(jnp.concatenate([high, low], axis=1), ((0, 0), (0, 128 - 2 * experts)))
    width = mixed.shape[1] // CUTS
    pieces = [mixed[:, at * width : (at + 1) * width] for at in range(CUTS)]
    pieces[0] = jnp.concatenate([pieces[0], tail], axis=1)
    homing = sort_pieces(spread, arrival_sources(group_dest))
    near = []
    for piece in pieces:
        blocks = gather_quad(gather_far(piece))
        blocks[1], homing = lax.optimization_barrier((blocks[1], homing))
        near.append(jnp.concatenate(blocks, axis=0))
    state = ()
    for at in range(CUTS):
        state = run_up(at, near[at], swap(near[at], 0, 1), expert_gate, expert_up, state, width, experts)
    out = []
    width = mixed.shape[1] // DOWN_CUTS
    sums = [reduce_core(*run_down(at, state, expert_down, width), 2 * dp_count) for at in range(DOWN_CUTS)]
    home = lax.all_to_all(homing, "tp", split_axis=0, concat_axis=0, tiled=True)
    sums[-1][0], home = lax.optimization_barrier((sums[-1][0], home))
    arrived = join_pieces(home, leaving.shape)
    for at in range(DOWN_CUTS):
        routed = reduce_rows(sums[at], rows_dev)
        out.append(wide(middle[:, at * width : (at + 1) * width]) + routed)
    moving = leaving.shape[0]
    source = arrival_sources(group_dest)
    mine = lax.dynamic_slice_in_dim(source, tp_rank * moving, moving, 0)
    arrived_len = jnp.take(group_len.reshape(-1), mine, axis=0, mode="clip")
    stay = resident.shape[0]
    context_stay = attend(queries[:stay], resident, res_len, new_latent[:stay])
    context_moved = attend(queries[stay:], arrived[:, 0], arrived_len, new_latent[stay:])
    context = jnp.concatenate([context_stay, context_moved], axis=0)

    stream_out = jnp.concatenate(out, axis=1).astype(jnp.bfloat16)
    return (context, arrived, stream_out)


def solution(mesh):
    placed = (
        P(("dp", "tp"), None, None),
        P(("dp", "tp"), None),
        P(("dp", "tp"), None, None),
        P(("dp", "tp"), None, None, None),
        P(("dp", "tp")),
        P(),
        P(),
        P(("dp", "tp"), None),
        P(),
        P("dp", "tp"),
        P("dp", "tp"),
        P("tp", "dp"),
        P(),
        P("tp", None, "dp"),
        P("tp", None, "dp"),
        P("tp", "dp", None),
        P(("dp", "tp"), None),
        P(("dp", "tp"), None),
    )
    return jax.shard_map(
        on_device,
        mesh=mesh,
        in_specs=placed,
        out_specs=(
            P(("dp", "tp"), None, None),
            P(("dp", "tp"), None, None, None),
            P(("dp", "tp"), None),
        ),
        check_vma=False,
    )
```

time: 252 us -> 212 us (0.84)
  waiting for transfers between devices: 123 us -> 78.6 us
  matrix products: 44.8 us -> 10.3 us
  Pallas kernels: 0 us -> 33.7 us
  starting transfers between devices: 47.2 us -> 63.5 us
  local copies, waits for them, and re-layouts: 20.4 us -> 10 us
    ppermute x30 -> x39, waiting for transfers between devices: 123 us -> 68.1 us  [swap(): return lax.ppermute(block, AXES, pairs)]
    dot_general x5 -> x2, matrix products: 41.5 us -> 6.79 us  [on_device(): jnp.dot(block, w_down, preferred_element_type=jnp.float32)]
    pallas_call x0 -> x5, Pallas kernels: none -> 33.7 us  [the longest x1 13.6 us: run_up(): pl.pallas_call(functools.partial(up_kernel, first, last, cut * width, wid...]
    ppermute x30 -> x39, starting transfers between devices: 37 us -> 52.6 us  [swap(): return lax.ppermute(block, AXES, pairs)]
    all_to_all x2, waiting for transfers between devices: 0.01 us -> 10.5 us  [the longest x1 10.5 us: on_device(): lax.all_to_all(outgoing, 'tp', split_axis=0, concat_axis=0, tiled=True)]
    unnamed x60 -> x48, local copies, waits for them, and re-layouts: 9.86 us -> 4.54 us
    add x3 -> x2, other arithmetic: 4.17 us -> 0.06 us  [the longest x1 0.06 us: reduce_core(): wide(mine[at:at + size]) + wide(got[at:at + size])]
    slice x7 -> x5, local copies, waits for them, and re-layouts: 3.28 us -> 0.12 us  [the longest x2 0.06 us: on_device(): near += reduce_core(down[:half], down[half:], 2)]
  transfers between devices with their start and end apart: 32 -> 41, of which waited for: 17 -> 20; matrix products, arithmetic and copies ran while one was open for 27% -> 11% of each run, Pallas kernels for 0% -> 13%
where the time goes in v2:
time: 212 us
  waiting for transfers between devices  78.6 us (37%)
  starting transfers between devices  63.5 us (30%)
  Pallas kernels  33.7 us (16%)
  other arithmetic  14.5 us (7%)
  matrix products  10.3 us (5%)
  local copies, waits for them, and re-layouts  10 us (5%)
    ppermute x39, waiting for transfers between devices, swap(): return lax.ppermute(block, AXES, pairs)  68.1 us
    ppermute x39, starting transfers between devices, swap(): return lax.ppermute(block, AXES, pairs)  52.6 us
    pallas_call x1, Pallas kernels, run_up(): pl.pallas_call(functools.partial(up_kernel, first, last, cut * width, wid...  13.6 us
    pallas_call x2, Pallas kernels, run_dense(): pl.pallas_call(functools.partial(dense_kernel, groups), out_shape=(jax.Sh...  10.8 us
    all_to_all x1, waiting for transfers between devices, on_device(): lax.all_to_all(outgoing, 'tp', split_axis=0, concat_axis=0, tiled=True)  10.5 us
    pallas_call x2, Pallas kernels, run_down(): pl.pallas_call(functools.partial(down_kernel, cut * width), out_shape=(ha...  9.23 us
    dot_general x2, matrix products, on_device(): jnp.dot(block, w_down, preferred_element_type=jnp.float32)  6.79 us
    all_to_all x1, starting transfers between devices, on_device(): lax.all_to_all(outgoing, 'tp', split_axis=0, concat_axis=0, tiled=True)  6.09 us
  transfers between devices with their start and end apart: 41, of which 20 were waited for; matrix products, arithmetic and copies ran while one was open for 11% of the time, Pallas kernels for 13%

profile of v2, /device:TPU:0, one launch (start us, length us, event | category | flops | bytes accessed | tf_op | source)
XLA Modules:
  0.0 211.8 jit_solution(9371915167642032855)
XLA Ops:
  2.7 3.1 %collective-permute-start = (bf16[8,7168]{1,0:T(8,128)(2,1)S(1)}, bf16[8,7168]{1,0:T(8,128)(2,1)S(1)}, u32[]{:S(2)}, u32[]{:S(2)}) collective-permute-start(bf16[8,7168]{1,0:T(8,128)(2,1)S(1)} %fusion.23), channel_id=1, source_target_pairs={{0,4},{1,5},{2,6},{3,7},{4,0},{5,1},{6,2},{7,3},{8,12},{9,13},{10,... | collective-permute-start | bytes 344072 | tf_op jit(solution)/shard_map/ppermute | solution.py:64
  5.8 2.6 %collective-permute-start.1 = (bf16[8,7168]{1,0:T(8,128)(2,1)S(1)}, bf16[8,7168]{1,0:T(8,128)(2,1)S(1)}, u32[]{:S(2)}, u32[]{:S(2)}) collective-permute-start(bf16[8,7168]{1,0:T(8,128)(2,1)S(1)} %fusion.23), channel_id=1, source_target_pairs={{0,8},{1,9},{2,10},{3,11},{4,12},{5,13},{6,14},{7,15},{8,0},{9,1},... | collective-permute-start | bytes 344072 | tf_op jit(solution)/shard_map/ppermute | solution.py:64
  9.4 8.1 %collective-permute-done.1 = bf16[8,7168]{1,0:T(8,128)(2,1)S(1)} collective-permute-done((bf16[8,7168]{1,0:T(8,128)(2,1)S(1)}, bf16[8,7168]{1,0:T(8,128)(2,1)S(1)}, u32[]{:S(2)}, u32[]{:S(2)}) %collective-permute-start.1) | collective-permute-done | bytes 114720 | tf_op jit(solution)/shard_map/ppermute | solution.py:64
  21.2 5.0 %collective-permute-done.3 = bf16[32,3584]{1,0:T(8,128)(2,1)S(1)} collective-permute-done((bf16[32,3584]{1,0:T(8,128)(2,1)S(1)}, bf16[32,3584]{1,0:T(8,128)(2,1)S(1)}, u32[]{:S(2)}, u32[]{:S(2)}) %collective-permute-start.3) | collective-permute-done | bytes 229408 | tf_op jit(solution)/shard_map/ppermute | solution.py:64
  26.5 2.4 %collective-permute-done.5 = bf16[32,3584]{1,0:T(8,128)(2,1)S(1)} collective-permute-done((bf16[32,3584]{1,0:T(8,128)(2,1)S(1)}, bf16[32,3584]{1,0:T(8,128)(2,1)S(1)}, u32[]{:S(2)}, u32[]{:S(2)}) %collective-permute-start.5) | collective-permute-done | bytes 229408 | tf_op jit(solution)/shard_map/ppermute | solution.py:64
  29.0 2.5 %collective-permute-done.6.other_ref = bf16[128,3584]{1,0:T(8,128)(2,1)S(1)} collective-permute-done((bf16[128,3584]{1,0:T(8,128)(2,1)S(1)}, bf16[128,3584]{1,0:T(8,128)(2,1)S(1)}, u32[]{:S(2)}, u32[]{:S(2)}) %collective-permute-start.6) | collective-permute-done | bytes 917536 | tf_op jit(solution)/shard_map/ppermute | solution.py:64
  31.5 5.4 %shard_map.193 = (f32[128,1152]{1,0:T(8,128)S(1)}, bf16[128,1152]{1,0:T(8,128)(2,1)S(1)}) custom-call(bf16[128,3584]{1,0:T(8,128)(2,1)S(1)} %pad_maximum_fusion.3.near_ref, bf16[128,3584]{1,0:T(8,128)(2,1)S(1)} %collective-permute-done.6.other_ref, bf16[3584,1152]{1,0:T(8,128)(2,1)} %hbm.2), custom_call_target="tpu_custom_call" | custom-call | tf_op jit(solution)/shard_map/pallas_call | solution.py:221
  38.5 5.4 %shard_map.194 = (f32[128,1152]{1,0:T(8,128)S(1)}, bf16[128,1152]{1,0:T(8,128)(2,1)S(1)}) custom-call(bf16[128,3584]{1,0:T(8,128)(2,1)S(1)} %pad_maximum_fusion.3.near_ref, bf16[128,3584]{1,0:T(8,128)(2,1)S(1)} %collective-permute-done.6.other_ref, bf16[3584,1152]{1,0:T(8,128)(2,1)} %hbm.3), custom_call_target="tpu_custom_call" | custom-call | tf_op jit(solution)/shard_map/pallas_call | solution.py:221
  45.8 6.1 %all-to-all-start = ((bf16[16,2,72,256]{3,2,1,0:T(8,128)(2,1)}), bf16[16,2,72,256]{3,2,1,0:T(8,128)(2,1)S(1)}, u32[]{:S(2)}, u32[]{:S(2)}) async-start(bf16[16,2,72,256]{3,2,1,0:T(8,128)(2,1)} %copy.56), calls=%async_computation | async-start | bytes 2359296 | tf_op jit(solution)/shard_map/all_to_all | solution.py:386
  54.2 5.4 %convolution_convert_fusion.1 = bf16[128,3584]{1,0:T(8,128)(2,1)S(1)} fusion(bf16[128,1152]{1,0:T(8,128)(2,1)S(1)} %multiply_convert_fusion, bf16[1152,3584]{1,0:T(8,128)(2,1)} %param.29), kind=kOutput, calls=%fused_computation.3 | convolution fusion | flops 1057423360 | bytes 9469952 | tf_op jit(solution)/shard_map/dot_general | solution.py:393
  66.5 10.5 %all-to-all-done = bf16[16,2,72,256]{3,2,1,0:T(8,128)(2,1)S(1)} async-done(((bf16[16,2,72,256]{3,2,1,0:T(8,128)(2,1)}), bf16[16,2,72,256]{3,2,1,0:T(8,128)(2,1)S(1)}, u32[]{:S(2)}, u32[]{:S(2)}) %all-to-all-start) | async-done | bytes 1179680 | tf_op jit(solution)/shard_map/all_to_all | solution.py:386
  77.0 3.1 %collective-permute-start.14 = (bf16[32,3584]{1,0:T(8,128)(2,1)S(1)}, bf16[32,3584]{1,0:T(8,128)(2,1)}, u32[]{:S(2)}, u32[]{:S(2)}) collective-permute-start(bf16[32,3584]{1,0:T(8,128)(2,1)S(1)} %convert_add_fusion.4), channel_id=1, source_target_pairs={{0,18},{1,19},{2,16},{3,17},{4,22},{5,23},{6,20},{7,21},{8,26},{9,... | collective-permute-start | bytes 688136 | tf_op jit(solution)/shard_map/ppermute | solution.py:64
  80.9 5.6 %collective-permute-done.14 = bf16[32,3584]{1,0:T(8,128)(2,1)} collective-permute-done((bf16[32,3584]{1,0:T(8,128)(2,1)S(1)}, bf16[32,3584]{1,0:T(8,128)(2,1)}, u32[]{:S(2)}, u32[]{:S(2)}) %collective-permute-start.14) | collective-permute-done | bytes 229408 | tf_op jit(solution)/shard_map/ppermute | solution.py:64
  88.0 3.5 %collective-permute-start.15 = (bf16[8,7168]{1,0:T(8,128)(2,1)S(1)}, bf16[8,7168]{1,0:T(8,128)(2,1)S(1)}, u32[]{:S(2)}, u32[]{:S(2)}) collective-permute-start(bf16[8,7168]{1,0:T(8,128)(2,1)S(1)} %get-tuple-element.67), channel_id=1, source_target_pairs={{0,4},{1,5},{2,6},{3,7},{4,0},{5,1},{6,2},{7,3},{8,12},{9,13},{10,... | collective-permute-start | bytes 344072 | tf_op jit(solution)/shard_map/ppermute | solution.py:64
  95.1 7.1 %collective-permute-done.16 = bf16[8,7168]{1,0:T(8,128)(2,1)S(1)} collective-permute-done((bf16[8,7168]{1,0:T(8,128)(2,1)S(1)}, bf16[8,7168]{1,0:T(8,128)(2,1)S(1)}, u32[]{:S(2)}, u32[]{:S(2)}) %collective-permute-start.16) | collective-permute-done | bytes 114720 | tf_op jit(solution)/shard_map/ppermute | solution.py:64
  102.5 2.7 %collective-permute-start.18 = (bf16[8,7296]{1,0:T(8,128)(2,1)S(1)}, bf16[8,7296]{1,0:T(8,128)(2,1)S(1)}, u32[]{:S(2)}, u32[]{:S(2)}) collective-permute-start(bf16[8,7296]{1,0:T(8,128)(2,1)S(1)} %get-tuple-element.79), channel_id=1, source_target_pairs={{0,4},{1,5},{2,6},{3,7},{4,0},{5,1},{6,2},{7,3},{8,12},{9,13},{10,... | collective-permute-start | bytes 350216 | tf_op jit(solution)/shard_map/ppermute | solution.py:64
  105.5 2.1 collective-permute-start.20
  108.8 7.4 %collective-permute-done.19 = bf16[8,7296]{1,0:T(8,128)(2,1)S(1)} collective-permute-done((bf16[8,7296]{1,0:T(8,128)(2,1)S(1)}, bf16[8,7296]{1,0:T(8,128)(2,1)S(1)}, u32[]{:S(2)}, u32[]{:S(2)}) %collective-permute-start.19) | collective-permute-done | bytes 116768 | tf_op jit(solution)/shard_map/ppermute | solution.py:64
  121.6 7.4 %collective-permute-done.21 = bf16[32,7296]{1,0:T(8,128)(2,1)S(1)} collective-permute-done((bf16[32,7296]{1,0:T(8,128)(2,1)S(1)}, bf16[32,7296]{1,0:T(8,128)(2,1)S(1)}, u32[]{:S(2)}, u32[]{:S(2)}) %collective-permute-start.21) | collective-permute-done | bytes 466976 | tf_op jit(solution)/shard_map/ppermute | solution.py:64
  129.1 1.9 collective-permute-done.22
  131.7 7.0 %collective-permute-done.23 = bf16[32,7296]{1,0:T(8,128)(2,1)} collective-permute-done((bf16[32,7296]{1,0:T(8,128)(2,1)S(1)}, bf16[32,7296]{1,0:T(8,128)(2,1)}, u32[]{:S(2)}, u32[]{:S(2)}) %collective-permute-start.23) | collective-permute-done | bytes 466976 | tf_op jit(solution)/shard_map/ppermute | solution.py:64
  143.8 4.8 %all-to-all-start.1 = ((bf16[16,2,72,256]{3,2,1,0:T(8,128)(2,1)}), bf16[16,2,72,256]{3,2,1,0:T(8,128)(2,1)}, u32[]{:S(2)}, u32[]{:S(2)}) async-start(bf16[16,2,72,256]{3,2,1,0:T(8,128)(2,1)} %bitcast.71), calls=%async_computation.1 | async-start | bytes 2359296 | tf_op jit(solution)/shard_map/all_to_all | solution.py:423
  149.4 13.6 %shard_map.195.inner_ref = bf16[256,1024]{1,0:T(8,128)(2,1)S(1)} custom-call(bf16[128,7296]{1,0:T(8,128)(2,1)S(1)} %pad_maximum_fusion.refs_0_, bf16[128,7296]{1,0:T(8,128)(2,1)} %collective-permute-done.24.refs_1_, bf16[1,7168,1024]{2,1,0:T(8,128)(2,1)} %refs_2_.1, bf16[1,7168,1024]{2,1,0:T(8,128)(2,1)} %refs_3_.1), custom_call_target="tpu_custom_call" | custom-call | tf_op jit(solution)/shard_map/pallas_call | solution.py:306
  163.1 4.8 %shard_map.196 = (bf16[128,3584]{1,0:T(8,128)(2,1)S(1)}, bf16[128,3584]{1,0:T(8,128)(2,1)S(1)}) custom-call(bf16[256,1024]{1,0:T(8,128)(2,1)S(1)} %shard_map.195.inner_ref, bf16[1,1024,7168]{2,1,0:T(8,128)(2,1)} %down_hbm.3), custom_call_target="tpu_custom_call" | custom-call | tf_op jit(solution)/shard_map/pallas_call | solution.py:342
  170.1 4.4 %shard_map.197 = (bf16[128,3584]{1,0:T(8,128)(2,1)S(1)}, bf16[128,3584]{1,0:T(8,128)(2,1)S(1)}) custom-call(bf16[256,1024]{1,0:T(8,128)(2,1)S(1)} %shard_map.195.inner_ref, bf16[1,1024,7168]{2,1,0:T(8,128)(2,1)} %down_hbm.3), custom_call_target="tpu_custom_call" | custom-call | tf_op jit(solution)/shard_map/pallas_call | solution.py:342
  175.8 1.9 collective-permute-start.33
  180.6 1.9 collective-permute-start.27
  188.0 2.9 %collective-permute-done.35 = bf16[32,3584]{1,0:T(8,128)(2,1)} collective-permute-done((bf16[32,3584]{1,0:T(8,128)(2,1)}, bf16[32,3584]{1,0:T(8,128)(2,1)}, u32[]{:S(2)}, u32[]{:S(2)}) %collective-permute-start.35) | collective-permute-done | bytes 229408 | tf_op jit(solution)/shard_map/ppermute | solution.py:64
  192.3 2.8 %collective-permute-start.36 = (bf16[8,3584]{1,0:T(8,128)(2,1)S(1)}, bf16[8,3584]{1,0:T(8,128)(2,1)S(1)}, u32[]{:S(2)}, u32[]{:S(2)}) collective-permute-start(bf16[8,3584]{1,0:T(8,128)(2,1)S(1)} %get-tuple-element.75), channel_id=1, source_target_pairs={{0,4},{1,5},{2,6},{3,7},{4,0},{5,1},{6,2},{7,3},{8,12},{9,13},{10,... | collective-permute-start | bytes 172040 | tf_op jit(solution)/shard_map/ppermute | solution.py:64
  197.5 2.3 %collective-permute-done.29 = bf16[32,3584]{1,0:T(8,128)(2,1)S(1)} collective-permute-done((bf16[32,3584]{1,0:T(8,128)(2,1)S(1)}, bf16[32,3584]{1,0:T(8,128)(2,1)S(1)}, u32[]{:S(2)}, u32[]{:S(2)}) %collective-permute-start.29) | collective-permute-done | bytes 229408 | tf_op jit(solution)/shard_map/ppermute | solution.py:64
  200.9 3.0 %collective-permute-start.30 = (bf16[8,3584]{1,0:T(8,128)(2,1)S(1)}, bf16[8,3584]{1,0:T(8,128)(2,1)S(1)}, u32[]{:S(2)}, u32[]{:S(2)}) collective-permute-start(bf16[8,3584]{1,0:T(8,128)(2,1)S(1)} %get-tuple-element.72), channel_id=1, source_target_pairs={{0,4},{1,5},{2,6},{3,7},{4,0},{5,1},{6,2},{7,3},{8,12},{9,13},{10,... | collective-permute-start | bytes 172040 | tf_op jit(solution)/shard_map/ppermute | solution.py:64
  207.4 2.6 %collective-permute-done.31 = bf16[8,3584]{1,0:T(8,128)(2,1)S(1)} collective-permute-done((bf16[8,3584]{1,0:T(8,128)(2,1)S(1)}, bf16[8,3584]{1,0:T(8,128)(2,1)S(1)}, u32[]{:S(2)}, u32[]{:S(2)}) %collective-permute-start.31) | collective-permute-done | bytes 57376 | tf_op jit(solution)/shard_map/ppermute | solution.py:64
  (178 shorter events, 61.4 us)
Async XLA Ops:
  5.8 11.7 %collective-permute-start.1 = (bf16[8,7168]{1,0:T(8,128)(2,1)S(1)}, bf16[8,7168]{1,0:T(8,128)(2,1)S(1)}, u32[]{:S(2)}, u32[]{:S(2)}) collective-permute-start(bf16[8,7168]{1,0:T(8,128)(2,1)S(1)} %fusion.23), channel_id=1, source_target_pairs={{0,8},{1,9},{2,10},{3,11},{4,12},{5,13},{6,14},{7,15},{8,0},{9,1},... | collective-permute-start | bytes 344072 | tf_op jit(solution)/shard_map/ppermute | solution.py:64
  8.4 9.1 %collective-permute-start.2 = (bf16[8,7168]{1,0:T(8,128)(2,1)S(1)}, bf16[8,7168]{1,0:T(8,128)(2,1)S(1)}, u32[]{:S(2)}, u32[]{:S(2)}) collective-permute-start(bf16[8,7168]{1,0:T(8,128)(2,1)S(1)} %fusion.23), channel_id=1, source_target_pairs={{0,12},{1,13},{2,14},{3,15},{4,8},{5,9},{6,10},{7,11},{8,4},{9,5},... | collective-permute-start | bytes 344072 | tf_op jit(solution)/shard_map/ppermute | solution.py:64
  17.6 8.5 %collective-permute-start.3 = (bf16[32,3584]{1,0:T(8,128)(2,1)S(1)}, bf16[32,3584]{1,0:T(8,128)(2,1)S(1)}, u32[]{:S(2)}, u32[]{:S(2)}) collective-permute-start(bf16[32,3584]{1,0:T(8,128)(2,1)S(1)} %get-tuple-element.70), channel_id=1, source_target_pairs={{0,2},{1,3},{2,0},{3,1},{4,6},{5,7},{6,4},{7,5},{8,10},{9,11},{10,... | collective-permute-start | bytes 688136 | tf_op jit(solution)/shard_map/ppermute | solution.py:64
  19.2 7.3 %collective-permute-start.4 = (bf16[32,3584]{1,0:T(8,128)(2,1)S(1)}, bf16[32,3584]{1,0:T(8,128)(2,1)S(1)}, u32[]{:S(2)}, u32[]{:S(2)}) collective-permute-start(bf16[32,3584]{1,0:T(8,128)(2,1)S(1)} %get-tuple-element.71), channel_id=1, source_target_pairs={{0,16},{1,17},{2,18},{3,19},{4,20},{5,21},{6,22},{7,23},{8,24},{9,... | collective-permute-start | bytes 688136 | tf_op jit(solution)/shard_map/ppermute | solution.py:64
  20.7 8.2 %collective-permute-start.5 = (bf16[32,3584]{1,0:T(8,128)(2,1)S(1)}, bf16[32,3584]{1,0:T(8,128)(2,1)S(1)}, u32[]{:S(2)}, u32[]{:S(2)}) collective-permute-start(bf16[32,3584]{1,0:T(8,128)(2,1)S(1)} %get-tuple-element.71), channel_id=1, source_target_pairs={{0,18},{1,19},{2,16},{3,17},{4,22},{5,23},{6,20},{7,21},{8,26},{9,... | collective-permute-start | bytes 688136 | tf_op jit(solution)/shard_map/ppermute | solution.py:64
  36.9 15.0 %collective-permute-start.7 = (bf16[128,1152]{1,0:T(8,128)(2,1)S(1)}, bf16[128,1152]{1,0:T(8,128)(2,1)S(1)}, u32[]{:S(2)}, u32[]{:S(2)}) collective-permute-start(bf16[128,1152]{1,0:T(8,128)(2,1)S(1)} %get-tuple-element.21), channel_id=1, source_target_pairs={{0,16},{1,17},{2,18},{3,19},{4,20},{5,21},{6,22},{7,23},{8,24},{9,... | collective-permute-start | bytes 884744 | tf_op jit(solution)/shard_map/ppermute | solution.py:64
  43.9 8.8 %collective-permute-start.8 = (bf16[128,1152]{1,0:T(8,128)(2,1)S(1)}, bf16[128,1152]{1,0:T(8,128)(2,1)S(1)}, u32[]{:S(2)}, u32[]{:S(2)}) collective-permute-start(bf16[128,1152]{1,0:T(8,128)(2,1)S(1)} %get-tuple-element.23), channel_id=1, source_target_pairs={{0,16},{1,17},{2,18},{3,19},{4,20},{5,21},{6,22},{7,23},{8,24},{9,... | collective-permute-start | bytes 884744 | tf_op jit(solution)/shard_map/ppermute | solution.py:64
  45.8 31.2 %all-to-all-start = ((bf16[16,2,72,256]{3,2,1,0:T(8,128)(2,1)}), bf16[16,2,72,256]{3,2,1,0:T(8,128)(2,1)S(1)}, u32[]{:S(2)}, u32[]{:S(2)}) async-start(bf16[16,2,72,256]{3,2,1,0:T(8,128)(2,1)} %copy.56), calls=%async_computation | async-start | bytes 2359296 | tf_op jit(solution)/shard_map/all_to_all | solution.py:386
  53.0 8.6 %collective-permute-start.11 = (bf16[128,1152]{1,0:T(8,128)(2,1)S(1)}, bf16[128,1152]{1,0:T(8,128)(2,1)S(1)}, u32[]{:S(2)}, u32[]{:S(2)}) collective-permute-start(bf16[128,1152]{1,0:T(8,128)(2,1)S(1)} %multiply_convert_fusion), channel_id=1, source_target_pairs={{0,16},{1,17},{2,18},{3,19},{4,20},{5,21},{6,22},{7,23},{8,24},{9,... | collective-permute-start | bytes 884744 | tf_op jit(solution)/shard_map/ppermute | solution.py:64
  63.1 17.1 %collective-permute-start.10 = (bf16[32,3584]{1,0:T(8,128)(2,1)S(1)}, bf16[32,3584]{1,0:T(8,128)(2,1)S(1)}, u32[]{:S(2)}, u32[]{:S(2)}) collective-permute-start(bf16[32,3584]{1,0:T(8,128)(2,1)S(1)} %add_convert_fusion.8), channel_id=1, source_target_pairs={{0,2},{1,3},{2,0},{3,1},{4,6},{5,7},{6,4},{7,5},{8,10},{9,11},{10,... | collective-permute-start | bytes 688136 | tf_op jit(solution)/shard_map/ppermute | solution.py:64
  64.9 15.3 %collective-permute-start.13 = (bf16[32,3584]{1,0:T(8,128)(2,1)S(1)}, bf16[32,3584]{1,0:T(8,128)(2,1)S(1)}, u32[]{:S(2)}, u32[]{:S(2)}) collective-permute-start(bf16[32,3584]{1,0:T(8,128)(2,1)S(1)} %add_convert_fusion.7), channel_id=1, source_target_pairs={{0,16},{1,17},{2,18},{3,19},{4,20},{5,21},{6,22},{7,23},{8,24},{9,... | collective-permute-start | bytes 688136 | tf_op jit(solution)/shard_map/ppermute | solution.py:64
  77.0 9.5 %collective-permute-start.14 = (bf16[32,3584]{1,0:T(8,128)(2,1)S(1)}, bf16[32,3584]{1,0:T(8,128)(2,1)}, u32[]{:S(2)}, u32[]{:S(2)}) collective-permute-start(bf16[32,3584]{1,0:T(8,128)(2,1)S(1)} %convert_add_fusion.4), channel_id=1, source_target_pairs={{0,18},{1,19},{2,16},{3,17},{4,22},{5,23},{6,20},{7,21},{8,26},{9,... | collective-permute-start | bytes 688136 | tf_op jit(solution)/shard_map/ppermute | solution.py:64
  88.0 7.1 %collective-permute-start.15 = (bf16[8,7168]{1,0:T(8,128)(2,1)S(1)}, bf16[8,7168]{1,0:T(8,128)(2,1)S(1)}, u32[]{:S(2)}, u32[]{:S(2)}) collective-permute-start(bf16[8,7168]{1,0:T(8,128)(2,1)S(1)} %get-tuple-element.67), channel_id=1, source_target_pairs={{0,4},{1,5},{2,6},{3,7},{4,0},{5,1},{6,2},{7,3},{8,12},{9,13},{10,... | collective-permute-start | bytes 344072 | tf_op jit(solution)/shard_map/ppermute | solution.py:64
  91.5 10.7 %collective-permute-start.16 = (bf16[8,7168]{1,0:T(8,128)(2,1)S(1)}, bf16[8,7168]{1,0:T(8,128)(2,1)S(1)}, u32[]{:S(2)}, u32[]{:S(2)}) collective-permute-start(bf16[8,7168]{1,0:T(8,128)(2,1)S(1)} %get-tuple-element.69), channel_id=1, source_target_pairs={{0,8},{1,9},{2,10},{3,11},{4,12},{5,13},{6,14},{7,15},{8,0},{9,1},... | collective-permute-start | bytes 344072 | tf_op jit(solution)/shard_map/ppermute | solution.py:64
  92.8 9.3 %collective-permute-start.17 = (bf16[8,7168]{1,0:T(8,128)(2,1)S(1)}, bf16[8,7168]{1,0:T(8,128)(2,1)S(1)}, u32[]{:S(2)}, u32[]{:S(2)}) collective-permute-start(bf16[8,7168]{1,0:T(8,128)(2,1)S(1)} %get-tuple-element.68), channel_id=1, source_target_pairs={{0,12},{1,13},{2,14},{3,15},{4,8},{5,9},{6,10},{7,11},{8,4},{9,5},... | collective-permute-start | bytes 344072 | tf_op jit(solution)/shard_map/ppermute | solution.py:64
  105.2 11.0 %collective-permute-start.19 = (bf16[8,7296]{1,0:T(8,128)(2,1)S(1)}, bf16[8,7296]{1,0:T(8,128)(2,1)S(1)}, u32[]{:S(2)}, u32[]{:S(2)}) collective-permute-start(bf16[8,7296]{1,0:T(8,128)(2,1)S(1)} %get-tuple-element.79), channel_id=1, source_target_pairs={{0,8},{1,9},{2,10},{3,11},{4,12},{5,13},{6,14},{7,15},{8,0},{9,1},... | collective-permute-start | bytes 350216 | tf_op jit(solution)/shard_map/ppermute | solution.py:64
  105.5 10.7 %collective-permute-start.20 = (bf16[8,7296]{1,0:T(8,128)(2,1)S(1)}, bf16[8,7296]{1,0:T(8,128)(2,1)S(1)}, u32[]{:S(2)}, u32[]{:S(2)}) collective-permute-start(bf16[8,7296]{1,0:T(8,128)(2,1)S(1)} %get-tuple-element.79), channel_id=1, source_target_pairs={{0,12},{1,13},{2,14},{3,15},{4,8},{5,9},{6,10},{7,11},{8,4},{9,5},... | collective-permute-start | bytes 350216 | tf_op jit(solution)/shard_map/ppermute | solution.py:64
  116.3 12.8 %collective-permute-start.21 = (bf16[32,7296]{1,0:T(8,128)(2,1)S(1)}, bf16[32,7296]{1,0:T(8,128)(2,1)S(1)}, u32[]{:S(2)}, u32[]{:S(2)}) collective-permute-start(bf16[32,7296]{1,0:T(8,128)(2,1)S(1)} %maximum_bitcast_fusion), channel_id=1, source_target_pairs={{0,2},{1,3},{2,0},{3,1},{4,6},{5,7},{6,4},{7,5},{8,10},{9,11},{10,... | collective-permute-start | bytes 1400840 | tf_op jit(solution)/shard_map/ppermute | solution.py:64
  117.3 13.6 %collective-permute-start.22 = (bf16[32,7296]{1,0:T(8,128)(2,1)S(1)}, bf16[32,7296]{1,0:T(8,128)(2,1)S(1)}, u32[]{:S(2)}, u32[]{:S(2)}) collective-permute-start(bf16[32,7296]{1,0:T(8,128)(2,1)S(1)} %maximum_bitcast_fusion), channel_id=1, source_target_pairs={{0,16},{1,17},{2,18},{3,19},{4,20},{5,21},{6,22},{7,23},{8,24},{9,... | collective-permute-start | bytes 1400840 | tf_op jit(solution)/shard_map/ppermute | solution.py:64
  118.8 19.9 %collective-permute-start.23 = (bf16[32,7296]{1,0:T(8,128)(2,1)S(1)}, bf16[32,7296]{1,0:T(8,128)(2,1)}, u32[]{:S(2)}, u32[]{:S(2)}) collective-permute-start(bf16[32,7296]{1,0:T(8,128)(2,1)S(1)} %maximum_bitcast_fusion), channel_id=1, source_target_pairs={{0,18},{1,19},{2,16},{3,17},{4,22},{5,23},{6,20},{7,21},{8,26},{9,... | collective-permute-start | bytes 1400840 | tf_op jit(solution)/shard_map/ppermute | solution.py:64
  140.2 9.2 %collective-permute-start.24 = (bf16[128,7296]{1,0:T(8,128)(2,1)S(1)}, bf16[128,7296]{1,0:T(8,128)(2,1)}, u32[]{:S(2)}, u32[]{:S(2)}) collective-permute-start(bf16[128,7296]{1,0:T(8,128)(2,1)S(1)} %pad_maximum_fusion.refs_0_), channel_id=1, source_target_pairs={{0,1},{1,0},{2,3},{3,2},{4,5},{5,4},{6,7},{7,6},{8,9},{9,8},{10,11... | collective-permute-start | bytes 5603336 | tf_op jit(solution)/shard_map/ppermute | solution.py:64
  143.8 35.5 %all-to-all-start.1 = ((bf16[16,2,72,256]{3,2,1,0:T(8,128)(2,1)}), bf16[16,2,72,256]{3,2,1,0:T(8,128)(2,1)}, u32[]{:S(2)}, u32[]{:S(2)}) async-start(bf16[16,2,72,256]{3,2,1,0:T(8,128)(2,1)} %bitcast.71), calls=%async_computation.1 | async-start | bytes 2359296 | tf_op jit(solution)/shard_map/all_to_all | solution.py:423
  167.9 6.9 %collective-permute-start.25 = (bf16[128,3584]{1,0:T(8,128)(2,1)S(1)}, bf16[128,3584]{1,0:T(8,128)(2,1)S(1)}, u32[]{:S(2)}, u32[]{:S(2)}) collective-permute-start(bf16[128,3584]{1,0:T(8,128)(2,1)S(1)} %get-tuple-element.29), channel_id=1, source_target_pairs={{0,1},{1,0},{2,3},{3,2},{4,5},{5,4},{6,7},{7,6},{8,9},{9,8},{10,11... | collective-permute-start | bytes 2752520 | tf_op jit(solution)/shard_map/ppermute | solution.py:64
  175.8 11.7 %collective-permute-start.33 = (bf16[32,3584]{1,0:T(8,128)(2,1)}, bf16[32,3584]{1,0:T(8,128)(2,1)}, u32[]{:S(2)}, u32[]{:S(2)}) collective-permute-start(bf16[32,3584]{1,0:T(8,128)(2,1)} %get-tuple-element.63), channel_id=1, source_target_pairs={{0,2},{1,3},{2,0},{3,1},{4,6},{5,7},{6,4},{7,5},{8,10},{9,11},{10,... | collective-permute-start | bytes 688136 | tf_op jit(solution)/shard_map/ppermute | solution.py:64
  177.6 10.4 %collective-permute-start.34 = (bf16[32,3584]{1,0:T(8,128)(2,1)}, bf16[32,3584]{1,0:T(8,128)(2,1)}, u32[]{:S(2)}, u32[]{:S(2)}) collective-permute-start(bf16[32,3584]{1,0:T(8,128)(2,1)} %get-tuple-element.65), channel_id=1, source_target_pairs={{0,16},{1,17},{2,18},{3,19},{4,20},{5,21},{6,22},{7,23},{8,24},{9,... | collective-permute-start | bytes 688136 | tf_op jit(solution)/shard_map/ppermute | solution.py:64
  179.1 11.8 %collective-permute-start.35 = (bf16[32,3584]{1,0:T(8,128)(2,1)}, bf16[32,3584]{1,0:T(8,128)(2,1)}, u32[]{:S(2)}, u32[]{:S(2)}) collective-permute-start(bf16[32,3584]{1,0:T(8,128)(2,1)} %get-tuple-element.64), channel_id=1, source_target_pairs={{0,18},{1,19},{2,16},{3,17},{4,22},{5,23},{6,20},{7,21},{8,26},{9,... | collective-permute-start | bytes 688136 | tf_op jit(solution)/shard_map/ppermute | solution.py:64
  180.6 16.0 %collective-permute-start.27 = (bf16[32,3584]{1,0:T(8,128)(2,1)S(1)}, bf16[32,3584]{1,0:T(8,128)(2,1)S(1)}, u32[]{:S(2)}, u32[]{:S(2)}) collective-permute-start(bf16[32,3584]{1,0:T(8,128)(2,1)S(1)} %get-tuple-element.60), channel_id=1, source_target_pairs={{0,2},{1,3},{2,0},{3,1},{4,6},{5,7},{6,4},{7,5},{8,10},{9,11},{10,... | collective-permute-start | bytes 688136 | tf_op jit(solution)/shard_map/ppermute | solution.py:64
  182.5 15.0 %collective-permute-start.28 = (bf16[32,3584]{1,0:T(8,128)(2,1)S(1)}, bf16[32,3584]{1,0:T(8,128)(2,1)S(1)}, u32[]{:S(2)}, u32[]{:S(2)}) collective-permute-start(bf16[32,3584]{1,0:T(8,128)(2,1)S(1)} %get-tuple-element.62), channel_id=1, source_target_pairs={{0,16},{1,17},{2,18},{3,19},{4,20},{5,21},{6,22},{7,23},{8,24},{9,... | collective-permute-start | bytes 688136 | tf_op jit(solution)/shard_map/ppermute | solution.py:64
  187.5 12.3 %collective-permute-start.29 = (bf16[32,3584]{1,0:T(8,128)(2,1)S(1)}, bf16[32,3584]{1,0:T(8,128)(2,1)S(1)}, u32[]{:S(2)}, u32[]{:S(2)}) collective-permute-start(bf16[32,3584]{1,0:T(8,128)(2,1)S(1)} %get-tuple-element.61), channel_id=1, source_target_pairs={{0,18},{1,19},{2,16},{3,17},{4,22},{5,23},{6,20},{7,21},{8,26},{9,... | collective-permute-start | bytes 688136 | tf_op jit(solution)/shard_map/ppermute | solution.py:64
  192.3 12.8 %collective-permute-start.36 = (bf16[8,3584]{1,0:T(8,128)(2,1)S(1)}, bf16[8,3584]{1,0:T(8,128)(2,1)S(1)}, u32[]{:S(2)}, u32[]{:S(2)}) collective-permute-start(bf16[8,3584]{1,0:T(8,128)(2,1)S(1)} %get-tuple-element.75), channel_id=1, source_target_pairs={{0,4},{1,5},{2,6},{3,7},{4,0},{5,1},{6,2},{7,3},{8,12},{9,13},{10,... | collective-permute-start | bytes 172040 | tf_op jit(solution)/shard_map/ppermute | solution.py:64
  195.1 12.3 %collective-permute-start.37 = (bf16[8,3584]{1,0:T(8,128)(2,1)S(1)}, bf16[8,3584]{1,0:T(8,128)(2,1)S(1)}, u32[]{:S(2)}, u32[]{:S(2)}) collective-permute-start(bf16[8,3584]{1,0:T(8,128)(2,1)S(1)} %get-tuple-element.77), channel_id=1, source_target_pairs={{0,8},{1,9},{2,10},{3,11},{4,12},{5,13},{6,14},{7,15},{8,0},{9,1},... | collective-permute-start | bytes 172040 | tf_op jit(solution)/shard_map/ppermute | solution.py:64
  196.6 10.8 %collective-permute-start.38 = (bf16[8,3584]{1,0:T(8,128)(2,1)S(1)}, bf16[8,3584]{1,0:T(8,128)(2,1)S(1)}, u32[]{:S(2)}, u32[]{:S(2)}) collective-permute-start(bf16[8,3584]{1,0:T(8,128)(2,1)S(1)} %get-tuple-element.76), channel_id=1, source_target_pairs={{0,12},{1,13},{2,14},{3,15},{4,8},{5,9},{6,10},{7,11},{8,4},{9,5},... | collective-permute-start | bytes 172040 | tf_op jit(solution)/shard_map/ppermute | solution.py:64
  (33 other events, 286.6 us)

commit v3 on v2

--- a/solution.py
+++ b/solution.py
@@ -14,7 +14,7 @@
 EPS = 1e-06
 ROUTE_SCALE = 2.5
 AXES = ("dp", "tp")
-CUTS = 1
+CUTS = 2
 DOWN_CUTS = 2
 DOWN_STEP = 896
 STEP = 1024
@@ -235,53 +235,47 @@
     )(near, other, in_hbm(weights))
 
 
-def up_kernel(first, last, base, width, experts, *refs):
-    refs = list(refs)
-    near_ref, other_ref, gate_hbm, up_hbm = refs[:4]
-    del refs[:4]
-    if not first:
-        gate_in, up_in, share_in = refs[:3]
-        del refs[:3]
-    if last:
-        inner_ref = refs.pop(0)
-        gate_acc, up_acc = refs.pop(0), refs.pop(0)
-    else:
-        gate_acc, up_acc, share_out = refs[:3]
-        del refs[:3]
-    gate_buf, up_buf, gate_sem, up_sem = refs
-    count = width // STEP
+def expert_kernel(outs, experts, *refs):
+    parts, refs = refs[:2], refs[2:]
+    gate_hbm, up_hbm, down_hbm = refs[:3]
+    results, refs = refs[3 : 3 + 2 * outs], refs[3 + 2 * outs :]
+    rows_ref, tail_ref, inner_ref, gate_buf, up_buf, down_buf, gate_acc, up_acc, row_sem, gate_sem, up_sem, down_sem = refs
+    half, width = rows_ref.shape[0] // 2, rows_ref.shape[1]
+    span = width // outs
 
     def copies(hbm, buf, sem):
         def make(at):
             slot = lax.rem(at, SLOTS)
             return pltpu.make_async_copy(
-                hbm.at[0, pl.ds(base + at * STEP, STEP)], buf.at[slot], sem.at[slot]
+                hbm.at[0, pl.ds(at * STEP, STEP)], buf.at[slot], sem.at[slot]
             )
 
-        return count, make
-
+        return width // STEP, make
+
+    def make_down(at):
+        slot = lax.rem(at, SLOTS)
+        where = pl.ds(pl.multiple_of(at * DOWN_STEP, 128), DOWN_STEP)
+        return pltpu.make_async_copy(down_hbm.at[0, :, where], down_buf.at[slot], down_sem.at[slot])
+
+    moves = []
+    for side in range(2):
+        where = pl.ds(side * half, half)
+        moves.append((parts[side].at[:, pl.ds(0, width)], rows_ref.at[where]))
+        moves.append((parts[side].at[:, pl.ds(width, 128)], tail_ref.at[where]))
+    moves = [pltpu.make_async_copy(*move, row_sem.at[at]) for at, move in enumerate(moves)]
+    for move in moves:
+        move.start()
     gate_wait, gate_free = ring(copies(gate_hbm, gate_buf, gate_sem), SLOTS)
     up_wait, up_free = ring(copies(up_hbm, up_buf, up_sem), SLOTS)
-    if first:
-        gate_acc[...] = jnp.zeros_like(gate_acc)
-        up_acc[...] = jnp.zeros_like(up_acc)
-        lane = lax.broadcasted_iota(jnp.int32, (1, 128), 1)
-        rank = lax.axis_index("tp")
-        mine = (lane == rank) | (lane == rank + experts)
-        tail = jnp.concatenate([near_ref[:, width:], other_ref[:, width:]], axis=0)
-        tail = jnp.where(mine, tail.astype(jnp.float32), 0.0)
-        share = jnp.sum(tail, axis=1, keepdims=True)
-    else:
-        gate_acc[...] = gate_in[...]
-        up_acc[...] = up_in[...]
-        share = share_in[:, :1]
-    if not last:
-        share_out[...] = jnp.broadcast_to(share, share_out.shape)
-
-    @pl.loop(0, count)
+    down_wait, down_free = ring((width // DOWN_STEP, make_down), SLOTS)
+    gate_acc[...] = jnp.zeros_like(gate_acc)
+    up_acc[...] = jnp.zeros_like(up_acc)
+    for move in moves:
+        move.wait()
+
+    @pl.loop(0, width // STEP)
     def _(at):
-        where = pl.ds(pl.multiple_of(at * STEP, 128), STEP)
-        rows = jnp.concatenate([near_ref[:, where], other_ref[:, where]], axis=0)
+        rows = rows_ref[:, pl.ds(pl.multiple_of(at * STEP, 128), STEP)]
         slot = lax.rem(at, SLOTS)
         gate_wait(at)
         gate_acc[...] += jnp.dot(rows, gate_buf[slot], preferred_element_type=jnp.float32)
@@ -290,66 +284,58 @@
         up_acc[...] += jnp.dot(rows, up_buf[slot], preferred_element_type=jnp.float32)
         up_free(at)
 
-    if last:
-        gate = gate_acc[...]
-        inner_ref[...] = (gate / (1.0 + jnp.exp(-gate)) * up_acc[...] * share).astype(jnp.bfloat16)
-
-
-def run_up(cut, near, other, gate_w, up_w, state, width, experts):
-    first, last = cut == 0, cut == CUTS - 1
-    count, hidden = 2 * near.shape[0], gate_w.shape[2]
+    lane = lax.broadcasted_iota(jnp.int32, (1, 128), 1)
+    rank = lax.axis_index("tp")
+    mine = (lane == rank) | (lane == rank + experts)
+    share = jnp.sum(jnp.where(mine, tail_ref[...].astype(jnp.float32), 0.0), axis=1, keepdims=True)
+    gate = gate_acc[...]
+    inner_ref[...] = (gate / (1.0 + jnp.exp(-gate)) * up_acc[...] * share).astype(jnp.bfloat16)
+
+    for one in range(outs):
+        near_ref, away_ref = results[2 * one : 2 * one + 2]
+        first = one * (span // DOWN_STEP)
+
+        @pl.loop(0, span // DOWN_STEP)
+        def _(step, near_ref=near_ref, away_ref=away_ref, first=first):
+            at = first + step
+            down_wait(at)
+            where = pl.ds(pl.multiple_of(step * DOWN_STEP, 128), DOWN_STEP)
+            weights = down_buf[lax.rem(at, SLOTS)]
+            out = jnp.dot(inner_ref[...], weights, preferred_element_type=jnp.float32)
+            near_ref[:, where] = out[:half].astype(jnp.bfloat16)
+            away_ref[:, where] = out[half:].astype(jnp.bfloat16)
+            down_free(at)
+
+
+def run_expert(near, other, gate_w, up_w, down_w, experts):
+    count, width, hidden = 2 * near.shape[0], gate_w.shape[1], gate_w.shape[2]
     vmem, far = pl.BlockSpec(memory_space=pltpu.VMEM), pl.BlockSpec(memory_space=HBM)
-    total = jax.ShapeDtypeStruct((count, hidden), jnp.float32)
-    inner = jax.ShapeDtypeStruct((count, hidden), jnp.bfloat16)
-    share = jax.ShapeDtypeStruct((count, 128), jnp.float32)
-    scratch = [pltpu.VMEM((count, hidden), jnp.float32)] * 2 if last else []
-    return pl.pallas_call(
-        functools.partial(up_kernel, first, last, cut * width, width, experts),
-        out_shape=inner if last else (total, total, share),
-        in_specs=[vmem, vmem, far, far] + [vmem] * len(state),
-        out_specs=vmem if last else (vmem, vmem, vmem),
-        scratch_shapes=scratch
-        + [pltpu.VMEM((SLOTS, STEP, hidden), jnp.bfloat16)] * 2
-        + [pltpu.SemaphoreType.DMA((SLOTS,))] * 2,
-        compiler_params=pltpu.CompilerParams(vmem_limit_bytes=18 * 1024 * 1024),
-    )(near, other, in_hbm(gate_w), in_hbm(up_w), *state)
-
-
-def down_kernel(base, inner_ref, down_hbm, near_ref, away_ref, buf, sem):
-    half, width = near_ref.shape
-
-    def make(at):
-        slot = lax.rem(at, SLOTS)
-        where = pl.ds(base + at * DOWN_STEP, DOWN_STEP)
-        return pltpu.make_async_copy(down_hbm.at[0, :, where], buf.at[slot], sem.at[slot])
-
-    wait, free = ring((width // DOWN_STEP, make), SLOTS)
-
-    @pl.loop(0, width // DOWN_STEP)
-    def _(at):
-        wait(at)
-        where = pl.ds(pl.multiple_of(at * DOWN_STEP, 128), DOWN_STEP)
-        out = jnp.dot(inner_ref[...], buf[lax.rem(at, SLOTS)], preferred_element_type=jnp.float32)
-        near_ref[:, where] = out[:half].astype(jnp.bfloat16)
-        away_ref[:, where] = out[half:].astype(jnp.bfloat16)
-        free(at)
-
-
-def run_down(cut, inner, down_w, width):
-    count, hidden = inner.shape
-    vmem, far = pl.BlockSpec(memory_space=pltpu.VMEM), pl.BlockSpec(memory_space=HBM)
-    half = jax.ShapeDtypeStruct((count // 2, width), jnp.bfloat16)
-    return pl.pallas_call(
-        functools.partial(down_kernel, cut * width),
-        out_shape=(half, half),
-        in_specs=[vmem, far],
-        out_specs=(vmem, vmem),
+    total = pltpu.VMEM((count, hidden), jnp.float32)
+    weights = pltpu.VMEM((SLOTS, STEP, hidden), jnp.bfloat16)
+    half = jax.ShapeDtypeStruct((count // 2, width // DOWN_CUTS), jnp.bfloat16)
+    sems = pltpu.SemaphoreType.DMA((SLOTS,))
+    out = pl.pallas_call(
+        functools.partial(expert_kernel, DOWN_CUTS, experts),
+        out_shape=(half,) * (2 * DOWN_CUTS),
+        in_specs=[pl.BlockSpec(memory_space=pl.ANY)] * 2 + [far] * 3,
+        out_specs=(vmem,) * (2 * DOWN_CUTS),
         scratch_shapes=[
+            pltpu.VMEM((count, width), jnp.bfloat16),
+            pltpu.VMEM((count, 128), jnp.bfloat16),
+            pltpu.VMEM((count, hidden), jnp.bfloat16),
+            weights,
+            weights,
             pltpu.VMEM((SLOTS, hidden, DOWN_STEP), jnp.bfloat16),
-            pltpu.SemaphoreType.DMA((SLOTS,)),
+            total,
+            total,
+            pltpu.SemaphoreType.DMA((4,)),
+            sems,
+            sems,
+            sems,
         ],
-        compiler_params=pltpu.CompilerParams(vmem_limit_bytes=12 * 1024 * 1024),
-    )(inner, in_hbm(down_w))
+        compiler_params=pltpu.CompilerParams(vmem_limit_bytes=32 * 1024 * 1024),
+    )(near, other, in_hbm(gate_w), in_hbm(up_w), in_hbm(down_w))
+    return [out[2 * at : 2 * at + 2] for at in range(DOWN_CUTS)]
 
 
 def on_device(
@@ -383,8 +369,9 @@
     near = near_parts(gather_far(normed), dp_rank, dp_count)
     other = swap(near, 0, 1)
     near, outgoing = lax.optimization_barrier((near, cut_pieces(leaving)))
+    gate_parts = run_dense(near, other, w_gate, dp_count)
     spread = lax.all_to_all(outgoing, "tp", split_axis=0, concat_axis=0, tiled=True)
-    gate = sum_dp(run_dense(near, other, w_gate, dp_count), dp_count)
+    gate = sum_dp(gate_parts, dp_count)
     up = sum_dp(run_dense(near, other, w_up, dp_count), dp_count)
     hidden = (jax.nn.silu(gate) * up).astype(jnp.bfloat16)
     near = []
@@ -393,7 +380,10 @@
         down = jnp.dot(block, w_down, preferred_element_type=jnp.float32).astype(jnp.bfloat16)
         half = down.shape[0] // 2
         near += reduce_core(down[:half], down[half:], 2)
-    near[-1], spread = lax.optimization_barrier((near[-1], spread))
+    stay = resident.shape[0]
+    context_stay = attend(queries[:stay], resident, res_len, new_latent[:stay])
+    near[-1], context_stay = lax.optimization_barrier((near[-1], context_stay))
+    near[0], spread = lax.optimization_barrier((near[0], spread))
     ffn = reduce_parts(near, dp_rank, dp_count, rows_dev)
     middle = (stream.astype(jnp.float32) + ffn).astype(jnp.bfloat16)
     mixed = rms_scale(middle, moe_gain)
@@ -407,21 +397,16 @@
     tail = jnp.pad(jnp.concatenate([high, low], axis=1), ((0, 0), (0, 128 - 2 * experts)))
     width = mixed.shape[1] // CUTS
     pieces = [mixed[:, at * width : (at + 1) * width] for at in range(CUTS)]
-    pieces[0] = jnp.concatenate([pieces[0], tail], axis=1)
+    pieces[-1] = jnp.concatenate([pieces[-1], tail], axis=1)
     homing = sort_pieces(spread, arrival_sources(group_dest))
-    near = []
-    for piece in pieces:
-        blocks = gather_quad(gather_far(piece))
-        blocks[1], homing = lax.optimization_barrier((blocks[1], homing))
-        near.append(jnp.concatenate(blocks, axis=0))
-    state = ()
-    for at in range(CUTS):
-        state = run_up(at, near[at], swap(near[at], 0, 1), expert_gate, expert_up, state, width, experts)
+    cuts = [gather_quad(gather_far(piece)) for piece in pieces]
+    cuts[0][-1], homing = lax.optimization_barrier((cuts[0][-1], homing))
+    near = jnp.concatenate([jnp.concatenate(row, axis=1) for row in zip(*cuts)], axis=0)
+    halves = run_expert(near, swap(near, 0, 1), expert_gate, expert_up, expert_down, experts)
     out = []
     width = mixed.shape[1] // DOWN_CUTS
-    sums = [reduce_core(*run_down(at, state, expert_down, width), 2 * dp_count) for at in range(DOWN_CUTS)]
+    sums = [reduce_core(*half, 2 * dp_count) for half in halves]
     home = lax.all_to_all(homing, "tp", split_axis=0, concat_axis=0, tiled=True)
-    sums[-1][0], home = lax.optimization_barrier((sums[-1][0], home))
     arrived = join_pieces(home, leaving.shape)
     for at in range(DOWN_CUTS):
         routed = reduce_rows(sums[at], rows_dev)
@@ -430,8 +415,6 @@
     source = arrival_sources(group_dest)
     mine = lax.dynamic_slice_in_dim(source, tp_rank * moving, moving, 0)
     arrived_len = jnp.take(group_len.reshape(-1), mine, axis=0, mode="clip")
-    stay = resident.shape[0]
-    context_stay = attend(queries[:stay], resident, res_len, new_latent[:stay])
     context_moved = attend(queries[stay:], arrived[:, 0], arrived_len, new_latent[stay:])
     context = jnp.concatenate([context_stay, context_moved], axis=0)
 

time: 212 us -> 200 us (0.943)
  waiting for transfers between devices: 78.6 us -> 59.9 us
  starting transfers between devices: 63.5 us -> 68.3 us
  matrix products: 10.3 us -> 14.3 us
    ppermute x39 -> x45, waiting for transfers between devices: 68.1 us -> 49.4 us  [swap(): return lax.ppermute(block, AXES, pairs)]
    ppermute x39 -> x45, starting transfers between devices: 52.6 us -> 57.1 us  [swap(): return lax.ppermute(block, AXES, pairs)]
    dot_general x2, matrix products: 1.07 us -> 4.08 us  [attend(): jnp.einsum('rhl,rcl->rhc', queries, keys, preferred_element_type=jnp.floa...]
    concatenate x1, other arithmetic: 1.43 us -> 4.12 us  [on_device(): jnp.concatenate([jnp.concatenate(row, axis=1) for row in zip(*cuts)], axi...]
    unnamed x48 -> x44, local copies, waits for them, and re-layouts: 4.54 us -> 3.4 us
    pallas_call x3 -> x1, Pallas kernels: 22.9 us -> 22.3 us  [run_expert(): pl.pallas_call(functools.partial(expert_kernel, DOWN_CUTS, experts), out_...]
  transfers between devices with their start and end apart: 41 -> 47, of which waited for: 20 -> 21; matrix products, arithmetic and copies ran while one was open for 11% -> 15% of each run, Pallas kernels for 13% -> 14%
where the time goes in v3:
time: 200 us
  starting transfers between devices  68.3 us (34%)
  waiting for transfers between devices  59.9 us (30%)
  Pallas kernels  33.1 us (17%)
  matrix products  14.3 us (7%)
  other arithmetic  13.3 us (7%)
  local copies, waits for them, and re-layouts  9.62 us (5%)
    ppermute x45, starting transfers between devices, swap(): return lax.ppermute(block, AXES, pairs)  57.1 us
    ppermute x45, waiting for transfers between devices, swap(): return lax.ppermute(block, AXES, pairs)  49.4 us
    pallas_call x1, Pallas kernels, run_expert(): pl.pallas_call(functools.partial(expert_kernel, DOWN_CUTS, experts), out_...  22.3 us
    pallas_call x2, Pallas kernels, run_dense(): pl.pallas_call(functools.partial(dense_kernel, groups), out_shape=(jax.Sh...  10.8 us
    all_to_all x1, waiting for transfers between devices, on_device(): lax.all_to_all(outgoing, 'tp', split_axis=0, concat_axis=0, tiled=True)  10.4 us
    dot_general x2, matrix products, on_device(): jnp.dot(block, w_down, preferred_element_type=jnp.float32)  6.8 us
    all_to_all x1, starting transfers between devices, on_device(): home = lax.all_to_all(homing, 'tp', split_axis=0, concat_axis=0, tiled=True)  5.95 us
    all_to_all x1, starting transfers between devices, on_device(): lax.all_to_all(outgoing, 'tp', split_axis=0, concat_axis=0, tiled=True)  5.17 us
  transfers between devices with their start and end apart: 47, of which 21 were waited for; matrix products, arithmetic and copies ran while one was open for 15% of the time, Pallas kernels for 14%

profile of v3, /device:TPU:0, one launch (start us, length us, event | category | flops | bytes accessed | tf_op | source)
XLA Modules:
  0.0 199.6 jit_solution(12488475126240238698)
XLA Ops:
  2.7 3.1 %collective-permute-start = (bf16[8,7168]{1,0:T(8,128)(2,1)S(1)}, bf16[8,7168]{1,0:T(8,128)(2,1)S(1)}, u32[]{:S(2)}, u32[]{:S(2)}) collective-permute-start(bf16[8,7168]{1,0:T(8,128)(2,1)S(1)} %fusion.23), channel_id=1, source_target_pairs={{0,4},{1,5},{2,6},{3,7},{4,0},{5,1},{6,2},{7,3},{8,12},{9,13},{10,... | collective-permute-start | bytes 344072 | tf_op jit(solution)/shard_map/ppermute | solution.py:64
  5.8 2.6 %collective-permute-start.1 = (bf16[8,7168]{1,0:T(8,128)(2,1)S(1)}, bf16[8,7168]{1,0:T(8,128)(2,1)S(1)}, u32[]{:S(2)}, u32[]{:S(2)}) collective-permute-start(bf16[8,7168]{1,0:T(8,128)(2,1)S(1)} %fusion.23), channel_id=1, source_target_pairs={{0,8},{1,9},{2,10},{3,11},{4,12},{5,13},{6,14},{7,15},{8,0},{9,1},... | collective-permute-start | bytes 344072 | tf_op jit(solution)/shard_map/ppermute | solution.py:64
  10.8 2.5 %fusion.66 = (f32[6,128]{1,0:T(8,128)S(1)}, f32[6,128,256]{2,1,0:T(8,128)S(1)}) fusion(bf16[8,128,576]{1,2,0:T(8,128)(2,1)} %param.18, bf16[6,256,576]{1,2,0:T(8,128)(2,1)} %param.20, pred[6,256]{1,0:T(8,128)(4,1)S(1)} %iota_compare_fusion.2), kind=kOutput, calls=%fused_computation.143 | convolution fusion | flops 227081472 | bytes 3740160 | tf_op jit(solution)/shard_map/rhl,rcl->rhc/dot_general | solution.py:35
  14.1 3.4 %collective-permute-done.1 = bf16[8,7168]{1,0:T(8,128)(2,1)S(1)} collective-permute-done((bf16[8,7168]{1,0:T(8,128)(2,1)S(1)}, bf16[8,7168]{1,0:T(8,128)(2,1)S(1)}, u32[]{:S(2)}, u32[]{:S(2)}) %collective-permute-start.1) | collective-permute-done | bytes 114720 | tf_op jit(solution)/shard_map/ppermute | solution.py:64
  21.3 8.8 %collective-permute-done.3 = bf16[32,3584]{1,0:T(8,128)(2,1)S(1)} collective-permute-done((bf16[32,3584]{1,0:T(8,128)(2,1)S(1)}, bf16[32,3584]{1,0:T(8,128)(2,1)S(1)}, u32[]{:S(2)}, u32[]{:S(2)}) %collective-permute-start.3) | collective-permute-done | bytes 229408 | tf_op jit(solution)/shard_map/ppermute | solution.py:64
  32.7 5.4 %shard_map.193 = (f32[128,1152]{1,0:T(8,128)S(1)}, bf16[128,1152]{1,0:T(8,128)(2,1)S(1)}) custom-call(bf16[128,3584]{1,0:T(8,128)(2,1)S(1)} %pad_maximum_fusion.2.near_ref, bf16[128,3584]{1,0:T(8,128)(2,1)S(1)} %collective-permute-done.6.other_ref, bf16[3584,1152]{1,0:T(8,128)(2,1)} %hbm.2), custom_call_target="tpu_custom_call" | custom-call | tf_op jit(solution)/shard_map/pallas_call | solution.py:221
  39.7 5.4 %shard_map.194 = (f32[128,1152]{1,0:T(8,128)S(1)}, bf16[128,1152]{1,0:T(8,128)(2,1)S(1)}) custom-call(bf16[128,3584]{1,0:T(8,128)(2,1)S(1)} %pad_maximum_fusion.2.near_ref, bf16[128,3584]{1,0:T(8,128)(2,1)S(1)} %collective-permute-done.6.other_ref, bf16[3584,1152]{1,0:T(8,128)(2,1)} %hbm.3), custom_call_target="tpu_custom_call" | custom-call | tf_op jit(solution)/shard_map/pallas_call | solution.py:221
  48.4 5.2 %all-to-all-start = ((bf16[16,2,72,256]{3,2,1,0:T(8,128)(2,1)}), bf16[16,2,72,256]{3,2,1,0:T(8,128)(2,1)S(1)}, u32[]{:S(2)}, u32[]{:S(2)}) async-start(bf16[16,2,72,256]{3,2,1,0:T(8,128)(2,1)} %copy.56), calls=%async_computation | async-start | bytes 2359296 | tf_op jit(solution)/shard_map/all_to_all | solution.py:373
  55.4 5.4 %convolution_convert_fusion = bf16[128,3584]{1,0:T(8,128)(2,1)S(1)} fusion(bf16[128,1152]{1,0:T(8,128)(2,1)S(1)} %multiply_convert_fusion, bf16[1152,3584]{1,0:T(8,128)(2,1)} %param.29), kind=kOutput, calls=%fused_computation.2 | convolution fusion | flops 1057423360 | bytes 9469952 | tf_op jit(solution)/shard_map/dot_general | solution.py:380
  61.1 2.1 %collective-permute-done.9 = bf16[128,1152]{1,0:T(8,128)(2,1)S(1)} collective-permute-done((bf16[128,1152]{1,0:T(8,128)(2,1)S(1)}, bf16[128,1152]{1,0:T(8,128)(2,1)S(1)}, u32[]{:S(2)}, u32[]{:S(2)}) %collective-permute-start.9) | collective-permute-done | bytes 294944 | tf_op jit(solution)/shard_map/ppermute | solution.py:64
  64.9 1.7 collective-permute-start.12
  70.3 10.4 %all-to-all-done = bf16[16,2,72,256]{3,2,1,0:T(8,128)(2,1)S(1)} async-done(((bf16[16,2,72,256]{3,2,1,0:T(8,128)(2,1)}), bf16[16,2,72,256]{3,2,1,0:T(8,128)(2,1)S(1)}, u32[]{:S(2)}, u32[]{:S(2)}) %all-to-all-start) | async-done | bytes 1179680 | tf_op jit(solution)/shard_map/all_to_all | solution.py:373
  81.5 1.7 collective-permute-done.14
  83.4 1.7 collective-permute-start.15
  89.5 7.2 %collective-permute-done.16 = bf16[8,7168]{1,0:T(8,128)(2,1)S(1)} collective-permute-done((bf16[8,7168]{1,0:T(8,128)(2,1)S(1)}, bf16[8,7168]{1,0:T(8,128)(2,1)S(1)}, u32[]{:S(2)}, u32[]{:S(2)}) %collective-permute-start.16) | collective-permute-done | bytes 114720 | tf_op jit(solution)/shard_map/ppermute | solution.py:64
  97.0 2.1 %collective-permute-start.18 = (bf16[8,3584]{1,0:T(8,128)(2,1)S(1)}, bf16[8,3584]{1,0:T(8,128)(2,1)S(1)}, u32[]{:S(2)}, u32[]{:S(2)}) collective-permute-start(bf16[8,3584]{1,0:T(8,128)(2,1)S(1)} %get-tuple-element.83), channel_id=1, source_target_pairs={{0,4},{1,5},{2,6},{3,7},{4,0},{5,1},{6,2},{7,3},{8,12},{9,13},{10,... | collective-permute-start | bytes 172040 | tf_op jit(solution)/shard_map/ppermute | solution.py:64
  102.7 2.1 %collective-permute-start.23 = (bf16[8,3712]{1,0:T(8,128)(2,1)S(1)}, bf16[8,3712]{1,0:T(8,128)(2,1)S(1)}, u32[]{:S(2)}, u32[]{:S(2)}) collective-permute-start(bf16[8,3712]{1,0:T(8,128)(2,1)S(1)} %get-tuple-element.85), channel_id=1, source_target_pairs={{0,8},{1,9},{2,10},{3,11},{4,12},{5,13},{6,14},{7,15},{8,0},{9,1},... | collective-permute-start | bytes 178184 | tf_op jit(solution)/shard_map/ppermute | solution.py:64
  107.3 2.4 %collective-permute-start.21 = (bf16[32,3584]{1,0:T(8,128)(2,1)S(1)}, bf16[32,3584]{1,0:T(8,128)(2,1)S(1)}, u32[]{:S(2)}, u32[]{:S(2)}) collective-permute-start(bf16[32,3584]{1,0:T(8,128)(2,1)S(1)} %maximum_bitcast_fusion.2), channel_id=1, source_target_pairs={{0,18},{1,19},{2,16},{3,17},{4,22},{5,23},{6,20},{7,21},{8,26},{9,... | collective-permute-start | bytes 688136 | tf_op jit(solution)/shard_map/ppermute | solution.py:64
  113.8 3.0 %collective-permute-done.21 = bf16[32,3584]{1,0:T(8,128)(2,1)S(1)} collective-permute-done((bf16[32,3584]{1,0:T(8,128)(2,1)S(1)}, bf16[32,3584]{1,0:T(8,128)(2,1)S(1)}, u32[]{:S(2)}, u32[]{:S(2)}) %collective-permute-start.21) | collective-permute-done | bytes 229408 | tf_op jit(solution)/shard_map/ppermute | solution.py:64
  116.8 2.3 %collective-permute-start.29 = (bf16[32,3712]{1,0:T(8,128)(2,1)S(1)}, bf16[32,3712]{1,0:T(8,128)(2,1)}, u32[]{:S(2)}, u32[]{:S(2)}) collective-permute-start(bf16[32,3712]{1,0:T(8,128)(2,1)S(1)} %maximum_bitcast_fusion.1), channel_id=1, source_target_pairs={{0,18},{1,19},{2,16},{3,17},{4,22},{5,23},{6,20},{7,21},{8,26},{9,... | collective-permute-start | bytes 712712 | tf_op jit(solution)/shard_map/ppermute | solution.py:64
  120.9 5.9 %all-to-all-start.1 = ((bf16[16,2,72,256]{3,2,1,0:T(8,128)(2,1)}), bf16[16,2,72,256]{3,2,1,0:T(8,128)(2,1)}, u32[]{:S(2)}, u32[]{:S(2)}) async-start(bf16[16,2,72,256]{3,2,1,0:T(8,128)(2,1)} %bitcast.16), calls=%async_computation.1 | async-start | bytes 2359296 | tf_op jit(solution)/shard_map/all_to_all | solution.py:409
  128.7 4.1 %maximum_maximum_fusion.refs_0_ = bf16[128,7296]{1,0:T(8,128)(2,1)S(1)} fusion(bf16[32,3712]{1,0:T(8,128)(2,1)} %collective-permute-done.29, bf16[32,3584]{1,0:T(8,128)(2,1)} %copy-done.8, bf16[32,3712]{1,0:T(8,128)(2,1)} %copy-done.7, bf16[32,3584]{1,0:T(8,128)(2,1)} %copy-done.10, bf16[32,3712]{1,0:T(8,128)(2,1)} %collective-permute-done.26, ...), kind=kLoop, calls=%fused_computation.4 | loop fusion | flops 14942208 | bytes 3735552 | tf_op jit(solution)/shard_map/concatenate | solution.py:404
  135.1 1.8 collective-permute-done.30.refs_1_
  136.9 22.3 %shard_map.195 = (bf16[128,3584]{1,0:T(8,128)(2,1)S(1)}, bf16[128,3584]{1,0:T(8,128)(2,1)}, bf16[128,3584]{1,0:T(8,128)(2,1)S(1)}, bf16[128,3584]{1,0:T(8,128)(2,1)}) custom-call(bf16[128,7296]{1,0:T(8,128)(2,1)S(1)} %maximum_maximum_fusion.refs_0_, bf16[128,7296]{1,0:T(8,128)(2,1)} %collective-permute-done.30.refs_1_, bf16[1,7168,1024]{2,1,0:T(8,128)(2,1)} %refs_2_.1, ...), custom_call_target="tpu_custom_call" | custom-call | tf_op jit(solution)/shard_map/pallas_call | solution.py:317
  167.0 1.7 collective-permute-start.41
  170.7 3.7 %collective-permute-done.39 = bf16[32,3584]{1,0:T(8,128)(2,1)S(1)} collective-permute-done((bf16[32,3584]{1,0:T(8,128)(2,1)S(1)}, bf16[32,3584]{1,0:T(8,128)(2,1)S(1)}, u32[]{:S(2)}, u32[]{:S(2)}) %collective-permute-start.39) | collective-permute-done | bytes 229408 | tf_op jit(solution)/shard_map/ppermute | solution.py:64
  175.1 5.0 %collective-permute-done.41 = bf16[32,3584]{1,0:T(8,128)(2,1)S(1)} collective-permute-done((bf16[32,3584]{1,0:T(8,128)(2,1)S(1)}, bf16[32,3584]{1,0:T(8,128)(2,1)S(1)}, u32[]{:S(2)}, u32[]{:S(2)}) %collective-permute-start.41) | collective-permute-done | bytes 229408 | tf_op jit(solution)/shard_map/ppermute | solution.py:64
  181.8 2.4 %collective-permute-start.43 = (bf16[8,3584]{1,0:T(8,128)(2,1)S(1)}, bf16[8,3584]{1,0:T(8,128)(2,1)S(1)}, u32[]{:S(2)}, u32[]{:S(2)}) collective-permute-start(bf16[8,3584]{1,0:T(8,128)(2,1)S(1)} %get-tuple-element.78), channel_id=1, source_target_pairs={{0,8},{1,9},{2,10},{3,11},{4,12},{5,13},{6,14},{7,15},{8,0},{9,1},... | collective-permute-start | bytes 172040 | tf_op jit(solution)/shard_map/ppermute | solution.py:64
  184.2 1.8 collective-permute-start.44
  186.0 2.8 %collective-permute-done.34 = bf16[32,3584]{1,0:T(8,128)(2,1)S(1)} collective-permute-done((bf16[32,3584]{1,0:T(8,128)(2,1)S(1)}, bf16[32,3584]{1,0:T(8,128)(2,1)S(1)}, u32[]{:S(2)}, u32[]{:S(2)}) %collective-permute-start.34) | collective-permute-done | bytes 229408 | tf_op jit(solution)/shard_map/ppermute | solution.py:64
  190.5 2.4 %collective-permute-start.36 = (bf16[8,3584]{1,0:T(8,128)(2,1)S(1)}, bf16[8,3584]{1,0:T(8,128)(2,1)S(1)}, u32[]{:S(2)}, u32[]{:S(2)}) collective-permute-start(bf16[8,3584]{1,0:T(8,128)(2,1)S(1)} %get-tuple-element.75), channel_id=1, source_target_pairs={{0,8},{1,9},{2,10},{3,11},{4,12},{5,13},{6,14},{7,15},{8,0},{9,1},... | collective-permute-start | bytes 172040 | tf_op jit(solution)/shard_map/ppermute | solution.py:64
  196.4 2.4 %collective-permute-done.37 = bf16[8,3584]{1,0:T(8,128)(2,1)S(1)} collective-permute-done((bf16[8,3584]{1,0:T(8,128)(2,1)S(1)}, bf16[8,3584]{1,0:T(8,128)(2,1)S(1)}, u32[]{:S(2)}, u32[]{:S(2)}) %collective-permute-start.37) | collective-permute-done | bytes 57376 | tf_op jit(solution)/shard_map/ppermute | solution.py:64
  (186 shorter events, 63.6 us)
Async XLA Ops:
  2.7 11.4 %collective-permute-start = (bf16[8,7168]{1,0:T(8,128)(2,1)S(1)}, bf16[8,7168]{1,0:T(8,128)(2,1)S(1)}, u32[]{:S(2)}, u32[]{:S(2)}) collective-permute-start(bf16[8,7168]{1,0:T(8,128)(2,1)S(1)} %fusion.23), channel_id=1, source_target_pairs={{0,4},{1,5},{2,6},{3,7},{4,0},{5,1},{6,2},{7,3},{8,12},{9,13},{10,... | collective-permute-start | bytes 344072 | tf_op jit(solution)/shard_map/ppermute | solution.py:64
  5.8 11.7 %collective-permute-start.1 = (bf16[8,7168]{1,0:T(8,128)(2,1)S(1)}, bf16[8,7168]{1,0:T(8,128)(2,1)S(1)}, u32[]{:S(2)}, u32[]{:S(2)}) collective-permute-start(bf16[8,7168]{1,0:T(8,128)(2,1)S(1)} %fusion.23), channel_id=1, source_target_pairs={{0,8},{1,9},{2,10},{3,11},{4,12},{5,13},{6,14},{7,15},{8,0},{9,1},... | collective-permute-start | bytes 344072 | tf_op jit(solution)/shard_map/ppermute | solution.py:64
  8.4 9.1 %collective-permute-start.2 = (bf16[8,7168]{1,0:T(8,128)(2,1)S(1)}, bf16[8,7168]{1,0:T(8,128)(2,1)S(1)}, u32[]{:S(2)}, u32[]{:S(2)}) collective-permute-start(bf16[8,7168]{1,0:T(8,128)(2,1)S(1)} %fusion.23), channel_id=1, source_target_pairs={{0,12},{1,13},{2,14},{3,15},{4,8},{5,9},{6,10},{7,11},{8,4},{9,5},... | collective-permute-start | bytes 344072 | tf_op jit(solution)/shard_map/ppermute | solution.py:64
  17.6 12.5 %collective-permute-start.4 = (bf16[32,3584]{1,0:T(8,128)(2,1)S(1)}, bf16[32,3584]{1,0:T(8,128)(2,1)S(1)}, u32[]{:S(2)}, u32[]{:S(2)}) collective-permute-start(bf16[32,3584]{1,0:T(8,128)(2,1)S(1)} %get-tuple-element.72), channel_id=1, source_target_pairs={{0,16},{1,17},{2,18},{3,19},{4,20},{5,21},{6,22},{7,23},{8,24},{9,... | collective-permute-start | bytes 688136 | tf_op jit(solution)/shard_map/ppermute | solution.py:64
  19.2 10.9 %collective-permute-start.5 = (bf16[32,3584]{1,0:T(8,128)(2,1)S(1)}, bf16[32,3584]{1,0:T(8,128)(2,1)S(1)}, u32[]{:S(2)}, u32[]{:S(2)}) collective-permute-start(bf16[32,3584]{1,0:T(8,128)(2,1)S(1)} %get-tuple-element.72), channel_id=1, source_target_pairs={{0,18},{1,19},{2,16},{3,17},{4,22},{5,23},{6,20},{7,21},{8,26},{9,... | collective-permute-start | bytes 688136 | tf_op jit(solution)/shard_map/ppermute | solution.py:64
  20.7 9.4 %collective-permute-start.3 = (bf16[32,3584]{1,0:T(8,128)(2,1)S(1)}, bf16[32,3584]{1,0:T(8,128)(2,1)S(1)}, u32[]{:S(2)}, u32[]{:S(2)}) collective-permute-start(bf16[32,3584]{1,0:T(8,128)(2,1)S(1)} %get-tuple-element.71), channel_id=1, source_target_pairs={{0,2},{1,3},{2,0},{3,1},{4,6},{5,7},{6,4},{7,5},{8,10},{9,11},{10,... | collective-permute-start | bytes 688136 | tf_op jit(solution)/shard_map/ppermute | solution.py:64
  38.1 15.4 %collective-permute-start.7 = (bf16[128,1152]{1,0:T(8,128)(2,1)S(1)}, bf16[128,1152]{1,0:T(8,128)(2,1)S(1)}, u32[]{:S(2)}, u32[]{:S(2)}) collective-permute-start(bf16[128,1152]{1,0:T(8,128)(2,1)S(1)} %get-tuple-element.21), channel_id=1, source_target_pairs={{0,16},{1,17},{2,18},{3,19},{4,20},{5,21},{6,22},{7,23},{8,24},{9,... | collective-permute-start | bytes 884744 | tf_op jit(solution)/shard_map/ppermute | solution.py:64
  45.1 8.8 %collective-permute-start.8 = (bf16[128,1152]{1,0:T(8,128)(2,1)S(1)}, bf16[128,1152]{1,0:T(8,128)(2,1)S(1)}, u32[]{:S(2)}, u32[]{:S(2)}) collective-permute-start(bf16[128,1152]{1,0:T(8,128)(2,1)S(1)} %get-tuple-element.23), channel_id=1, source_target_pairs={{0,16},{1,17},{2,18},{3,19},{4,20},{5,21},{6,22},{7,23},{8,24},{9,... | collective-permute-start | bytes 884744 | tf_op jit(solution)/shard_map/ppermute | solution.py:64
  48.4 32.3 %all-to-all-start = ((bf16[16,2,72,256]{3,2,1,0:T(8,128)(2,1)}), bf16[16,2,72,256]{3,2,1,0:T(8,128)(2,1)S(1)}, u32[]{:S(2)}, u32[]{:S(2)}) async-start(bf16[16,2,72,256]{3,2,1,0:T(8,128)(2,1)} %copy.56), calls=%async_computation | async-start | bytes 2359296 | tf_op jit(solution)/shard_map/all_to_all | solution.py:373
  54.2 9.1 %collective-permute-start.9 = (bf16[128,1152]{1,0:T(8,128)(2,1)S(1)}, bf16[128,1152]{1,0:T(8,128)(2,1)S(1)}, u32[]{:S(2)}, u32[]{:S(2)}) collective-permute-start(bf16[128,1152]{1,0:T(8,128)(2,1)S(1)} %multiply_convert_fusion), channel_id=1, source_target_pairs={{0,16},{1,17},{2,18},{3,19},{4,20},{5,21},{6,22},{7,23},{8,24},{9,... | collective-permute-start | bytes 884744 | tf_op jit(solution)/shard_map/ppermute | solution.py:64
  64.9 16.6 %collective-permute-start.12 = (bf16[32,3584]{1,0:T(8,128)(2,1)S(1)}, bf16[32,3584]{1,0:T(8,128)(2,1)S(1)}, u32[]{:S(2)}, u32[]{:S(2)}) collective-permute-start(bf16[32,3584]{1,0:T(8,128)(2,1)S(1)} %get-tuple-element.64), channel_id=1, source_target_pairs={{0,2},{1,3},{2,0},{3,1},{4,6},{5,7},{6,4},{7,5},{8,10},{9,11},{10,... | collective-permute-start | bytes 688136 | tf_op jit(solution)/shard_map/ppermute | solution.py:64
  66.7 14.8 %collective-permute-start.13 = (bf16[32,3584]{1,0:T(8,128)(2,1)S(1)}, bf16[32,3584]{1,0:T(8,128)(2,1)S(1)}, u32[]{:S(2)}, u32[]{:S(2)}) collective-permute-start(bf16[32,3584]{1,0:T(8,128)(2,1)S(1)} %add_convert_fusion.7), channel_id=1, source_target_pairs={{0,16},{1,17},{2,18},{3,19},{4,20},{5,21},{6,22},{7,23},{8,24},{9,... | collective-permute-start | bytes 688136 | tf_op jit(solution)/shard_map/ppermute | solution.py:64
  68.3 14.9 %collective-permute-start.14 = (bf16[32,3584]{1,0:T(8,128)(2,1)S(1)}, bf16[32,3584]{1,0:T(8,128)(2,1)S(1)}, u32[]{:S(2)}, u32[]{:S(2)}) collective-permute-start(bf16[32,3584]{1,0:T(8,128)(2,1)S(1)} %convert_add_fusion.5), channel_id=1, source_target_pairs={{0,18},{1,19},{2,16},{3,17},{4,22},{5,23},{6,20},{7,21},{8,26},{9,... | collective-permute-start | bytes 688136 | tf_op jit(solution)/shard_map/ppermute | solution.py:64
  85.1 11.5 %collective-permute-start.16 = (bf16[8,7168]{1,0:T(8,128)(2,1)S(1)}, bf16[8,7168]{1,0:T(8,128)(2,1)S(1)}, u32[]{:S(2)}, u32[]{:S(2)}) collective-permute-start(bf16[8,7168]{1,0:T(8,128)(2,1)S(1)} %get-tuple-element.70), channel_id=1, source_target_pairs={{0,8},{1,9},{2,10},{3,11},{4,12},{5,13},{6,14},{7,15},{8,0},{9,1},... | collective-permute-start | bytes 344072 | tf_op jit(solution)/shard_map/ppermute | solution.py:64
  86.5 10.2 %collective-permute-start.17 = (bf16[8,7168]{1,0:T(8,128)(2,1)S(1)}, bf16[8,7168]{1,0:T(8,128)(2,1)S(1)}, u32[]{:S(2)}, u32[]{:S(2)}) collective-permute-start(bf16[8,7168]{1,0:T(8,128)(2,1)S(1)} %get-tuple-element.69), channel_id=1, source_target_pairs={{0,12},{1,13},{2,14},{3,15},{4,8},{5,9},{6,10},{7,11},{8,4},{9,5},... | collective-permute-start | bytes 344072 | tf_op jit(solution)/shard_map/ppermute | solution.py:64
  101.7 8.8 %collective-permute-start.22 = (bf16[8,3712]{1,0:T(8,128)(2,1)S(1)}, bf16[8,3712]{1,0:T(8,128)(2,1)S(1)}, u32[]{:S(2)}, u32[]{:S(2)}) collective-permute-start(bf16[8,3712]{1,0:T(8,128)(2,1)S(1)} %get-tuple-element.85), channel_id=1, source_target_pairs={{0,4},{1,5},{2,6},{3,7},{4,0},{5,1},{6,2},{7,3},{8,12},{9,13},{10,... | collective-permute-start | bytes 178184 | tf_op jit(solution)/shard_map/ppermute | solution.py:64
  102.7 8.6 %collective-permute-start.23 = (bf16[8,3712]{1,0:T(8,128)(2,1)S(1)}, bf16[8,3712]{1,0:T(8,128)(2,1)S(1)}, u32[]{:S(2)}, u32[]{:S(2)}) collective-permute-start(bf16[8,3712]{1,0:T(8,128)(2,1)S(1)} %get-tuple-element.85), channel_id=1, source_target_pairs={{0,8},{1,9},{2,10},{3,11},{4,12},{5,13},{6,14},{7,15},{8,0},{9,1},... | collective-permute-start | bytes 178184 | tf_op jit(solution)/shard_map/ppermute | solution.py:64
  107.3 9.5 %collective-permute-start.21 = (bf16[32,3584]{1,0:T(8,128)(2,1)S(1)}, bf16[32,3584]{1,0:T(8,128)(2,1)S(1)}, u32[]{:S(2)}, u32[]{:S(2)}) collective-permute-start(bf16[32,3584]{1,0:T(8,128)(2,1)S(1)} %maximum_bitcast_fusion.2), channel_id=1, source_target_pairs={{0,18},{1,19},{2,16},{3,17},{4,22},{5,23},{6,20},{7,21},{8,26},{9,... | collective-permute-start | bytes 688136 | tf_op jit(solution)/shard_map/ppermute | solution.py:64
  109.7 17.2 %collective-permute-start.25 = (bf16[32,3584]{1,0:T(8,128)(2,1)S(1)}, bf16[32,3584]{1,0:T(8,128)(2,1)S(1)}, u32[]{:S(2)}, u32[]{:S(2)}) collective-permute-start(bf16[32,3584]{1,0:T(8,128)(2,1)S(1)} %maximum_bitcast_fusion.2), channel_id=1, source_target_pairs={{0,2},{1,3},{2,0},{3,1},{4,6},{5,7},{6,4},{7,5},{8,10},{9,11},{10,... | collective-permute-start | bytes 688136 | tf_op jit(solution)/shard_map/ppermute | solution.py:64
  110.6 16.3 %collective-permute-start.27 = (bf16[32,3584]{1,0:T(8,128)(2,1)S(1)}, bf16[32,3584]{1,0:T(8,128)(2,1)S(1)}, u32[]{:S(2)}, u32[]{:S(2)}) collective-permute-start(bf16[32,3584]{1,0:T(8,128)(2,1)S(1)} %maximum_bitcast_fusion.2), channel_id=1, source_target_pairs={{0,16},{1,17},{2,18},{3,19},{4,20},{5,21},{6,22},{7,23},{8,24},{9,... | collective-permute-start | bytes 688136 | tf_op jit(solution)/shard_map/ppermute | solution.py:64
  111.4 15.5 %collective-permute-start.26 = (bf16[32,3712]{1,0:T(8,128)(2,1)S(1)}, bf16[32,3712]{1,0:T(8,128)(2,1)}, u32[]{:S(2)}, u32[]{:S(2)}) collective-permute-start(bf16[32,3712]{1,0:T(8,128)(2,1)S(1)} %maximum_bitcast_fusion.1), channel_id=1, source_target_pairs={{0,2},{1,3},{2,0},{3,1},{4,6},{5,7},{6,4},{7,5},{8,10},{9,11},{10,... | collective-permute-start | bytes 712712 | tf_op jit(solution)/shard_map/ppermute | solution.py:64
  112.4 14.5 %collective-permute-start.28 = (bf16[32,3712]{1,0:T(8,128)(2,1)S(1)}, bf16[32,3712]{1,0:T(8,128)(2,1)S(1)}, u32[]{:S(2)}, u32[]{:S(2)}) collective-permute-start(bf16[32,3712]{1,0:T(8,128)(2,1)S(1)} %maximum_bitcast_fusion.1), channel_id=1, source_target_pairs={{0,16},{1,17},{2,18},{3,19},{4,20},{5,21},{6,22},{7,23},{8,24},{9,... | collective-permute-start | bytes 712712 | tf_op jit(solution)/shard_map/ppermute | solution.py:64
  116.8 11.9 %collective-permute-start.29 = (bf16[32,3712]{1,0:T(8,128)(2,1)S(1)}, bf16[32,3712]{1,0:T(8,128)(2,1)}, u32[]{:S(2)}, u32[]{:S(2)}) collective-permute-start(bf16[32,3712]{1,0:T(8,128)(2,1)S(1)} %maximum_bitcast_fusion.1), channel_id=1, source_target_pairs={{0,18},{1,19},{2,16},{3,17},{4,22},{5,23},{6,20},{7,21},{8,26},{9,... | collective-permute-start | bytes 712712 | tf_op jit(solution)/shard_map/ppermute | solution.py:64
  120.9 39.8 %all-to-all-start.1 = ((bf16[16,2,72,256]{3,2,1,0:T(8,128)(2,1)}), bf16[16,2,72,256]{3,2,1,0:T(8,128)(2,1)}, u32[]{:S(2)}, u32[]{:S(2)}) async-start(bf16[16,2,72,256]{3,2,1,0:T(8,128)(2,1)} %bitcast.16), calls=%async_computation.1 | async-start | bytes 2359296 | tf_op jit(solution)/shard_map/all_to_all | solution.py:409
  165.1 9.3 %collective-permute-start.39 = (bf16[32,3584]{1,0:T(8,128)(2,1)S(1)}, bf16[32,3584]{1,0:T(8,128)(2,1)S(1)}, u32[]{:S(2)}, u32[]{:S(2)}) collective-permute-start(bf16[32,3584]{1,0:T(8,128)(2,1)S(1)} %get-tuple-element.61), channel_id=1, source_target_pairs={{0,2},{1,3},{2,0},{3,1},{4,6},{5,7},{6,4},{7,5},{8,10},{9,11},{10,... | collective-permute-start | bytes 688136 | tf_op jit(solution)/shard_map/ppermute | solution.py:64
  167.0 13.1 %collective-permute-start.41 = (bf16[32,3584]{1,0:T(8,128)(2,1)S(1)}, bf16[32,3584]{1,0:T(8,128)(2,1)S(1)}, u32[]{:S(2)}, u32[]{:S(2)}) collective-permute-start(bf16[32,3584]{1,0:T(8,128)(2,1)S(1)} %get-tuple-element.62), channel_id=1, source_target_pairs={{0,18},{1,19},{2,16},{3,17},{4,22},{5,23},{6,20},{7,21},{8,26},{9,... | collective-permute-start | bytes 688136 | tf_op jit(solution)/shard_map/ppermute | solution.py:64
  168.8 15.3 %collective-permute-start.32 = (bf16[32,3584]{1,0:T(8,128)(2,1)S(1)}, bf16[32,3584]{1,0:T(8,128)(2,1)S(1)}, u32[]{:S(2)}, u32[]{:S(2)}) collective-permute-start(bf16[32,3584]{1,0:T(8,128)(2,1)S(1)} %get-tuple-element.58), channel_id=1, source_target_pairs={{0,2},{1,3},{2,0},{3,1},{4,6},{5,7},{6,4},{7,5},{8,10},{9,11},{10,... | collective-permute-start | bytes 688136 | tf_op jit(solution)/shard_map/ppermute | solution.py:64
  170.4 15.6 %collective-permute-start.33 = (bf16[32,3584]{1,0:T(8,128)(2,1)S(1)}, bf16[32,3584]{1,0:T(8,128)(2,1)S(1)}, u32[]{:S(2)}, u32[]{:S(2)}) collective-permute-start(bf16[32,3584]{1,0:T(8,128)(2,1)S(1)} %get-tuple-element.60), channel_id=1, source_target_pairs={{0,16},{1,17},{2,18},{3,19},{4,20},{5,21},{6,22},{7,23},{8,24},{9,... | collective-permute-start | bytes 688136 | tf_op jit(solution)/shard_map/ppermute | solution.py:64
  174.4 14.4 %collective-permute-start.34 = (bf16[32,3584]{1,0:T(8,128)(2,1)S(1)}, bf16[32,3584]{1,0:T(8,128)(2,1)S(1)}, u32[]{:S(2)}, u32[]{:S(2)}) collective-permute-start(bf16[32,3584]{1,0:T(8,128)(2,1)S(1)} %get-tuple-element.59), channel_id=1, source_target_pairs={{0,18},{1,19},{2,16},{3,17},{4,22},{5,23},{6,20},{7,21},{8,26},{9,... | collective-permute-start | bytes 688136 | tf_op jit(solution)/shard_map/ppermute | solution.py:64
  180.3 12.6 %collective-permute-start.42 = (bf16[8,3584]{1,0:T(8,128)(2,1)S(1)}, bf16[8,3584]{1,0:T(8,128)(2,1)S(1)}, u32[]{:S(2)}, u32[]{:S(2)}) collective-permute-start(bf16[8,3584]{1,0:T(8,128)(2,1)S(1)} %get-tuple-element.76), channel_id=1, source_target_pairs={{0,4},{1,5},{2,6},{3,7},{4,0},{5,1},{6,2},{7,3},{8,12},{9,13},{10,... | collective-permute-start | bytes 172040 | tf_op jit(solution)/shard_map/ppermute | solution.py:64
  181.8 13.2 %collective-permute-start.43 = (bf16[8,3584]{1,0:T(8,128)(2,1)S(1)}, bf16[8,3584]{1,0:T(8,128)(2,1)S(1)}, u32[]{:S(2)}, u32[]{:S(2)}) collective-permute-start(bf16[8,3584]{1,0:T(8,128)(2,1)S(1)} %get-tuple-element.78), channel_id=1, source_target_pairs={{0,8},{1,9},{2,10},{3,11},{4,12},{5,13},{6,14},{7,15},{8,0},{9,1},... | collective-permute-start | bytes 172040 | tf_op jit(solution)/shard_map/ppermute | solution.py:64
  184.2 10.8 %collective-permute-start.44 = (bf16[8,3584]{1,0:T(8,128)(2,1)S(1)}, bf16[8,3584]{1,0:T(8,128)(2,1)S(1)}, u32[]{:S(2)}, u32[]{:S(2)}) collective-permute-start(bf16[8,3584]{1,0:T(8,128)(2,1)S(1)} %get-tuple-element.77), channel_id=1, source_target_pairs={{0,12},{1,13},{2,14},{3,15},{4,8},{5,9},{6,10},{7,11},{8,4},{9,5},... | collective-permute-start | bytes 172040 | tf_op jit(solution)/shard_map/ppermute | solution.py:64
  (37 other events, 225.1 us)

commit v4 on v3

--- a/solution.py
+++ b/solution.py
@@ -65,7 +65,8 @@
 
 
 def far_masks():
-    return range(4, lax.axis_size("tp"), 4)
+    masks = list(range(4, lax.axis_size("tp"), 4))
+    return masks[1:] + masks[:1]
 
 
 def quad():
@@ -401,7 +402,8 @@
     homing = sort_pieces(spread, arrival_sources(group_dest))
     cuts = [gather_quad(gather_far(piece)) for piece in pieces]
     cuts[0][-1], homing = lax.optimization_barrier((cuts[0][-1], homing))
-    near = jnp.concatenate([jnp.concatenate(row, axis=1) for row in zip(*cuts)], axis=0)
+    near = [lax.optimization_barrier(jnp.concatenate(row, axis=1)) for row in zip(*cuts)]
+    near = jnp.concatenate(near, axis=0)
     halves = run_expert(near, swap(near, 0, 1), expert_gate, expert_up, expert_down, experts)
     out = []
     width = mixed.shape[1] // DOWN_CUTS

time: 200 us -> 195 us (0.975)
  starting transfers between devices: 68.3 us -> 63.7 us
  other arithmetic: 13.3 us -> 10.7 us
  waiting for transfers between devices: 59.9 us -> 62.3 us
    ppermute x45, starting transfers between devices: 57.1 us -> 53.1 us  [swap(): return lax.ppermute(block, AXES, pairs)]
    concatenate x1 -> x5, other arithmetic: 4.12 us -> 0.26 us  [the longest x4 0.13 us: on_device(): jnp.concatenate(row, axis=1)]
    ppermute x45, waiting for transfers between devices: 49.4 us -> 51.6 us  [swap(): return lax.ppermute(block, AXES, pairs)]
  transfers between devices with their start and end apart: 47 -> 47, of which waited for: 21 -> 19; matrix products, arithmetic and copies ran while one was open for 15% -> 14% of each run, Pallas kernels for 14% -> 14%
where the time goes in v4:
time: 195 us; the launch traced here: 194 us
  starting transfers between devices  63.7 us (33%)
  waiting for transfers between devices  62.3 us (32%)
  Pallas kernels  33.1 us (17%)
  matrix products  13.7 us (7%)
  other arithmetic  10.7 us (5%)
  local copies, waits for them, and re-layouts  9.28 us (5%)
    ppermute x45, starting transfers between devices, swap(): return lax.ppermute(block, AXES, pairs)  53.1 us
    ppermute x45, waiting for transfers between devices, swap(): return lax.ppermute(block, AXES, pairs)  51.6 us
    pallas_call x1, Pallas kernels, run_expert(): pl.pallas_call(functools.partial(expert_kernel, DOWN_CUTS, experts), out_...  22.3 us
    pallas_call x2, Pallas kernels, run_dense(): pl.pallas_call(functools.partial(dense_kernel, groups), out_shape=(jax.Sh...  10.8 us
    all_to_all x1, waiting for transfers between devices, on_device(): lax.all_to_all(outgoing, 'tp', split_axis=0, concat_axis=0, tiled=True)  10.7 us
    dot_general x2, matrix products, on_device(): jnp.dot(block, w_down, preferred_element_type=jnp.float32)  6.75 us
    all_to_all x1, starting transfers between devices, on_device(): lax.all_to_all(outgoing, 'tp', split_axis=0, concat_axis=0, tiled=True)  6.17 us
    all_to_all x1, starting transfers between devices, on_device(): home = lax.all_to_all(homing, 'tp', split_axis=0, concat_axis=0, tiled=True)  4.43 us
  transfers between devices with their start and end apart: 47, of which 19 were waited for; matrix products, arithmetic and copies ran while one was open for 14% of the time, Pallas kernels for 14%

profile of v4, /device:TPU:0, one launch (start us, length us, event | category | flops | bytes accessed | tf_op | source)
XLA Modules:
  0.0 194.0 jit_solution(248997270406930984)
XLA Ops:
  2.7 4.1 %collective-permute-start = (bf16[8,7168]{1,0:T(8,128)(2,1)S(1)}, bf16[8,7168]{1,0:T(8,128)(2,1)S(1)}, u32[]{:S(2)}, u32[]{:S(2)}) collective-permute-start(bf16[8,7168]{1,0:T(8,128)(2,1)S(1)} %fusion.23), channel_id=1, source_target_pairs={{0,8},{1,9},{2,10},{3,11},{4,12},{5,13},{6,14},{7,15},{8,0},{9,1},... | collective-permute-start | bytes 344072 | tf_op jit(solution)/shard_map/ppermute | solution.py:64
  20.1 10.2 %collective-permute-done.3 = bf16[32,3584]{1,0:T(8,128)(2,1)S(1)} collective-permute-done((bf16[32,3584]{1,0:T(8,128)(2,1)S(1)}, bf16[32,3584]{1,0:T(8,128)(2,1)S(1)}, u32[]{:S(2)}, u32[]{:S(2)}) %collective-permute-start.3) | collective-permute-done | bytes 229408 | tf_op jit(solution)/shard_map/ppermute | solution.py:64
  32.9 5.4 %shard_map.193 = (f32[128,1152]{1,0:T(8,128)S(1)}, bf16[128,1152]{1,0:T(8,128)(2,1)S(1)}) custom-call(bf16[128,3584]{1,0:T(8,128)(2,1)S(1)} %pad_maximum_fusion.3.near_ref, bf16[128,3584]{1,0:T(8,128)(2,1)S(1)} %collective-permute-done.6.other_ref, bf16[3584,1152]{1,0:T(8,128)(2,1)} %hbm.2), custom_call_target="tpu_custom_call" | custom-call | tf_op jit(solution)/shard_map/pallas_call | solution.py:222
  39.9 5.4 %shard_map.194 = (f32[128,1152]{1,0:T(8,128)S(1)}, bf16[128,1152]{1,0:T(8,128)(2,1)S(1)}) custom-call(bf16[128,3584]{1,0:T(8,128)(2,1)S(1)} %pad_maximum_fusion.3.near_ref, bf16[128,3584]{1,0:T(8,128)(2,1)S(1)} %collective-permute-done.6.other_ref, bf16[3584,1152]{1,0:T(8,128)(2,1)} %hbm.3), custom_call_target="tpu_custom_call" | custom-call | tf_op jit(solution)/shard_map/pallas_call | solution.py:222
  45.9 1.6 add_convert_fusion
  48.6 6.2 %all-to-all-start = ((bf16[16,2,72,256]{3,2,1,0:T(8,128)(2,1)}), bf16[16,2,72,256]{3,2,1,0:T(8,128)(2,1)S(1)}, u32[]{:S(2)}, u32[]{:S(2)}) async-start(bf16[16,2,72,256]{3,2,1,0:T(8,128)(2,1)} %copy.56), calls=%async_computation | async-start | bytes 2359296 | tf_op jit(solution)/shard_map/all_to_all | solution.py:374
  56.6 5.4 %convolution_convert_fusion = bf16[128,3584]{1,0:T(8,128)(2,1)S(1)} fusion(bf16[128,1152]{1,0:T(8,128)(2,1)S(1)} %multiply_convert_fusion, bf16[1152,3584]{1,0:T(8,128)(2,1)} %param.29), kind=kOutput, calls=%fused_computation.2 | convolution fusion | flops 1057423360 | bytes 9469952 | tf_op jit(solution)/shard_map/dot_general | solution.py:381
  62.4 2.1 %collective-permute-done.9 = bf16[128,1152]{1,0:T(8,128)(2,1)S(1)} collective-permute-done((bf16[128,1152]{1,0:T(8,128)(2,1)S(1)}, bf16[128,1152]{1,0:T(8,128)(2,1)S(1)}, u32[]{:S(2)}, u32[]{:S(2)}) %collective-permute-start.9) | collective-permute-done | bytes 294944 | tf_op jit(solution)/shard_map/ppermute | solution.py:64
  66.1 1.7 collective-permute-start.12
  69.5 1.7 collective-permute-start.14
  71.3 10.7 %all-to-all-done = bf16[16,2,72,256]{3,2,1,0:T(8,128)(2,1)S(1)} async-done(((bf16[16,2,72,256]{3,2,1,0:T(8,128)(2,1)}), bf16[16,2,72,256]{3,2,1,0:T(8,128)(2,1)S(1)}, u32[]{:S(2)}, u32[]{:S(2)}) %all-to-all-start) | async-done | bytes 1179680 | tf_op jit(solution)/shard_map/all_to_all | solution.py:374
  82.7 1.7 collective-permute-done.14
  84.6 3.0 %collective-permute-start.15 = (bf16[8,7168]{1,0:T(8,128)(2,1)S(1)}, bf16[8,7168]{1,0:T(8,128)(2,1)S(1)}, u32[]{:S(2)}, u32[]{:S(2)}) collective-permute-start(bf16[8,7168]{1,0:T(8,128)(2,1)S(1)} %get-tuple-element.68), channel_id=1, source_target_pairs={{0,8},{1,9},{2,10},{3,11},{4,12},{5,13},{6,14},{7,15},{8,0},{9,1},... | collective-permute-start | bytes 344072 | tf_op jit(solution)/shard_map/ppermute | solution.py:64
  88.8 1.6 gather_fusion.1
  90.4 5.9 %collective-permute-done.15 = bf16[8,7168]{1,0:T(8,128)(2,1)S(1)} collective-permute-done((bf16[8,7168]{1,0:T(8,128)(2,1)S(1)}, bf16[8,7168]{1,0:T(8,128)(2,1)S(1)}, u32[]{:S(2)}, u32[]{:S(2)}) %collective-permute-start.15) | collective-permute-done | bytes 114720 | tf_op jit(solution)/shard_map/ppermute | solution.py:64
  97.5 1.8 collective-permute-start.18
  99.3 2.4 %collective-permute-start.19 = (bf16[8,3584]{1,0:T(8,128)(2,1)S(1)}, bf16[8,3584]{1,0:T(8,128)(2,1)S(1)}, u32[]{:S(2)}, u32[]{:S(2)}) collective-permute-start(bf16[8,3584]{1,0:T(8,128)(2,1)S(1)} %get-tuple-element.83), channel_id=1, source_target_pairs={{0,12},{1,13},{2,14},{3,15},{4,8},{5,9},{6,10},{7,11},{8,4},{9,5},... | collective-permute-start | bytes 172040 | tf_op jit(solution)/shard_map/ppermute | solution.py:64
  101.7 2.1 %collective-permute-start.22 = (bf16[8,3712]{1,0:T(8,128)(2,1)S(1)}, bf16[8,3712]{1,0:T(8,128)(2,1)S(1)}, u32[]{:S(2)}, u32[]{:S(2)}) collective-permute-start(bf16[8,3712]{1,0:T(8,128)(2,1)S(1)} %get-tuple-element.85), channel_id=1, source_target_pairs={{0,8},{1,9},{2,10},{3,11},{4,12},{5,13},{6,14},{7,15},{8,0},{9,1},... | collective-permute-start | bytes 178184 | tf_op jit(solution)/shard_map/ppermute | solution.py:64
  103.8 2.4 %collective-permute-start.23 = (bf16[8,3712]{1,0:T(8,128)(2,1)S(1)}, bf16[8,3712]{1,0:T(8,128)(2,1)S(1)}, u32[]{:S(2)}, u32[]{:S(2)}) collective-permute-start(bf16[8,3712]{1,0:T(8,128)(2,1)S(1)} %get-tuple-element.85), channel_id=1, source_target_pairs={{0,12},{1,13},{2,14},{3,15},{4,8},{5,9},{6,10},{7,11},{8,4},{9,5},... | collective-permute-start | bytes 178184 | tf_op jit(solution)/shard_map/ppermute | solution.py:64
  108.4 1.6 collective-permute-done.22
  110.6 2.6 %collective-permute-start.26 = (bf16[32,3712]{1,0:T(8,128)(2,1)S(1)}, bf16[32,3712]{1,0:T(8,128)(2,1)S(1)}, u32[]{:S(2)}, u32[]{:S(2)}) collective-permute-start(bf16[32,3712]{1,0:T(8,128)(2,1)S(1)} %maximum_bitcast_fusion.1), channel_id=1, source_target_pairs={{0,2},{1,3},{2,0},{3,1},{4,6},{5,7},{6,4},{7,5},{8,10},{9,11},{10,... | collective-permute-start | bytes 712712 | tf_op jit(solution)/shard_map/ppermute | solution.py:64
  113.7 7.4 %collective-permute-done.21 = bf16[32,3584]{1,0:T(8,128)(2,1)S(1)} collective-permute-done((bf16[32,3584]{1,0:T(8,128)(2,1)S(1)}, bf16[32,3584]{1,0:T(8,128)(2,1)S(1)}, u32[]{:S(2)}, u32[]{:S(2)}) %collective-permute-start.21) | collective-permute-done | bytes 229408 | tf_op jit(solution)/shard_map/ppermute | solution.py:64
  121.1 1.7 collective-permute-start.29
  122.8 4.4 %all-to-all-start.1 = ((bf16[16,2,72,256]{3,2,1,0:T(8,128)(2,1)}), bf16[16,2,72,256]{3,2,1,0:T(8,128)(2,1)}, u32[]{:S(2)}, u32[]{:S(2)}) async-start(bf16[16,2,72,256]{3,2,1,0:T(8,128)(2,1)} %bitcast.16), calls=%async_computation.1 | async-start | bytes 2359296 | tf_op jit(solution)/shard_map/all_to_all | solution.py:411
  133.0 22.3 %shard_map.195 = (bf16[128,3584]{1,0:T(8,128)(2,1)S(1)}, bf16[128,3584]{1,0:T(8,128)(2,1)}, bf16[128,3584]{1,0:T(8,128)(2,1)S(1)}, bf16[128,3584]{1,0:T(8,128)(2,1)}) custom-call(bf16[128,7296]{1,0:T(8,128)(2,1)S(1)} %pad_maximum_fusion.refs_0_, bf16[128,7296]{1,0:T(8,128)(2,1)} %collective-permute-done.30.refs_1_, bf16[1,7168,1024]{2,1,0:T(8,128)(2,1)} %refs_2_.1, ...), custom_call_target="tpu_custom_call" | custom-call | tf_op jit(solution)/shard_map/pallas_call | solution.py:318
  158.2 1.6 fusion.67
  163.1 1.7 collective-permute-start.41
  166.8 3.7 %collective-permute-done.39 = bf16[32,3584]{1,0:T(8,128)(2,1)S(1)} collective-permute-done((bf16[32,3584]{1,0:T(8,128)(2,1)S(1)}, bf16[32,3584]{1,0:T(8,128)(2,1)S(1)}, u32[]{:S(2)}, u32[]{:S(2)}) %collective-permute-start.39) | collective-permute-done | bytes 229408 | tf_op jit(solution)/shard_map/ppermute | solution.py:64
  171.2 5.0 %collective-permute-done.41 = bf16[32,3584]{1,0:T(8,128)(2,1)S(1)} collective-permute-done((bf16[32,3584]{1,0:T(8,128)(2,1)S(1)}, bf16[32,3584]{1,0:T(8,128)(2,1)S(1)}, u32[]{:S(2)}, u32[]{:S(2)}) %collective-permute-start.41) | collective-permute-done | bytes 229408 | tf_op jit(solution)/shard_map/ppermute | solution.py:64
  177.9 2.4 %collective-permute-start.43 = (bf16[8,3584]{1,0:T(8,128)(2,1)S(1)}, bf16[8,3584]{1,0:T(8,128)(2,1)S(1)}, u32[]{:S(2)}, u32[]{:S(2)}) collective-permute-start(bf16[8,3584]{1,0:T(8,128)(2,1)S(1)} %get-tuple-element.78), channel_id=1, source_target_pairs={{0,12},{1,13},{2,14},{3,15},{4,8},{5,9},{6,10},{7,11},{8,4},{9,5},... | collective-permute-start | bytes 172040 | tf_op jit(solution)/shard_map/ppermute | solution.py:64
  180.3 4.6 %collective-permute-done.34 = bf16[32,3584]{1,0:T(8,128)(2,1)S(1)} collective-permute-done((bf16[32,3584]{1,0:T(8,128)(2,1)S(1)}, bf16[32,3584]{1,0:T(8,128)(2,1)S(1)}, u32[]{:S(2)}, u32[]{:S(2)}) %collective-permute-start.34) | collective-permute-done | bytes 229408 | tf_op jit(solution)/shard_map/ppermute | solution.py:64
  186.6 2.4 %collective-permute-start.36 = (bf16[8,3584]{1,0:T(8,128)(2,1)S(1)}, bf16[8,3584]{1,0:T(8,128)(2,1)S(1)}, u32[]{:S(2)}, u32[]{:S(2)}) collective-permute-start(bf16[8,3584]{1,0:T(8,128)(2,1)S(1)} %get-tuple-element.75), channel_id=1, source_target_pairs={{0,12},{1,13},{2,14},{3,15},{4,8},{5,9},{6,10},{7,11},{8,4},{9,5},... | collective-permute-start | bytes 172040 | tf_op jit(solution)/shard_map/ppermute | solution.py:64
  (186 shorter events, 56.0 us)
Async XLA Ops:
  2.7 13.2 %collective-permute-start = (bf16[8,7168]{1,0:T(8,128)(2,1)S(1)}, bf16[8,7168]{1,0:T(8,128)(2,1)S(1)}, u32[]{:S(2)}, u32[]{:S(2)}) collective-permute-start(bf16[8,7168]{1,0:T(8,128)(2,1)S(1)} %fusion.23), channel_id=1, source_target_pairs={{0,8},{1,9},{2,10},{3,11},{4,12},{5,13},{6,14},{7,15},{8,0},{9,1},... | collective-permute-start | bytes 344072 | tf_op jit(solution)/shard_map/ppermute | solution.py:64
  6.8 9.1 %collective-permute-start.1 = (bf16[8,7168]{1,0:T(8,128)(2,1)S(1)}, bf16[8,7168]{1,0:T(8,128)(2,1)S(1)}, u32[]{:S(2)}, u32[]{:S(2)}) collective-permute-start(bf16[8,7168]{1,0:T(8,128)(2,1)S(1)} %fusion.23), channel_id=1, source_target_pairs={{0,12},{1,13},{2,14},{3,15},{4,8},{5,9},{6,10},{7,11},{8,4},{9,5},... | collective-permute-start | bytes 344072 | tf_op jit(solution)/shard_map/ppermute | solution.py:64
  16.4 13.9 %collective-permute-start.4 = (bf16[32,3584]{1,0:T(8,128)(2,1)S(1)}, bf16[32,3584]{1,0:T(8,128)(2,1)S(1)}, u32[]{:S(2)}, u32[]{:S(2)}) collective-permute-start(bf16[32,3584]{1,0:T(8,128)(2,1)S(1)} %get-tuple-element.72), channel_id=1, source_target_pairs={{0,16},{1,17},{2,18},{3,19},{4,20},{5,21},{6,22},{7,23},{8,24},{9,... | collective-permute-start | bytes 688136 | tf_op jit(solution)/shard_map/ppermute | solution.py:64
  18.0 12.3 %collective-permute-start.5 = (bf16[32,3584]{1,0:T(8,128)(2,1)S(1)}, bf16[32,3584]{1,0:T(8,128)(2,1)S(1)}, u32[]{:S(2)}, u32[]{:S(2)}) collective-permute-start(bf16[32,3584]{1,0:T(8,128)(2,1)S(1)} %get-tuple-element.72), channel_id=1, source_target_pairs={{0,18},{1,19},{2,16},{3,17},{4,22},{5,23},{6,20},{7,21},{8,26},{9,... | collective-permute-start | bytes 688136 | tf_op jit(solution)/shard_map/ppermute | solution.py:64
  19.5 10.8 %collective-permute-start.3 = (bf16[32,3584]{1,0:T(8,128)(2,1)S(1)}, bf16[32,3584]{1,0:T(8,128)(2,1)S(1)}, u32[]{:S(2)}, u32[]{:S(2)}) collective-permute-start(bf16[32,3584]{1,0:T(8,128)(2,1)S(1)} %get-tuple-element.71), channel_id=1, source_target_pairs={{0,2},{1,3},{2,0},{3,1},{4,6},{5,7},{6,4},{7,5},{8,10},{9,11},{10,... | collective-permute-start | bytes 688136 | tf_op jit(solution)/shard_map/ppermute | solution.py:64
  38.3 16.5 %collective-permute-start.7 = (bf16[128,1152]{1,0:T(8,128)(2,1)S(1)}, bf16[128,1152]{1,0:T(8,128)(2,1)S(1)}, u32[]{:S(2)}, u32[]{:S(2)}) collective-permute-start(bf16[128,1152]{1,0:T(8,128)(2,1)S(1)} %get-tuple-element.21), channel_id=1, source_target_pairs={{0,16},{1,17},{2,18},{3,19},{4,20},{5,21},{6,22},{7,23},{8,24},{9,... | collective-permute-start | bytes 884744 | tf_op jit(solution)/shard_map/ppermute | solution.py:64
  45.3 9.5 %collective-permute-start.8 = (bf16[128,1152]{1,0:T(8,128)(2,1)S(1)}, bf16[128,1152]{1,0:T(8,128)(2,1)S(1)}, u32[]{:S(2)}, u32[]{:S(2)}) collective-permute-start(bf16[128,1152]{1,0:T(8,128)(2,1)S(1)} %get-tuple-element.23), channel_id=1, source_target_pairs={{0,16},{1,17},{2,18},{3,19},{4,20},{5,21},{6,22},{7,23},{8,24},{9,... | collective-permute-start | bytes 884744 | tf_op jit(solution)/shard_map/ppermute | solution.py:64
  48.6 33.4 %all-to-all-start = ((bf16[16,2,72,256]{3,2,1,0:T(8,128)(2,1)}), bf16[16,2,72,256]{3,2,1,0:T(8,128)(2,1)S(1)}, u32[]{:S(2)}, u32[]{:S(2)}) async-start(bf16[16,2,72,256]{3,2,1,0:T(8,128)(2,1)} %copy.56), calls=%async_computation | async-start | bytes 2359296 | tf_op jit(solution)/shard_map/all_to_all | solution.py:374
  55.1 9.4 %collective-permute-start.9 = (bf16[128,1152]{1,0:T(8,128)(2,1)S(1)}, bf16[128,1152]{1,0:T(8,128)(2,1)S(1)}, u32[]{:S(2)}, u32[]{:S(2)}) collective-permute-start(bf16[128,1152]{1,0:T(8,128)(2,1)S(1)} %multiply_convert_fusion), channel_id=1, source_target_pairs={{0,16},{1,17},{2,18},{3,19},{4,20},{5,21},{6,22},{7,23},{8,24},{9,... | collective-permute-start | bytes 884744 | tf_op jit(solution)/shard_map/ppermute | solution.py:64
  66.1 16.6 %collective-permute-start.12 = (bf16[32,3584]{1,0:T(8,128)(2,1)S(1)}, bf16[32,3584]{1,0:T(8,128)(2,1)S(1)}, u32[]{:S(2)}, u32[]{:S(2)}) collective-permute-start(bf16[32,3584]{1,0:T(8,128)(2,1)S(1)} %get-tuple-element.64), channel_id=1, source_target_pairs={{0,2},{1,3},{2,0},{3,1},{4,6},{5,7},{6,4},{7,5},{8,10},{9,11},{10,... | collective-permute-start | bytes 688136 | tf_op jit(solution)/shard_map/ppermute | solution.py:64
  67.9 14.8 %collective-permute-start.13 = (bf16[32,3584]{1,0:T(8,128)(2,1)S(1)}, bf16[32,3584]{1,0:T(8,128)(2,1)S(1)}, u32[]{:S(2)}, u32[]{:S(2)}) collective-permute-start(bf16[32,3584]{1,0:T(8,128)(2,1)S(1)} %add_convert_fusion.7), channel_id=1, source_target_pairs={{0,16},{1,17},{2,18},{3,19},{4,20},{5,21},{6,22},{7,23},{8,24},{9,... | collective-permute-start | bytes 688136 | tf_op jit(solution)/shard_map/ppermute | solution.py:64
  69.5 14.9 %collective-permute-start.14 = (bf16[32,3584]{1,0:T(8,128)(2,1)S(1)}, bf16[32,3584]{1,0:T(8,128)(2,1)S(1)}, u32[]{:S(2)}, u32[]{:S(2)}) collective-permute-start(bf16[32,3584]{1,0:T(8,128)(2,1)S(1)} %convert_add_fusion.5), channel_id=1, source_target_pairs={{0,18},{1,19},{2,16},{3,17},{4,22},{5,23},{6,20},{7,21},{8,26},{9,... | collective-permute-start | bytes 688136 | tf_op jit(solution)/shard_map/ppermute | solution.py:64
  84.6 11.7 %collective-permute-start.15 = (bf16[8,7168]{1,0:T(8,128)(2,1)S(1)}, bf16[8,7168]{1,0:T(8,128)(2,1)S(1)}, u32[]{:S(2)}, u32[]{:S(2)}) collective-permute-start(bf16[8,7168]{1,0:T(8,128)(2,1)S(1)} %get-tuple-element.68), channel_id=1, source_target_pairs={{0,8},{1,9},{2,10},{3,11},{4,12},{5,13},{6,14},{7,15},{8,0},{9,1},... | collective-permute-start | bytes 344072 | tf_op jit(solution)/shard_map/ppermute | solution.py:64
  87.6 8.7 %collective-permute-start.16 = (bf16[8,7168]{1,0:T(8,128)(2,1)S(1)}, bf16[8,7168]{1,0:T(8,128)(2,1)S(1)}, u32[]{:S(2)}, u32[]{:S(2)}) collective-permute-start(bf16[8,7168]{1,0:T(8,128)(2,1)S(1)} %get-tuple-element.70), channel_id=1, source_target_pairs={{0,12},{1,13},{2,14},{3,15},{4,8},{5,9},{6,10},{7,11},{8,4},{9,5},... | collective-permute-start | bytes 344072 | tf_op jit(solution)/shard_map/ppermute | solution.py:64
  88.7 8.4 %collective-permute-start.17 = (bf16[8,7168]{1,0:T(8,128)(2,1)S(1)}, bf16[8,7168]{1,0:T(8,128)(2,1)S(1)}, u32[]{:S(2)}, u32[]{:S(2)}) collective-permute-start(bf16[8,7168]{1,0:T(8,128)(2,1)S(1)} %get-tuple-element.69), channel_id=1, source_target_pairs={{0,4},{1,5},{2,6},{3,7},{4,0},{5,1},{6,2},{7,3},{8,12},{9,13},{10,... | collective-permute-start | bytes 344072 | tf_op jit(solution)/shard_map/ppermute | solution.py:64
  97.5 8.7 %collective-permute-start.18 = (bf16[8,3584]{1,0:T(8,128)(2,1)S(1)}, bf16[8,3584]{1,0:T(8,128)(2,1)S(1)}, u32[]{:S(2)}, u32[]{:S(2)}) collective-permute-start(bf16[8,3584]{1,0:T(8,128)(2,1)S(1)} %get-tuple-element.83), channel_id=1, source_target_pairs={{0,8},{1,9},{2,10},{3,11},{4,12},{5,13},{6,14},{7,15},{8,0},{9,1},... | collective-permute-start | bytes 172040 | tf_op jit(solution)/shard_map/ppermute | solution.py:64
  106.2 21.1 %collective-permute-start.25 = (bf16[32,3584]{1,0:T(8,128)(2,1)S(1)}, bf16[32,3584]{1,0:T(8,128)(2,1)S(1)}, u32[]{:S(2)}, u32[]{:S(2)}) collective-permute-start(bf16[32,3584]{1,0:T(8,128)(2,1)S(1)} %maximum_bitcast_fusion.2), channel_id=1, source_target_pairs={{0,2},{1,3},{2,0},{3,1},{4,6},{5,7},{6,4},{7,5},{8,10},{9,11},{10,... | collective-permute-start | bytes 688136 | tf_op jit(solution)/shard_map/ppermute | solution.py:64
  106.9 20.4 %collective-permute-start.27 = (bf16[32,3584]{1,0:T(8,128)(2,1)S(1)}, bf16[32,3584]{1,0:T(8,128)(2,1)S(1)}, u32[]{:S(2)}, u32[]{:S(2)}) collective-permute-start(bf16[32,3584]{1,0:T(8,128)(2,1)S(1)} %maximum_bitcast_fusion.2), channel_id=1, source_target_pairs={{0,16},{1,17},{2,18},{3,19},{4,20},{5,21},{6,22},{7,23},{8,24},{9,... | collective-permute-start | bytes 688136 | tf_op jit(solution)/shard_map/ppermute | solution.py:64
  110.0 11.1 %collective-permute-start.21 = (bf16[32,3584]{1,0:T(8,128)(2,1)S(1)}, bf16[32,3584]{1,0:T(8,128)(2,1)S(1)}, u32[]{:S(2)}, u32[]{:S(2)}) collective-permute-start(bf16[32,3584]{1,0:T(8,128)(2,1)S(1)} %maximum_bitcast_fusion.2), channel_id=1, source_target_pairs={{0,18},{1,19},{2,16},{3,17},{4,22},{5,23},{6,20},{7,21},{8,26},{9,... | collective-permute-start | bytes 688136 | tf_op jit(solution)/shard_map/ppermute | solution.py:64
  110.6 16.6 %collective-permute-start.26 = (bf16[32,3712]{1,0:T(8,128)(2,1)S(1)}, bf16[32,3712]{1,0:T(8,128)(2,1)S(1)}, u32[]{:S(2)}, u32[]{:S(2)}) collective-permute-start(bf16[32,3712]{1,0:T(8,128)(2,1)S(1)} %maximum_bitcast_fusion.1), channel_id=1, source_target_pairs={{0,2},{1,3},{2,0},{3,1},{4,6},{5,7},{6,4},{7,5},{8,10},{9,11},{10,... | collective-permute-start | bytes 712712 | tf_op jit(solution)/shard_map/ppermute | solution.py:64
  113.2 14.1 %collective-permute-start.28 = (bf16[32,3712]{1,0:T(8,128)(2,1)S(1)}, bf16[32,3712]{1,0:T(8,128)(2,1)S(1)}, u32[]{:S(2)}, u32[]{:S(2)}) collective-permute-start(bf16[32,3712]{1,0:T(8,128)(2,1)S(1)} %maximum_bitcast_fusion.1), channel_id=1, source_target_pairs={{0,16},{1,17},{2,18},{3,19},{4,20},{5,21},{6,22},{7,23},{8,24},{9,... | collective-permute-start | bytes 712712 | tf_op jit(solution)/shard_map/ppermute | solution.py:64
  122.8 33.9 %all-to-all-start.1 = ((bf16[16,2,72,256]{3,2,1,0:T(8,128)(2,1)}), bf16[16,2,72,256]{3,2,1,0:T(8,128)(2,1)}, u32[]{:S(2)}, u32[]{:S(2)}) async-start(bf16[16,2,72,256]{3,2,1,0:T(8,128)(2,1)} %bitcast.16), calls=%async_computation.1 | async-start | bytes 2359296 | tf_op jit(solution)/shard_map/all_to_all | solution.py:411
  156.4 8.4 %collective-permute-start.31 = (bf16[128,3584]{1,0:T(8,128)(2,1)}, bf16[128,3584]{1,0:T(8,128)(2,1)S(1)}, u32[]{:S(2)}, u32[]{:S(2)}) collective-permute-start(bf16[128,3584]{1,0:T(8,128)(2,1)} %get-tuple-element.32), channel_id=1, source_target_pairs={{0,1},{1,0},{2,3},{3,2},{4,5},{5,4},{6,7},{7,6},{8,9},{9,8},{10,11... | collective-permute-start | bytes 2752520 | tf_op jit(solution)/shard_map/ppermute | solution.py:64
  161.2 9.3 %collective-permute-start.39 = (bf16[32,3584]{1,0:T(8,128)(2,1)S(1)}, bf16[32,3584]{1,0:T(8,128)(2,1)S(1)}, u32[]{:S(2)}, u32[]{:S(2)}) collective-permute-start(bf16[32,3584]{1,0:T(8,128)(2,1)S(1)} %get-tuple-element.61), channel_id=1, source_target_pairs={{0,2},{1,3},{2,0},{3,1},{4,6},{5,7},{6,4},{7,5},{8,10},{9,11},{10,... | collective-permute-start | bytes 688136 | tf_op jit(solution)/shard_map/ppermute | solution.py:64
  161.8 9.4 %collective-permute-start.40 = (bf16[32,3584]{1,0:T(8,128)(2,1)S(1)}, bf16[32,3584]{1,0:T(8,128)(2,1)S(1)}, u32[]{:S(2)}, u32[]{:S(2)}) collective-permute-start(bf16[32,3584]{1,0:T(8,128)(2,1)S(1)} %get-tuple-element.63), channel_id=1, source_target_pairs={{0,16},{1,17},{2,18},{3,19},{4,20},{5,21},{6,22},{7,23},{8,24},{9,... | collective-permute-start | bytes 688136 | tf_op jit(solution)/shard_map/ppermute | solution.py:64
  163.1 13.1 %collective-permute-start.41 = (bf16[32,3584]{1,0:T(8,128)(2,1)S(1)}, bf16[32,3584]{1,0:T(8,128)(2,1)S(1)}, u32[]{:S(2)}, u32[]{:S(2)}) collective-permute-start(bf16[32,3584]{1,0:T(8,128)(2,1)S(1)} %get-tuple-element.62), channel_id=1, source_target_pairs={{0,18},{1,19},{2,16},{3,17},{4,22},{5,23},{6,20},{7,21},{8,26},{9,... | collective-permute-start | bytes 688136 | tf_op jit(solution)/shard_map/ppermute | solution.py:64
  164.9 15.4 %collective-permute-start.32 = (bf16[32,3584]{1,0:T(8,128)(2,1)S(1)}, bf16[32,3584]{1,0:T(8,128)(2,1)S(1)}, u32[]{:S(2)}, u32[]{:S(2)}) collective-permute-start(bf16[32,3584]{1,0:T(8,128)(2,1)S(1)} %get-tuple-element.58), channel_id=1, source_target_pairs={{0,2},{1,3},{2,0},{3,1},{4,6},{5,7},{6,4},{7,5},{8,10},{9,11},{10,... | collective-permute-start | bytes 688136 | tf_op jit(solution)/shard_map/ppermute | solution.py:64
  165.5 14.8 %collective-permute-start.33 = (bf16[32,3584]{1,0:T(8,128)(2,1)S(1)}, bf16[32,3584]{1,0:T(8,128)(2,1)S(1)}, u32[]{:S(2)}, u32[]{:S(2)}) collective-permute-start(bf16[32,3584]{1,0:T(8,128)(2,1)S(1)} %get-tuple-element.60), channel_id=1, source_target_pairs={{0,16},{1,17},{2,18},{3,19},{4,20},{5,21},{6,22},{7,23},{8,24},{9,... | collective-permute-start | bytes 688136 | tf_op jit(solution)/shard_map/ppermute | solution.py:64
  170.5 14.4 %collective-permute-start.34 = (bf16[32,3584]{1,0:T(8,128)(2,1)S(1)}, bf16[32,3584]{1,0:T(8,128)(2,1)S(1)}, u32[]{:S(2)}, u32[]{:S(2)}) collective-permute-start(bf16[32,3584]{1,0:T(8,128)(2,1)S(1)} %get-tuple-element.59), channel_id=1, source_target_pairs={{0,18},{1,19},{2,16},{3,17},{4,22},{5,23},{6,20},{7,21},{8,26},{9,... | collective-permute-start | bytes 688136 | tf_op jit(solution)/shard_map/ppermute | solution.py:64
  176.4 12.6 %collective-permute-start.42 = (bf16[8,3584]{1,0:T(8,128)(2,1)S(1)}, bf16[8,3584]{1,0:T(8,128)(2,1)S(1)}, u32[]{:S(2)}, u32[]{:S(2)}) collective-permute-start(bf16[8,3584]{1,0:T(8,128)(2,1)S(1)} %get-tuple-element.76), channel_id=1, source_target_pairs={{0,8},{1,9},{2,10},{3,11},{4,12},{5,13},{6,14},{7,15},{8,0},{9,1},... | collective-permute-start | bytes 172040 | tf_op jit(solution)/shard_map/ppermute | solution.py:64
  177.9 12.2 %collective-permute-start.43 = (bf16[8,3584]{1,0:T(8,128)(2,1)S(1)}, bf16[8,3584]{1,0:T(8,128)(2,1)S(1)}, u32[]{:S(2)}, u32[]{:S(2)}) collective-permute-start(bf16[8,3584]{1,0:T(8,128)(2,1)S(1)} %get-tuple-element.78), channel_id=1, source_target_pairs={{0,12},{1,13},{2,14},{3,15},{4,8},{5,9},{6,10},{7,11},{8,4},{9,5},... | collective-permute-start | bytes 172040 | tf_op jit(solution)/shard_map/ppermute | solution.py:64
  180.3 9.8 %collective-permute-start.44 = (bf16[8,3584]{1,0:T(8,128)(2,1)S(1)}, bf16[8,3584]{1,0:T(8,128)(2,1)S(1)}, u32[]{:S(2)}, u32[]{:S(2)}) collective-permute-start(bf16[8,3584]{1,0:T(8,128)(2,1)S(1)} %get-tuple-element.77), channel_id=1, source_target_pairs={{0,4},{1,5},{2,6},{3,7},{4,0},{5,1},{6,2},{7,3},{8,12},{9,13},{10,... | collective-permute-start | bytes 172040 | tf_op jit(solution)/shard_map/ppermute | solution.py:64
  (35 other events, 207.7 us)

commit v5 on v4

--- a/solution.py
+++ b/solution.py
@@ -19,7 +19,7 @@
 DOWN_STEP = 896
 STEP = 1024
 SLOTS = 3
-DENSE_STEP = 896
+DENSE_STEPS = (512, 896)
 DENSE_VMEM = 14
 HBM = pltpu.MemorySpace.HBM
 
@@ -191,12 +191,13 @@
 
 def dense_kernel(groups, near_ref, other_ref, hbm, own_ref, away_ref, rows_ref, buf, sem):
     size = near_ref.shape[0] // groups
-    steps = near_ref.shape[1] // DENSE_STEP
+    piece = buf.shape[1]
+    steps = near_ref.shape[1] // piece
 
     def make(at):
         slot = lax.rem(at, SLOTS)
         return pltpu.make_async_copy(
-            hbm.at[pl.ds(at * DENSE_STEP, DENSE_STEP)], buf.at[slot], sem.at[slot]
+            hbm.at[pl.ds(at * piece, piece)], buf.at[slot], sem.at[slot]
         )
 
     wait, free = ring((steps, make), SLOTS)
@@ -207,7 +208,7 @@
     acc = jnp.zeros((rows_ref.shape[0], own_ref.shape[1]), jnp.float32)
     for at in range(steps):
         wait(at)
-        rows = rows_ref[:, at * DENSE_STEP : (at + 1) * DENSE_STEP]
+        rows = rows_ref[:, at * piece : (at + 1) * piece]
         acc = acc + jnp.dot(rows, buf[at % SLOTS], preferred_element_type=jnp.float32)
         free(at)
     own = own_ref.shape[0]
@@ -219,6 +220,7 @@
     count, width = 2 * near.shape[0], weights.shape[1]
     vmem, far = pl.BlockSpec(memory_space=pltpu.VMEM), pl.BlockSpec(memory_space=HBM)
     own = count // groups
+    step = next(step for step in DENSE_STEPS if near.shape[1] % step == 0)
     return pl.pallas_call(
         functools.partial(dense_kernel, groups),
         out_shape=(
@@ -229,7 +231,7 @@
         out_specs=(vmem, vmem),
         scratch_shapes=[
             pltpu.VMEM((count, near.shape[1]), jnp.bfloat16),
-            pltpu.VMEM((SLOTS, DENSE_STEP, width), jnp.bfloat16),
+            pltpu.VMEM((SLOTS, step, width), jnp.bfloat16),
             pltpu.SemaphoreType.DMA((SLOTS,)),
         ],
         compiler_params=pltpu.CompilerParams(vmem_limit_bytes=DENSE_VMEM * 1024 * 1024),

time: 195 us -> 194 us (level)
  transfers between devices with their start and end apart: 47 -> 47, of which waited for: 19 -> 20; matrix products, arithmetic and copies ran while one was open for 14% -> 14% of each run, Pallas kernels for 14% -> 14%
where the time goes in v5:
time: 194 us
  waiting for transfers between devices  63.4 us (33%)
  starting transfers between devices  62.7 us (32%)
  Pallas kernels  32.6 us (17%)
  matrix products  13.7 us (7%)
  other arithmetic  10.7 us (6%)
  local copies, waits for them, and re-layouts  9.28 us (5%)
    ppermute x45, waiting for transfers between devices, swap(): return lax.ppermute(block, AXES, pairs)  52.7 us
    ppermute x45, starting transfers between devices, swap(): return lax.ppermute(block, AXES, pairs)  52.1 us
    pallas_call x1, Pallas kernels, run_expert(): pl.pallas_call(functools.partial(expert_kernel, DOWN_CUTS, experts), out_...  22.3 us
    all_to_all x1, waiting for transfers between devices, on_device(): lax.all_to_all(outgoing, 'tp', split_axis=0, concat_axis=0, tiled=True)  10.7 us
    pallas_call x2, Pallas kernels, run_dense(): pl.pallas_call(functools.partial(dense_kernel, groups), out_shape=(jax.Sh...  10.3 us
    dot_general x2, matrix products, on_device(): jnp.dot(block, w_down, preferred_element_type=jnp.float32)  6.74 us
    all_to_all x1, starting transfers between devices, on_device(): lax.all_to_all(outgoing, 'tp', split_axis=0, concat_axis=0, tiled=True)  6.16 us
    all_to_all x1, starting transfers between devices, on_device(): home = lax.all_to_all(homing, 'tp', split_axis=0, concat_axis=0, tiled=True)  4.44 us
  transfers between devices with their start and end apart: 47, of which 20 were waited for; matrix products, arithmetic and copies ran while one was open for 14% of the time, Pallas kernels for 14%

profile of v5, /device:TPU:0, one launch (start us, length us, event | category | flops | bytes accessed | tf_op | source)
XLA Modules:
  0.0 193.6 jit_solution(1367514308384475997)
XLA Ops:
  2.7 4.1 %collective-permute-start = (bf16[8,7168]{1,0:T(8,128)(2,1)S(1)}, bf16[8,7168]{1,0:T(8,128)(2,1)S(1)}, u32[]{:S(2)}, u32[]{:S(2)}) collective-permute-start(bf16[8,7168]{1,0:T(8,128)(2,1)S(1)} %fusion.23), channel_id=1, source_target_pairs={{0,8},{1,9},{2,10},{3,11},{4,12},{5,13},{6,14},{7,15},{8,0},{9,1},... | collective-permute-start | bytes 344072 | tf_op jit(solution)/shard_map/ppermute | solution.py:64
  16.4 1.6 collective-permute-start.4
  20.1 10.2 %collective-permute-done.3 = bf16[32,3584]{1,0:T(8,128)(2,1)S(1)} collective-permute-done((bf16[32,3584]{1,0:T(8,128)(2,1)S(1)}, bf16[32,3584]{1,0:T(8,128)(2,1)S(1)}, u32[]{:S(2)}, u32[]{:S(2)}) %collective-permute-start.3) | collective-permute-done | bytes 229408 | tf_op jit(solution)/shard_map/ppermute | solution.py:64
  32.9 5.2 %shard_map.193 = (f32[128,1152]{1,0:T(8,128)S(1)}, bf16[128,1152]{1,0:T(8,128)(2,1)S(1)}) custom-call(bf16[128,3584]{1,0:T(8,128)(2,1)S(1)} %pad_maximum_fusion.3.near_ref, bf16[128,3584]{1,0:T(8,128)(2,1)S(1)} %collective-permute-done.6.other_ref, bf16[3584,1152]{1,0:T(8,128)(2,1)} %hbm.2), custom_call_target="tpu_custom_call" | custom-call | tf_op jit(solution)/shard_map/pallas_call | solution.py:224
  39.6 5.1 %shard_map.194 = (f32[128,1152]{1,0:T(8,128)S(1)}, bf16[128,1152]{1,0:T(8,128)(2,1)S(1)}) custom-call(bf16[128,3584]{1,0:T(8,128)(2,1)S(1)} %pad_maximum_fusion.3.near_ref, bf16[128,3584]{1,0:T(8,128)(2,1)S(1)} %collective-permute-done.6.other_ref, bf16[3584,1152]{1,0:T(8,128)(2,1)} %hbm.3), custom_call_target="tpu_custom_call" | custom-call | tf_op jit(solution)/shard_map/pallas_call | solution.py:224
  45.4 1.6 add_convert_fusion
  48.1 6.2 %all-to-all-start = ((bf16[16,2,72,256]{3,2,1,0:T(8,128)(2,1)}), bf16[16,2,72,256]{3,2,1,0:T(8,128)(2,1)S(1)}, u32[]{:S(2)}, u32[]{:S(2)}) async-start(bf16[16,2,72,256]{3,2,1,0:T(8,128)(2,1)} %copy.56), calls=%async_computation | async-start | bytes 2359296 | tf_op jit(solution)/shard_map/all_to_all | solution.py:376
  56.1 5.4 %convolution_convert_fusion = bf16[128,3584]{1,0:T(8,128)(2,1)S(1)} fusion(bf16[128,1152]{1,0:T(8,128)(2,1)S(1)} %multiply_convert_fusion, bf16[1152,3584]{1,0:T(8,128)(2,1)} %param.29), kind=kOutput, calls=%fused_computation.2 | convolution fusion | flops 1057423360 | bytes 9469952 | tf_op jit(solution)/shard_map/dot_general | solution.py:383
  61.9 2.1 %collective-permute-done.9 = bf16[128,1152]{1,0:T(8,128)(2,1)S(1)} collective-permute-done((bf16[128,1152]{1,0:T(8,128)(2,1)S(1)}, bf16[128,1152]{1,0:T(8,128)(2,1)S(1)}, u32[]{:S(2)}, u32[]{:S(2)}) %collective-permute-start.9) | collective-permute-done | bytes 294944 | tf_op jit(solution)/shard_map/ppermute | solution.py:64
  65.6 1.7 collective-permute-start.12
  69.0 1.6 collective-permute-start.14
  70.8 10.7 %all-to-all-done = bf16[16,2,72,256]{3,2,1,0:T(8,128)(2,1)S(1)} async-done(((bf16[16,2,72,256]{3,2,1,0:T(8,128)(2,1)}), bf16[16,2,72,256]{3,2,1,0:T(8,128)(2,1)S(1)}, u32[]{:S(2)}, u32[]{:S(2)}) %all-to-all-start) | async-done | bytes 1179680 | tf_op jit(solution)/shard_map/all_to_all | solution.py:376
  82.2 1.7 collective-permute-done.14
  84.1 3.1 %collective-permute-start.15 = (bf16[8,7168]{1,0:T(8,128)(2,1)S(1)}, bf16[8,7168]{1,0:T(8,128)(2,1)S(1)}, u32[]{:S(2)}, u32[]{:S(2)}) collective-permute-start(bf16[8,7168]{1,0:T(8,128)(2,1)S(1)} %get-tuple-element.68), channel_id=1, source_target_pairs={{0,8},{1,9},{2,10},{3,11},{4,12},{5,13},{6,14},{7,15},{8,0},{9,1},... | collective-permute-start | bytes 344072 | tf_op jit(solution)/shard_map/ppermute | solution.py:64
  88.3 1.6 gather_fusion.1
  89.9 5.9 %collective-permute-done.15 = bf16[8,7168]{1,0:T(8,128)(2,1)S(1)} collective-permute-done((bf16[8,7168]{1,0:T(8,128)(2,1)S(1)}, bf16[8,7168]{1,0:T(8,128)(2,1)S(1)}, u32[]{:S(2)}, u32[]{:S(2)}) %collective-permute-start.15) | collective-permute-done | bytes 114720 | tf_op jit(solution)/shard_map/ppermute | solution.py:64
  97.1 1.8 collective-permute-start.18
  98.9 2.4 %collective-permute-start.19 = (bf16[8,3584]{1,0:T(8,128)(2,1)S(1)}, bf16[8,3584]{1,0:T(8,128)(2,1)S(1)}, u32[]{:S(2)}, u32[]{:S(2)}) collective-permute-start(bf16[8,3584]{1,0:T(8,128)(2,1)S(1)} %get-tuple-element.83), channel_id=1, source_target_pairs={{0,12},{1,13},{2,14},{3,15},{4,8},{5,9},{6,10},{7,11},{8,4},{9,5},... | collective-permute-start | bytes 172040 | tf_op jit(solution)/shard_map/ppermute | solution.py:64
  101.3 2.1 %collective-permute-start.22 = (bf16[8,3712]{1,0:T(8,128)(2,1)S(1)}, bf16[8,3712]{1,0:T(8,128)(2,1)S(1)}, u32[]{:S(2)}, u32[]{:S(2)}) collective-permute-start(bf16[8,3712]{1,0:T(8,128)(2,1)S(1)} %get-tuple-element.85), channel_id=1, source_target_pairs={{0,8},{1,9},{2,10},{3,11},{4,12},{5,13},{6,14},{7,15},{8,0},{9,1},... | collective-permute-start | bytes 178184 | tf_op jit(solution)/shard_map/ppermute | solution.py:64
  103.4 2.4 %collective-permute-start.23 = (bf16[8,3712]{1,0:T(8,128)(2,1)S(1)}, bf16[8,3712]{1,0:T(8,128)(2,1)S(1)}, u32[]{:S(2)}, u32[]{:S(2)}) collective-permute-start(bf16[8,3712]{1,0:T(8,128)(2,1)S(1)} %get-tuple-element.85), channel_id=1, source_target_pairs={{0,12},{1,13},{2,14},{3,15},{4,8},{5,9},{6,10},{7,11},{8,4},{9,5},... | collective-permute-start | bytes 178184 | tf_op jit(solution)/shard_map/ppermute | solution.py:64
  107.9 1.7 collective-permute-done.22
  110.2 2.4 %collective-permute-start.26 = (bf16[32,3712]{1,0:T(8,128)(2,1)S(1)}, bf16[32,3712]{1,0:T(8,128)(2,1)S(1)}, u32[]{:S(2)}, u32[]{:S(2)}) collective-permute-start(bf16[32,3712]{1,0:T(8,128)(2,1)S(1)} %maximum_bitcast_fusion.1), channel_id=1, source_target_pairs={{0,2},{1,3},{2,0},{3,1},{4,6},{5,7},{6,4},{7,5},{8,10},{9,11},{10,... | collective-permute-start | bytes 712712 | tf_op jit(solution)/shard_map/ppermute | solution.py:64
  113.3 7.4 %collective-permute-done.21 = bf16[32,3584]{1,0:T(8,128)(2,1)S(1)} collective-permute-done((bf16[32,3584]{1,0:T(8,128)(2,1)S(1)}, bf16[32,3584]{1,0:T(8,128)(2,1)S(1)}, u32[]{:S(2)}, u32[]{:S(2)}) %collective-permute-start.21) | collective-permute-done | bytes 229408 | tf_op jit(solution)/shard_map/ppermute | solution.py:64
  122.3 4.4 %all-to-all-start.1 = ((bf16[16,2,72,256]{3,2,1,0:T(8,128)(2,1)}), bf16[16,2,72,256]{3,2,1,0:T(8,128)(2,1)}, u32[]{:S(2)}, u32[]{:S(2)}) async-start(bf16[16,2,72,256]{3,2,1,0:T(8,128)(2,1)} %bitcast.16), calls=%async_computation.1 | async-start | bytes 2359296 | tf_op jit(solution)/shard_map/all_to_all | solution.py:413
  132.7 22.3 %shard_map.195 = (bf16[128,3584]{1,0:T(8,128)(2,1)S(1)}, bf16[128,3584]{1,0:T(8,128)(2,1)}, bf16[128,3584]{1,0:T(8,128)(2,1)S(1)}, bf16[128,3584]{1,0:T(8,128)(2,1)}) custom-call(bf16[128,7296]{1,0:T(8,128)(2,1)S(1)} %pad_maximum_fusion.refs_0_, bf16[128,7296]{1,0:T(8,128)(2,1)} %collective-permute-done.30.refs_1_, bf16[1,7168,1024]{2,1,0:T(8,128)(2,1)} %refs_2_.1, ...), custom_call_target="tpu_custom_call" | custom-call | tf_op jit(solution)/shard_map/pallas_call | solution.py:320
  157.9 1.6 fusion.67
  162.5 1.9 collective-permute-start.41
  166.3 3.9 %collective-permute-done.39 = bf16[32,3584]{1,0:T(8,128)(2,1)S(1)} collective-permute-done((bf16[32,3584]{1,0:T(8,128)(2,1)S(1)}, bf16[32,3584]{1,0:T(8,128)(2,1)S(1)}, u32[]{:S(2)}, u32[]{:S(2)}) %collective-permute-start.39) | collective-permute-done | bytes 229408 | tf_op jit(solution)/shard_map/ppermute | solution.py:64
  170.5 5.3 %collective-permute-done.41 = bf16[32,3584]{1,0:T(8,128)(2,1)S(1)} collective-permute-done((bf16[32,3584]{1,0:T(8,128)(2,1)S(1)}, bf16[32,3584]{1,0:T(8,128)(2,1)S(1)}, u32[]{:S(2)}, u32[]{:S(2)}) %collective-permute-start.41) | collective-permute-done | bytes 229408 | tf_op jit(solution)/shard_map/ppermute | solution.py:64
  177.5 2.4 %collective-permute-start.43 = (bf16[8,3584]{1,0:T(8,128)(2,1)S(1)}, bf16[8,3584]{1,0:T(8,128)(2,1)S(1)}, u32[]{:S(2)}, u32[]{:S(2)}) collective-permute-start(bf16[8,3584]{1,0:T(8,128)(2,1)S(1)} %get-tuple-element.78), channel_id=1, source_target_pairs={{0,12},{1,13},{2,14},{3,15},{4,8},{5,9},{6,10},{7,11},{8,4},{9,5},... | collective-permute-start | bytes 172040 | tf_op jit(solution)/shard_map/ppermute | solution.py:64
  179.9 4.7 %collective-permute-done.34 = bf16[32,3584]{1,0:T(8,128)(2,1)S(1)} collective-permute-done((bf16[32,3584]{1,0:T(8,128)(2,1)S(1)}, bf16[32,3584]{1,0:T(8,128)(2,1)S(1)}, u32[]{:S(2)}, u32[]{:S(2)}) %collective-permute-start.34) | collective-permute-done | bytes 229408 | tf_op jit(solution)/shard_map/ppermute | solution.py:64
  186.3 2.4 %collective-permute-start.36 = (bf16[8,3584]{1,0:T(8,128)(2,1)S(1)}, bf16[8,3584]{1,0:T(8,128)(2,1)S(1)}, u32[]{:S(2)}, u32[]{:S(2)}) collective-permute-start(bf16[8,3584]{1,0:T(8,128)(2,1)S(1)} %get-tuple-element.75), channel_id=1, source_target_pairs={{0,12},{1,13},{2,14},{3,15},{4,8},{5,9},{6,10},{7,11},{8,4},{9,5},... | collective-permute-start | bytes 172040 | tf_op jit(solution)/shard_map/ppermute | solution.py:64
  (186 shorter events, 55.4 us)
Async XLA Ops:
  2.7 13.2 %collective-permute-start = (bf16[8,7168]{1,0:T(8,128)(2,1)S(1)}, bf16[8,7168]{1,0:T(8,128)(2,1)S(1)}, u32[]{:S(2)}, u32[]{:S(2)}) collective-permute-start(bf16[8,7168]{1,0:T(8,128)(2,1)S(1)} %fusion.23), channel_id=1, source_target_pairs={{0,8},{1,9},{2,10},{3,11},{4,12},{5,13},{6,14},{7,15},{8,0},{9,1},... | collective-permute-start | bytes 344072 | tf_op jit(solution)/shard_map/ppermute | solution.py:64
  6.8 9.1 %collective-permute-start.1 = (bf16[8,7168]{1,0:T(8,128)(2,1)S(1)}, bf16[8,7168]{1,0:T(8,128)(2,1)S(1)}, u32[]{:S(2)}, u32[]{:S(2)}) collective-permute-start(bf16[8,7168]{1,0:T(8,128)(2,1)S(1)} %fusion.23), channel_id=1, source_target_pairs={{0,12},{1,13},{2,14},{3,15},{4,8},{5,9},{6,10},{7,11},{8,4},{9,5},... | collective-permute-start | bytes 344072 | tf_op jit(solution)/shard_map/ppermute | solution.py:64
  16.4 13.9 %collective-permute-start.4 = (bf16[32,3584]{1,0:T(8,128)(2,1)S(1)}, bf16[32,3584]{1,0:T(8,128)(2,1)S(1)}, u32[]{:S(2)}, u32[]{:S(2)}) collective-permute-start(bf16[32,3584]{1,0:T(8,128)(2,1)S(1)} %get-tuple-element.72), channel_id=1, source_target_pairs={{0,16},{1,17},{2,18},{3,19},{4,20},{5,21},{6,22},{7,23},{8,24},{9,... | collective-permute-start | bytes 688136 | tf_op jit(solution)/shard_map/ppermute | solution.py:64
  18.0 12.3 %collective-permute-start.5 = (bf16[32,3584]{1,0:T(8,128)(2,1)S(1)}, bf16[32,3584]{1,0:T(8,128)(2,1)S(1)}, u32[]{:S(2)}, u32[]{:S(2)}) collective-permute-start(bf16[32,3584]{1,0:T(8,128)(2,1)S(1)} %get-tuple-element.72), channel_id=1, source_target_pairs={{0,18},{1,19},{2,16},{3,17},{4,22},{5,23},{6,20},{7,21},{8,26},{9,... | collective-permute-start | bytes 688136 | tf_op jit(solution)/shard_map/ppermute | solution.py:64
  19.5 10.8 %collective-permute-start.3 = (bf16[32,3584]{1,0:T(8,128)(2,1)S(1)}, bf16[32,3584]{1,0:T(8,128)(2,1)S(1)}, u32[]{:S(2)}, u32[]{:S(2)}) collective-permute-start(bf16[32,3584]{1,0:T(8,128)(2,1)S(1)} %get-tuple-element.71), channel_id=1, source_target_pairs={{0,2},{1,3},{2,0},{3,1},{4,6},{5,7},{6,4},{7,5},{8,10},{9,11},{10,... | collective-permute-start | bytes 688136 | tf_op jit(solution)/shard_map/ppermute | solution.py:64
  38.1 16.2 %collective-permute-start.7 = (bf16[128,1152]{1,0:T(8,128)(2,1)S(1)}, bf16[128,1152]{1,0:T(8,128)(2,1)S(1)}, u32[]{:S(2)}, u32[]{:S(2)}) collective-permute-start(bf16[128,1152]{1,0:T(8,128)(2,1)S(1)} %get-tuple-element.21), channel_id=1, source_target_pairs={{0,16},{1,17},{2,18},{3,19},{4,20},{5,21},{6,22},{7,23},{8,24},{9,... | collective-permute-start | bytes 884744 | tf_op jit(solution)/shard_map/ppermute | solution.py:64
  44.8 9.5 %collective-permute-start.8 = (bf16[128,1152]{1,0:T(8,128)(2,1)S(1)}, bf16[128,1152]{1,0:T(8,128)(2,1)S(1)}, u32[]{:S(2)}, u32[]{:S(2)}) collective-permute-start(bf16[128,1152]{1,0:T(8,128)(2,1)S(1)} %get-tuple-element.23), channel_id=1, source_target_pairs={{0,16},{1,17},{2,18},{3,19},{4,20},{5,21},{6,22},{7,23},{8,24},{9,... | collective-permute-start | bytes 884744 | tf_op jit(solution)/shard_map/ppermute | solution.py:64
  48.1 33.3 %all-to-all-start = ((bf16[16,2,72,256]{3,2,1,0:T(8,128)(2,1)}), bf16[16,2,72,256]{3,2,1,0:T(8,128)(2,1)S(1)}, u32[]{:S(2)}, u32[]{:S(2)}) async-start(bf16[16,2,72,256]{3,2,1,0:T(8,128)(2,1)} %copy.56), calls=%async_computation | async-start | bytes 2359296 | tf_op jit(solution)/shard_map/all_to_all | solution.py:376
  54.6 9.4 %collective-permute-start.9 = (bf16[128,1152]{1,0:T(8,128)(2,1)S(1)}, bf16[128,1152]{1,0:T(8,128)(2,1)S(1)}, u32[]{:S(2)}, u32[]{:S(2)}) collective-permute-start(bf16[128,1152]{1,0:T(8,128)(2,1)S(1)} %multiply_convert_fusion), channel_id=1, source_target_pairs={{0,16},{1,17},{2,18},{3,19},{4,20},{5,21},{6,22},{7,23},{8,24},{9,... | collective-permute-start | bytes 884744 | tf_op jit(solution)/shard_map/ppermute | solution.py:64
  65.6 16.6 %collective-permute-start.12 = (bf16[32,3584]{1,0:T(8,128)(2,1)S(1)}, bf16[32,3584]{1,0:T(8,128)(2,1)S(1)}, u32[]{:S(2)}, u32[]{:S(2)}) collective-permute-start(bf16[32,3584]{1,0:T(8,128)(2,1)S(1)} %get-tuple-element.64), channel_id=1, source_target_pairs={{0,2},{1,3},{2,0},{3,1},{4,6},{5,7},{6,4},{7,5},{8,10},{9,11},{10,... | collective-permute-start | bytes 688136 | tf_op jit(solution)/shard_map/ppermute | solution.py:64
  67.4 14.8 %collective-permute-start.13 = (bf16[32,3584]{1,0:T(8,128)(2,1)S(1)}, bf16[32,3584]{1,0:T(8,128)(2,1)S(1)}, u32[]{:S(2)}, u32[]{:S(2)}) collective-permute-start(bf16[32,3584]{1,0:T(8,128)(2,1)S(1)} %add_convert_fusion.7), channel_id=1, source_target_pairs={{0,16},{1,17},{2,18},{3,19},{4,20},{5,21},{6,22},{7,23},{8,24},{9,... | collective-permute-start | bytes 688136 | tf_op jit(solution)/shard_map/ppermute | solution.py:64
  69.0 14.9 %collective-permute-start.14 = (bf16[32,3584]{1,0:T(8,128)(2,1)S(1)}, bf16[32,3584]{1,0:T(8,128)(2,1)S(1)}, u32[]{:S(2)}, u32[]{:S(2)}) collective-permute-start(bf16[32,3584]{1,0:T(8,128)(2,1)S(1)} %convert_add_fusion.5), channel_id=1, source_target_pairs={{0,18},{1,19},{2,16},{3,17},{4,22},{5,23},{6,20},{7,21},{8,26},{9,... | collective-permute-start | bytes 688136 | tf_op jit(solution)/shard_map/ppermute | solution.py:64
  84.1 11.7 %collective-permute-start.15 = (bf16[8,7168]{1,0:T(8,128)(2,1)S(1)}, bf16[8,7168]{1,0:T(8,128)(2,1)S(1)}, u32[]{:S(2)}, u32[]{:S(2)}) collective-permute-start(bf16[8,7168]{1,0:T(8,128)(2,1)S(1)} %get-tuple-element.68), channel_id=1, source_target_pairs={{0,8},{1,9},{2,10},{3,11},{4,12},{5,13},{6,14},{7,15},{8,0},{9,1},... | collective-permute-start | bytes 344072 | tf_op jit(solution)/shard_map/ppermute | solution.py:64
  87.2 8.7 %collective-permute-start.16 = (bf16[8,7168]{1,0:T(8,128)(2,1)S(1)}, bf16[8,7168]{1,0:T(8,128)(2,1)S(1)}, u32[]{:S(2)}, u32[]{:S(2)}) collective-permute-start(bf16[8,7168]{1,0:T(8,128)(2,1)S(1)} %get-tuple-element.70), channel_id=1, source_target_pairs={{0,12},{1,13},{2,14},{3,15},{4,8},{5,9},{6,10},{7,11},{8,4},{9,5},... | collective-permute-start | bytes 344072 | tf_op jit(solution)/shard_map/ppermute | solution.py:64
  88.2 8.6 %collective-permute-start.17 = (bf16[8,7168]{1,0:T(8,128)(2,1)S(1)}, bf16[8,7168]{1,0:T(8,128)(2,1)S(1)}, u32[]{:S(2)}, u32[]{:S(2)}) collective-permute-start(bf16[8,7168]{1,0:T(8,128)(2,1)S(1)} %get-tuple-element.69), channel_id=1, source_target_pairs={{0,4},{1,5},{2,6},{3,7},{4,0},{5,1},{6,2},{7,3},{8,12},{9,13},{10,... | collective-permute-start | bytes 344072 | tf_op jit(solution)/shard_map/ppermute | solution.py:64
  97.1 8.7 %collective-permute-start.18 = (bf16[8,3584]{1,0:T(8,128)(2,1)S(1)}, bf16[8,3584]{1,0:T(8,128)(2,1)S(1)}, u32[]{:S(2)}, u32[]{:S(2)}) collective-permute-start(bf16[8,3584]{1,0:T(8,128)(2,1)S(1)} %get-tuple-element.83), channel_id=1, source_target_pairs={{0,8},{1,9},{2,10},{3,11},{4,12},{5,13},{6,14},{7,15},{8,0},{9,1},... | collective-permute-start | bytes 172040 | tf_op jit(solution)/shard_map/ppermute | solution.py:64
  105.8 20.9 %collective-permute-start.25 = (bf16[32,3584]{1,0:T(8,128)(2,1)S(1)}, bf16[32,3584]{1,0:T(8,128)(2,1)S(1)}, u32[]{:S(2)}, u32[]{:S(2)}) collective-permute-start(bf16[32,3584]{1,0:T(8,128)(2,1)S(1)} %maximum_bitcast_fusion.2), channel_id=1, source_target_pairs={{0,2},{1,3},{2,0},{3,1},{4,6},{5,7},{6,4},{7,5},{8,10},{9,11},{10,... | collective-permute-start | bytes 688136 | tf_op jit(solution)/shard_map/ppermute | solution.py:64
  106.4 20.5 %collective-permute-start.27 = (bf16[32,3584]{1,0:T(8,128)(2,1)S(1)}, bf16[32,3584]{1,0:T(8,128)(2,1)S(1)}, u32[]{:S(2)}, u32[]{:S(2)}) collective-permute-start(bf16[32,3584]{1,0:T(8,128)(2,1)S(1)} %maximum_bitcast_fusion.2), channel_id=1, source_target_pairs={{0,16},{1,17},{2,18},{3,19},{4,20},{5,21},{6,22},{7,23},{8,24},{9,... | collective-permute-start | bytes 688136 | tf_op jit(solution)/shard_map/ppermute | solution.py:64
  109.6 11.1 %collective-permute-start.21 = (bf16[32,3584]{1,0:T(8,128)(2,1)S(1)}, bf16[32,3584]{1,0:T(8,128)(2,1)S(1)}, u32[]{:S(2)}, u32[]{:S(2)}) collective-permute-start(bf16[32,3584]{1,0:T(8,128)(2,1)S(1)} %maximum_bitcast_fusion.2), channel_id=1, source_target_pairs={{0,18},{1,19},{2,16},{3,17},{4,22},{5,23},{6,20},{7,21},{8,26},{9,... | collective-permute-start | bytes 688136 | tf_op jit(solution)/shard_map/ppermute | solution.py:64
  110.2 16.6 %collective-permute-start.26 = (bf16[32,3712]{1,0:T(8,128)(2,1)S(1)}, bf16[32,3712]{1,0:T(8,128)(2,1)S(1)}, u32[]{:S(2)}, u32[]{:S(2)}) collective-permute-start(bf16[32,3712]{1,0:T(8,128)(2,1)S(1)} %maximum_bitcast_fusion.1), channel_id=1, source_target_pairs={{0,2},{1,3},{2,0},{3,1},{4,6},{5,7},{6,4},{7,5},{8,10},{9,11},{10,... | collective-permute-start | bytes 712712 | tf_op jit(solution)/shard_map/ppermute | solution.py:64
  112.7 14.2 %collective-permute-start.28 = (bf16[32,3712]{1,0:T(8,128)(2,1)S(1)}, bf16[32,3712]{1,0:T(8,128)(2,1)S(1)}, u32[]{:S(2)}, u32[]{:S(2)}) collective-permute-start(bf16[32,3712]{1,0:T(8,128)(2,1)S(1)} %maximum_bitcast_fusion.1), channel_id=1, source_target_pairs={{0,16},{1,17},{2,18},{3,19},{4,20},{5,21},{6,22},{7,23},{8,24},{9,... | collective-permute-start | bytes 712712 | tf_op jit(solution)/shard_map/ppermute | solution.py:64
  122.3 34.1 %all-to-all-start.1 = ((bf16[16,2,72,256]{3,2,1,0:T(8,128)(2,1)}), bf16[16,2,72,256]{3,2,1,0:T(8,128)(2,1)}, u32[]{:S(2)}, u32[]{:S(2)}) async-start(bf16[16,2,72,256]{3,2,1,0:T(8,128)(2,1)} %bitcast.16), calls=%async_computation.1 | async-start | bytes 2359296 | tf_op jit(solution)/shard_map/all_to_all | solution.py:413
  156.1 8.4 %collective-permute-start.31 = (bf16[128,3584]{1,0:T(8,128)(2,1)}, bf16[128,3584]{1,0:T(8,128)(2,1)S(1)}, u32[]{:S(2)}, u32[]{:S(2)}) collective-permute-start(bf16[128,3584]{1,0:T(8,128)(2,1)} %get-tuple-element.32), channel_id=1, source_target_pairs={{0,1},{1,0},{2,3},{3,2},{4,5},{5,4},{6,7},{7,6},{8,9},{9,8},{10,11... | collective-permute-start | bytes 2752520 | tf_op jit(solution)/shard_map/ppermute | solution.py:64
  160.9 9.3 %collective-permute-start.39 = (bf16[32,3584]{1,0:T(8,128)(2,1)S(1)}, bf16[32,3584]{1,0:T(8,128)(2,1)S(1)}, u32[]{:S(2)}, u32[]{:S(2)}) collective-permute-start(bf16[32,3584]{1,0:T(8,128)(2,1)S(1)} %get-tuple-element.61), channel_id=1, source_target_pairs={{0,2},{1,3},{2,0},{3,1},{4,6},{5,7},{6,4},{7,5},{8,10},{9,11},{10,... | collective-permute-start | bytes 688136 | tf_op jit(solution)/shard_map/ppermute | solution.py:64
  161.3 9.2 %collective-permute-start.40 = (bf16[32,3584]{1,0:T(8,128)(2,1)S(1)}, bf16[32,3584]{1,0:T(8,128)(2,1)S(1)}, u32[]{:S(2)}, u32[]{:S(2)}) collective-permute-start(bf16[32,3584]{1,0:T(8,128)(2,1)S(1)} %get-tuple-element.63), channel_id=1, source_target_pairs={{0,16},{1,17},{2,18},{3,19},{4,20},{5,21},{6,22},{7,23},{8,24},{9,... | collective-permute-start | bytes 688136 | tf_op jit(solution)/shard_map/ppermute | solution.py:64
  162.5 13.3 %collective-permute-start.41 = (bf16[32,3584]{1,0:T(8,128)(2,1)S(1)}, bf16[32,3584]{1,0:T(8,128)(2,1)S(1)}, u32[]{:S(2)}, u32[]{:S(2)}) collective-permute-start(bf16[32,3584]{1,0:T(8,128)(2,1)S(1)} %get-tuple-element.62), channel_id=1, source_target_pairs={{0,18},{1,19},{2,16},{3,17},{4,22},{5,23},{6,20},{7,21},{8,26},{9,... | collective-permute-start | bytes 688136 | tf_op jit(solution)/shard_map/ppermute | solution.py:64
  164.6 15.3 %collective-permute-start.32 = (bf16[32,3584]{1,0:T(8,128)(2,1)S(1)}, bf16[32,3584]{1,0:T(8,128)(2,1)S(1)}, u32[]{:S(2)}, u32[]{:S(2)}) collective-permute-start(bf16[32,3584]{1,0:T(8,128)(2,1)S(1)} %get-tuple-element.58), channel_id=1, source_target_pairs={{0,2},{1,3},{2,0},{3,1},{4,6},{5,7},{6,4},{7,5},{8,10},{9,11},{10,... | collective-permute-start | bytes 688136 | tf_op jit(solution)/shard_map/ppermute | solution.py:64
  165.0 14.9 %collective-permute-start.33 = (bf16[32,3584]{1,0:T(8,128)(2,1)S(1)}, bf16[32,3584]{1,0:T(8,128)(2,1)S(1)}, u32[]{:S(2)}, u32[]{:S(2)}) collective-permute-start(bf16[32,3584]{1,0:T(8,128)(2,1)S(1)} %get-tuple-element.60), channel_id=1, source_target_pairs={{0,16},{1,17},{2,18},{3,19},{4,20},{5,21},{6,22},{7,23},{8,24},{9,... | collective-permute-start | bytes 688136 | tf_op jit(solution)/shard_map/ppermute | solution.py:64
  170.2 14.4 %collective-permute-start.34 = (bf16[32,3584]{1,0:T(8,128)(2,1)S(1)}, bf16[32,3584]{1,0:T(8,128)(2,1)S(1)}, u32[]{:S(2)}, u32[]{:S(2)}) collective-permute-start(bf16[32,3584]{1,0:T(8,128)(2,1)S(1)} %get-tuple-element.59), channel_id=1, source_target_pairs={{0,18},{1,19},{2,16},{3,17},{4,22},{5,23},{6,20},{7,21},{8,26},{9,... | collective-permute-start | bytes 688136 | tf_op jit(solution)/shard_map/ppermute | solution.py:64
  176.1 12.6 %collective-permute-start.42 = (bf16[8,3584]{1,0:T(8,128)(2,1)S(1)}, bf16[8,3584]{1,0:T(8,128)(2,1)S(1)}, u32[]{:S(2)}, u32[]{:S(2)}) collective-permute-start(bf16[8,3584]{1,0:T(8,128)(2,1)S(1)} %get-tuple-element.76), channel_id=1, source_target_pairs={{0,8},{1,9},{2,10},{3,11},{4,12},{5,13},{6,14},{7,15},{8,0},{9,1},... | collective-permute-start | bytes 172040 | tf_op jit(solution)/shard_map/ppermute | solution.py:64
  177.5 12.2 %collective-permute-start.43 = (bf16[8,3584]{1,0:T(8,128)(2,1)S(1)}, bf16[8,3584]{1,0:T(8,128)(2,1)S(1)}, u32[]{:S(2)}, u32[]{:S(2)}) collective-permute-start(bf16[8,3584]{1,0:T(8,128)(2,1)S(1)} %get-tuple-element.78), channel_id=1, source_target_pairs={{0,12},{1,13},{2,14},{3,15},{4,8},{5,9},{6,10},{7,11},{8,4},{9,5},... | collective-permute-start | bytes 172040 | tf_op jit(solution)/shard_map/ppermute | solution.py:64
  179.9 9.8 %collective-permute-start.44 = (bf16[8,3584]{1,0:T(8,128)(2,1)S(1)}, bf16[8,3584]{1,0:T(8,128)(2,1)S(1)}, u32[]{:S(2)}, u32[]{:S(2)}) collective-permute-start(bf16[8,3584]{1,0:T(8,128)(2,1)S(1)} %get-tuple-element.77), channel_id=1, source_target_pairs={{0,4},{1,5},{2,6},{3,7},{4,0},{5,1},{6,2},{7,3},{8,12},{9,13},{10,... | collective-permute-start | bytes 172040 | tf_op jit(solution)/shard_map/ppermute | solution.py:64
  (35 other events, 207.2 us)
